TPU v7x, 256 devices: a whole 4x4x8 slice. The times are simulated.
256 devices in a mesh: sky: 64 (over x, z, core), tm: 4 (over y).
Axes of the slice: x: 4, y: 4, z: 8, core: 2. Of those that a mesh axis runs over, the one named last changes fastest.
Arguments:
- observed: float32 [32768, 128], P(('sky', 'tm')), may hold values from -12 to 12
- att_partials: bfloat16 [3, 32768, 128], P(None, ('sky', 'tm')), may hold values from -6 to 6
- src_partials: bfloat16 [5, 32768, 128], P(None, ('sky', 'tm')), may hold values from -6 to 6
- src_slot: int32 [32768], P(('sky', 'tm')), may hold values from 0 to 1023
- knot_block: int32 [32768], P(('sky', 'tm')), may hold values from 0 to 2047, as said below
- live_count: int32 [256], P(('sky', 'tm')), may hold values from 32 to 128, as said below
- sources: float32 [5, 65536], P(None, 'sky'), may hold values from -6 to 6
- inverses: float32 [5, 5, 65536], P(None, None, 'sky')
- attitude: float32 [3, 4, 32768], P(None, 'tm', 'sky'), may hold values from -6 to 6
- band_coef: float32 [3, 3, 4, 32768], P(None, None, 'tm', 'sky'), may hold values from 0.5 to 4
- extra_diag: float32 [3, 4, 32768], P(None, 'tm', 'sky'), may hold values from 0.05 to 0.5
- band_offsets: int32 [3], replicated, may hold values from 1 to 16, as said below
Outputs:
- sources_out: float32 [5, 65536], P(None, 'sky')
- attitude_out: float32 [3, 4, 32768], P(None, 'tm', 'sky')
Inputs may be any that keep to these rules, and one draw needn't show every extreme that they name: On every device, the crossings name blocks of one holder (knot_block // 32) at most 4 times, and some holder exactly 4 times; dead crossings carry blocks too. `live_count`: some device uses all its crossings. `band_offsets`: Distinct; one of them is 16.
All inputs are finite; a program needn't handle non-finite values.
Results may differ from a plain program's by a relative error of at most 0.0003.
Values sent between devices are 32-bit elements; how exact they have to be, the bound alone decides.
No kernel may reach another device: no remote copies, remote signals or barrier semaphores. Data moves between devices by JAX's collectives and lax.ppermute only.
A program may use at most 64 MiB of HBM per device.

v0:
```python
import jax
import jax.numpy as jnp
from jax import lax
from jax.sharding import Mesh
from jax.sharding import PartitionSpec as P

ROWS = 128
BLOCK_KNOTS = 16
HW = 16
SWEEPS = 3
ITERS = 2
SKY = ("sky_0", "sky_1", "sky_2")
SKY_TM = ("sky_0", "sky_1", "sky_2", "tm")


def padded_2(block, sides, width):
    for axis, dim in sides:
        count = lax.axis_size(axis)
        forward = [(i, i + 1) for i in range(count - 1)]
        forward.append((count - 1, 0))
        backward = [(target, source) for source, target in forward]
        low = lax.ppermute(
            lax.slice_in_dim(block, block.shape[dim] - width, None, axis=dim), axis, forward
        )
        high = lax.ppermute(lax.slice_in_dim(block, 0, width, axis=dim), axis, backward)
        block = jnp.concatenate([low, block, high], axis=dim)
    return block


def from_behind(value, axis, steps):
    count = lax.axis_size(axis)
    initial, last = (max(0, -steps), min(count, count - steps))
    return lax.ppermute(value, axis, [(source, source + steps) for source in range(initial, last)])


def in_blocks(array, dim, length):
    lengths = array.shape
    pieces = array.reshape(*lengths[:dim], length, lengths[dim] // length, *lengths[dim + 1 :])
    return jnp.moveaxis(pieces, dim, 0)


def joined_along(pieces, dim):
    lengths = list(pieces.shape[1:])
    lengths[dim] *= pieces.shape[0]
    return jnp.moveaxis(pieces, 0, dim).reshape(lengths)


def turned_blocks(pieces, axes, turns):
    inside = pieces.shape[1:]
    out = pieces.reshape(*(lax.axis_size(a) for a in axes), *inside)
    for k in turns:
        out = lax.all_to_all(out, axes[k], k, k, tiled=True)
    return out.reshape(-1, *inside)


def core_and_chips(array, groups, turns, split_dim, concat_dim):
    length = lax.axis_size(groups[0]) * lax.axis_size(groups[1])
    pieces = in_blocks(array, split_dim, length)
    return joined_along(turned_blocks(pieces, groups, turns), concat_dim)


def from_everyone(array, axis):
    length = lax.axis_size(axis)
    return lax.all_to_all(
        jnp.broadcast_to(array[None], (length, *array.shape)), axis, 0, 0, tiled=True
    )


def over_copies(array, axis):
    return from_everyone(array, axis).sum(axis=0)


def spline_table():
    rows_pos = jnp.arange(ROWS, dtype=jnp.float32)
    moments = 1.5 + (BLOCK_KNOTS - 3) * (rows_pos + 0.5) / ROWS
    knot_pos = jnp.arange(BLOCK_KNOTS, dtype=jnp.float32)
    dist = jnp.abs(moments[:, None] - knot_pos[None, :])
    inner = 2.0 / 3.0 - dist * dist + 0.5 * dist * dist * dist
    rest = 2.0 - dist
    outer = rest * rest * rest / 6.0
    return jnp.where(dist < 1.0, inner, jnp.where(dist < 2.0, outer, 0.0))


def source_term(src_partials, values):
    total = jnp.zeros(src_partials.shape[1:], jnp.float32)
    for component in range(5):
        total = total + src_partials[component].astype(jnp.float32) * values[component][:, None]
    return total


def neighbour_sum(field, band_terms, band_offsets, base, length):
    total = jnp.zeros(band_terms.shape[1:], jnp.float32)
    for band_index in range(band_terms.shape[0]):
        offset = band_offsets[band_index]
        upper = lax.dynamic_slice_in_dim(field, base + offset, length, 1)
        lower = lax.dynamic_slice_in_dim(field, base - offset, length, 1)
        total = total + band_terms[band_index] * (upper + lower)
    return total


def extend(field, width):
    padded = padded_2(field, ((SKY, 1),), width)
    inner_end = padded.shape[1] - width
    left_rim = padded[:, :width]
    right_rim = padded[:, inner_end:]
    from_before = from_behind(left_rim, "tm", 1)
    from_after = from_behind(right_rim, "tm", -1)
    position = lax.axis_index(SKY)
    left_rim = jnp.where(position == 0, from_before, left_rim)
    right_rim = jnp.where(position == lax.axis_size(SKY) - 1, from_after, right_rim)
    return jnp.concatenate([left_rim, padded[:, width:inner_end], right_rim], axis=1)


def per_device(
    observed,
    att_partials,
    src_partials,
    src_slot,
    knot_block,
    live_count,
    sources,
    inverses,
    attitude,
    band_coef,
    extra_diag,
    band_offsets,
):
    spline = spline_table()
    crossings_here = observed.shape[0]
    knots_here = attitude.shape[2]
    blocks_here = knots_here // BLOCK_KNOTS
    sky_count = lax.axis_size(SKY)
    capacity = 2 * crossings_here // sky_count
    slots_total = sky_count * capacity
    live_rows = (jnp.arange(crossings_here, dtype=jnp.int32) < live_count[0]).astype(jnp.float32)[
        :, None
    ]
    band_terms = band_coef[:, :, 0, :]
    extra_terms = extra_diag[:, 0, :]
    band_count = band_terms.shape[0]
    knots_now = attitude[:, 0, :]
    sources_now = sources
    holder = knot_block // blocks_here
    local_block = knot_block % blocks_here
    matches = (holder[:, None] == jnp.arange(sky_count, dtype=jnp.int32)[None, :]).astype(jnp.int32)
    earlier = jnp.cumsum(matches, axis=0) - matches
    column = holder * capacity + jnp.sum(earlier * matches, axis=1)
    asked = jnp.full((slots_total,), blocks_here, jnp.int32).at[column].set(local_block)
    wanted = core_and_chips(asked, (("sky_0", "sky_1"), "sky_2"), (1, 0), 0, 0)
    for outer_step in range(ITERS):
        spare = jnp.zeros((3, 1, BLOCK_KNOTS), jnp.float32)
        own_blocks = jnp.concatenate(
            [knots_now.reshape(3, blocks_here, BLOCK_KNOTS), spare], axis=1
        )
        served = jnp.take(jnp.transpose(own_blocks, (0, 2, 1)), wanted, axis=2)
        arrived = lax.all_to_all(served, SKY, split_axis=2, concat_axis=2, tiled=True)
        fetched = jnp.transpose(jnp.take(arrived, column, axis=2), (0, 2, 1))
        att_term = jnp.zeros(observed.shape, jnp.float32)
        for axis_index in range(3):
            att_term = att_term + att_partials[axis_index].astype(jnp.float32) * jnp.dot(
                fetched[axis_index], spline.T, precision=lax.Precision.HIGHEST
            )
        src_values = jnp.take(sources_now, src_slot, axis=1)
        resid = (observed - source_term(src_partials, src_values) - att_term) * live_rows
        rhs = jnp.stack(
            [
                jnp.sum(src_partials[component].astype(jnp.float32) * resid, axis=1)
                for component in range(5)
            ]
        )
        local_normal = jnp.zeros(sources_now.shape, jnp.float32).at[:, src_slot].add(rhs)
        normal = over_copies(local_normal, "tm")
        step = jnp.einsum("klm,lm->km", inverses, normal, precision=lax.Precision.HIGHEST)
        sources_now = sources_now + step
        resid = resid - live_rows * source_term(src_partials, jnp.take(step, src_slot, axis=1))
        grads = jnp.stack(
            [
                jnp.dot(
                    att_partials[axis_index].astype(jnp.float32) * resid,
                    spline,
                    precision=lax.Precision.HIGHEST,
                )
                for axis_index in range(3)
            ]
        )
        outgoing = (
            jnp.zeros((3, BLOCK_KNOTS, slots_total), jnp.float32)
            .at[:, :, column]
            .set(jnp.transpose(grads, (0, 2, 1)))
        )
        returned = lax.all_to_all(outgoing, SKY, split_axis=2, concat_axis=2, tiled=True)
        summed = (
            jnp.zeros((3, BLOCK_KNOTS, blocks_here + 1), jnp.float32).at[:, :, wanted].add(returned)
        )
        knot_grad = jnp.transpose(summed[:, :, :blocks_here], (0, 2, 1)).reshape(3, knots_here)
        margin = (SWEEPS - 1) * HW
        stacked = jnp.concatenate(
            [knot_grad, band_terms.reshape(band_count * 3, knots_here), extra_terms], axis=0
        )
        wide = extend(stacked, margin)
        span = knots_here + 2 * margin
        grad_wide = wide[:3]
        bands_wide = wide[3 : 3 + 3 * band_count].reshape(band_count, 3, span)
        diag_wide = wide[3 + 3 * band_count :] + 2.0 * jnp.sum(bands_wide, axis=0)
        safe_diag = jnp.where(diag_wide > 0.0, diag_wide, 1.0)
        delta = grad_wide / safe_diag
        for sweep_index in range(SWEEPS - 1):
            margin_next = margin - (sweep_index + 1) * HW
            start = margin - margin_next
            length = knots_here + 2 * margin_next
            delta = (
                grad_wide[:, start : start + length]
                + neighbour_sum(
                    delta, bands_wide[:, :, start : start + length], band_offsets, HW, length
                )
            ) / safe_diag[:, start : start + length]
        knots_now = knots_now + delta
    return (sources_now, knots_now[:, None, :])


def solution(mesh):
    torus = Mesh(mesh.devices.reshape(4, 8, 2, mesh.shape["tm"]), ("sky_0", "sky_1", "sky_2", "tm"))
    return jax.shard_map(
        per_device,
        mesh=torus,
        in_specs=(
            P(SKY_TM, None),
            P(None, SKY_TM, None),
            P(None, SKY_TM, None),
            P(SKY_TM),
            P(SKY_TM),
            P(SKY_TM),
            P(None, SKY),
            P(None, None, SKY),
            P(None, "tm", SKY),
            P(None, None, "tm", SKY),
            P(None, "tm", SKY),
            P(),
        ),
        out_specs=(P(None, SKY), P(None, "tm", SKY)),
        check_vma=False,
    )
```

profile of v0, /device:TPU:1, one launch (start us, length us, event | category | flops | bytes accessed | tf_op | source)
XLA Modules:
  0.0 194.4 jit_solution(12479490255764376969)
XLA Ops:
  0.6 0.7 and_select_fusion
  1.8 1.0 scatter_custom_fusion
  3.1 6.6 %all_to_all.40 = s32[2,1,128]{2,1,0:T(1,128)S(1)} all-to-all(s32[2,1,128]{2,1,0:T(1,128)S(1)} %reshape.342), channel_id=1, replica_groups=mesh['sky_0'=4,'sky_1'=8,'sky_2'=2,'tm'=4] {'sky_2'}, dimensions={0} | all-to-all | bytes 2048 | tf_op jit(solution)/shard_map/all_to_all | solution.py:52
  10.2 0.7 reduce.46
  10.9 0.7 copy.145
  11.6 9.4 %all-to-all-start.1 = ((s32[32,2,4]{2,1,0:T(2,128)}), s32[32,2,4]{2,1,0:T(2,128)S(1)}, u32[]{:S(2)}, u32[]{:S(2)}) async-start(s32[32,2,4]{2,1,0:T(2,128)} %copy.145), calls=%async_computation.1 | async-start | bytes 65536 | tf_op jit(solution)/shard_map/all_to_all | solution.py:52
  22.0 0.7 copy-done.1
  22.7 0.7 copy-done.5
  23.5 0.8 copy-done.2
  27.7 2.1 %all-to-all-done.1 = s32[32,2,4]{2,1,0:T(2,128)S(1)} async-done(((s32[32,2,4]{2,1,0:T(2,128)}), s32[32,2,4]{2,1,0:T(2,128)S(1)}, u32[]{:S(2)}, u32[]{:S(2)}) %all-to-all-start.1) | async-done | bytes 1056 | tf_op jit(solution)/shard_map/all_to_all | solution.py:52
  30.0 1.0 gather_fusion.1
  31.3 1.0 reshape.344
  32.4 8.5 %all-to-all-start.2 = ((f32[64,1,192]{2,1,0:T(1,128)}), f32[64,1,192]{2,1,0:T(1,128)S(1)}, u32[]{:S(2)}, u32[]{:S(2)}) async-start(f32[64,1,192]{2,1,0:T(1,128)} %reshape.344), calls=%async_computation.2 | async-start | bytes 131072 | tf_op jit(solution)/shard_map/all_to_all | solution.py:156
  40.8 9.8 %all-to-all-done.2 = f32[64,1,192]{2,1,0:T(1,128)S(1)} async-done(((f32[64,1,192]{2,1,0:T(1,128)}), f32[64,1,192]{2,1,0:T(1,128)S(1)}, u32[]{:S(2)}, u32[]{:S(2)}) %all-to-all-start.2) | async-done | bytes 49184 | tf_op jit(solution)/shard_map/all_to_all | solution.py:156
  51.1 0.8 reduce.47
  52.3 0.8 gather_fusion.2
  54.6 1.1 scatter_custom_fusion.1
  55.9 0.7 broadcast_in_dim.74
  56.6 4.3 %all-to-all-start.3 = ((f32[4,5,1024]{2,1,0:T(8,128)}), f32[4,5,1024]{2,1,0:T(8,128)S(1)}, u32[]{:S(2)}, u32[]{:S(2)}) async-start(f32[4,5,1024]{2,1,0:T(8,128)} %broadcast_in_dim.74), calls=%async_computation.3 | async-start | bytes 262144 | tf_op jit(solution)/shard_map/all_to_all | solution.py:64
  64.7 1.0 all-to-all-done.3
  69.0 4.3 %scatter_fusion = f32[3,16,256]{1,0,2:T(4,128)S(1)} fusion(f32[3,16,256]{1,0,2:T(4,128)S(1)} %broadcast.105.clone, s32[128]{0:T(128)S(1)} %get-tuple-element.52, f32[128,3,16]{2,1,0:T(4,128)S(1)} %copy.154), kind=kCustom, calls=%fused_computation.10 | custom fusion | bytes 74240 | tf_op jit(solution)/shard_map/scatter | solution.py:189
  73.4 1.0 reshape.346
  74.4 5.9 %all-to-all-start.4 = ((f32[64,1,192]{2,1,0:T(1,128)}), f32[64,1,192]{2,1,0:T(1,128)S(1)}, u32[]{:S(2)}, u32[]{:S(2)}) async-start(f32[64,1,192]{2,1,0:T(1,128)} %reshape.346), calls=%async_computation.4 | async-start | bytes 131072 | tf_op jit(solution)/shard_map/all_to_all | solution.py:191
  80.3 9.9 %all-to-all-done.4 = f32[64,1,192]{2,1,0:T(1,128)S(1)} async-done(((f32[64,1,192]{2,1,0:T(1,128)}), f32[64,1,192]{2,1,0:T(1,128)S(1)}, u32[]{:S(2)}, u32[]{:S(2)}) %all-to-all-start.4) | async-done | bytes 49184 | tf_op jit(solution)/shard_map/all_to_all | solution.py:191
  90.2 0.8 reduce.48
  91.5 8.6 %scatter_fusion.1 = f32[3,16,33]{1,0,2:T(4,128)S(1)} fusion(f32[3,16,33]{1,0,2:T(4,128)S(1)} %broadcast.102.clone, s32[256]{0:T(256)S(1)} %bitcast.328, f32[256,3,16]{2,1,0:T(4,128)S(1)} %bitcast_bitcast_fusion.1), kind=kCustom, calls=%fused_computation.11 | custom fusion | flops 12288 | bytes 148480 | tf_op jit(solution)/shard_map/scatter-add | solution.py:193
  109.1 1.4 collective-permute-start
  110.5 1.3 collective-permute-start.3
  111.9 4.0 %collective-permute-start.1 = (f32[15,32]{1,0:T(8,128)S(1)}, f32[15,32]{1,0:T(8,128)S(1)}, u32[]{:S(2)}, u32[]{:S(2)}) collective-permute-start(f32[15,32]{1,0:T(8,128)S(1)} %collective-permute-done), channel_id=1, source_target_pairs={{0,1},{1,2},{2,3},{4,5},{5,6},{6,7},{8,9},{9,10},{10,11},{12,13},{... | collective-permute-start | bytes 5768 | tf_op jit(solution)/shard_map/ppermute | solution.py:33
  115.9 0.8 collective-permute-done.1
  117.3 1.0 gather_fusion.5
  118.6 1.0 reshape.348
  119.6 7.6 %all-to-all-start.5 = ((f32[64,1,192]{2,1,0:T(1,128)}), f32[64,1,192]{2,1,0:T(1,128)S(1)}, u32[]{:S(2)}, u32[]{:S(2)}) async-start(f32[64,1,192]{2,1,0:T(1,128)} %reshape.348), calls=%async_computation.5 | async-start | bytes 131072 | tf_op jit(solution)/shard_map/all_to_all | solution.py:156
  127.5 9.6 %all-to-all-done.5 = f32[64,1,192]{2,1,0:T(1,128)S(1)} async-done(((f32[64,1,192]{2,1,0:T(1,128)}), f32[64,1,192]{2,1,0:T(1,128)S(1)}, u32[]{:S(2)}, u32[]{:S(2)}) %all-to-all-start.5) | async-done | bytes 49184 | tf_op jit(solution)/shard_map/all_to_all | solution.py:156
  137.2 0.8 reduce.49
  138.4 0.8 gather_fusion.6
  140.6 1.1 scatter_custom_fusion.4
  141.9 8.7 %all_to_all.42 = f32[4,5,1024]{2,1,0:T(8,128)S(1)} all-to-all(f32[4,5,1024]{2,1,0:T(8,128)S(1)} %broadcast_in_dim.76), channel_id=1, replica_groups=mesh['sky_0'=4,'sky_1'=8,'sky_2'=2,'tm'=4] {'tm'}, dimensions={0} | all-to-all | bytes 163840 | tf_op jit(solution)/shard_map/all_to_all | solution.py:64
  153.3 4.3 %scatter_fusion.2 = f32[3,16,256]{1,0,2:T(4,128)S(1)} fusion(f32[3,16,256]{1,0,2:T(4,128)S(1)} %broadcast.105, s32[128]{0:T(128)S(1)} %get-tuple-element.52, f32[128,3,16]{2,1,0:T(4,128)S(1)} %copy.160), kind=kCustom, calls=%fused_computation.13 | custom fusion | bytes 74240 | tf_op jit(solution)/shard_map/scatter | solution.py:189
  158.0 15.1 %all_to_all.41 = f32[64,1,192]{2,1,0:T(1,128)S(1)} all-to-all(f32[64,1,192]{2,1,0:T(1,128)S(1)} %reshape.350), channel_id=1, replica_groups=mesh['sky_0'=4,'sky_1'=8,'sky_2'=2,'tm'=4] {'sky_0','sky_1','sky_2'}, dimensions={0} | all-to-all | bytes 98304 | tf_op jit(solution)/shard_map/all_to_all | solution.py:191
  173.1 0.8 reduce.50
  174.4 8.6 %scatter_fusion.3 = f32[3,16,33]{1,0,2:T(4,128)S(1)} fusion(f32[3,16,33]{1,0,2:T(4,128)S(1)} %broadcast.102, s32[256]{0:T(256)S(1)} %bitcast.329, f32[256,3,16]{2,1,0:T(4,128)S(1)} %bitcast_bitcast_fusion), kind=kCustom, calls=%fused_computation.14 | custom fusion | flops 12288 | bytes 148480 | tf_op jit(solution)/shard_map/scatter-add | solution.py:193
  183.7 1.3 collective-permute-start.4
  185.1 1.3 collective-permute-done.6
  186.4 1.3 collective-permute-start.7
  187.8 0.8 copy.162
  188.6 4.0 %collective-permute-start.5 = (f32[15,32]{1,0:T(8,128)S(1)}, f32[15,32]{1,0:T(8,128)S(1)}, u32[]{:S(2)}, u32[]{:S(2)}) collective-permute-start(f32[15,32]{1,0:T(8,128)S(1)} %collective-permute-done.4), channel_id=1, source_target_pairs={{0,1},{1,2},{2,3},{4,5},{5,6},{6,7},{8,9},{9,10},{10,11},{12,13},{... | collective-permute-start | bytes 5768 | tf_op jit(solution)/shard_map/ppermute | solution.py:33
  192.6 0.8 collective-permute-done.5
  (158 shorter events, 21.8 us)
Async XLA Ops:
  11.6 10.1 %copy-start.4 = (f32[5,1024]{1,0:T(8,128)S(1)}, f32[5,1024]{1,0:T(8,128)}, u32[]{:S(2)}) copy-start(f32[5,1024]{1,0:T(8,128)} %param.24) | copy-start | bytes 61444
  11.6 18.2 %all-to-all-start.1 = ((s32[32,2,4]{2,1,0:T(2,128)}), s32[32,2,4]{2,1,0:T(2,128)S(1)}, u32[]{:S(2)}, u32[]{:S(2)}) async-start(s32[32,2,4]{2,1,0:T(2,128)} %copy.145), calls=%async_computation.1 | async-start | bytes 65536 | tf_op jit(solution)/shard_map/all_to_all | solution.py:52
  21.1 0.7 copy-start.9
  21.7 0.9 copy-start.1
  22.7 0.7 copy-start.5
  23.5 0.9 copy-start.2
  26.8 0.9 copy-start.3
  32.4 18.2 %all-to-all-start.2 = ((f32[64,1,192]{2,1,0:T(1,128)}), f32[64,1,192]{2,1,0:T(1,128)S(1)}, u32[]{:S(2)}, u32[]{:S(2)}) async-start(f32[64,1,192]{2,1,0:T(1,128)} %reshape.344), calls=%async_computation.2 | async-start | bytes 131072 | tf_op jit(solution)/shard_map/all_to_all | solution.py:156
  56.5 4.3 %copy-start.8 = (s32[3]{0:T(128)S(1)}, s32[3]{0:T(128)}, u32[]{:S(2)}) copy-start(s32[3]{0:T(128)} %param.29) | copy-start | bytes 40
  56.5 7.3 %copy-start.7 = (f32[3,1,512]{2,1,0:T(1,128)S(1)}, f32[3,1,512]{2,1,0:T(1,128)}, u32[]{:S(2)}) copy-start(f32[3,1,512]{2,1,0:T(1,128)} %param.28) | copy-start | bytes 18436
  56.6 9.1 %all-to-all-start.3 = ((f32[4,5,1024]{2,1,0:T(8,128)}), f32[4,5,1024]{2,1,0:T(8,128)S(1)}, u32[]{:S(2)}, u32[]{:S(2)}) async-start(f32[4,5,1024]{2,1,0:T(8,128)} %broadcast_in_dim.74), calls=%async_computation.3 | async-start | bytes 262144 | tf_op jit(solution)/shard_map/all_to_all | solution.py:64
  60.9 3.0 %copy-start.6 = (f32[3,3,1,512]{3,2,1,0:T(1,128)S(1)}, f32[3,3,1,512]{3,2,1,0:T(1,128)}, u32[]{:S(2)}) copy-start(f32[3,3,1,512]{3,2,1,0:T(1,128)} %param.27) | copy-start | bytes 55300
  61.5 4.2 %copy-start = (f32[5,5,1024]{2,1,0:T(8,128)S(1)}, f32[5,5,1024]{2,1,0:T(8,128)}, u32[]{:S(2)}) copy-start(f32[5,5,1024]{2,1,0:T(8,128)} %param.25) | copy-start | bytes 307204
  74.4 15.8 %all-to-all-start.4 = ((f32[64,1,192]{2,1,0:T(1,128)}), f32[64,1,192]{2,1,0:T(1,128)S(1)}, u32[]{:S(2)}, u32[]{:S(2)}) async-start(f32[64,1,192]{2,1,0:T(1,128)} %reshape.346), calls=%async_computation.4 | async-start | bytes 131072 | tf_op jit(solution)/shard_map/all_to_all | solution.py:191
  100.4 10.1 %collective-permute-start.2 = (f32[15,32]{1,0:T(8,128)S(1)}, f32[15,32]{1,0:T(8,128)S(1)}, u32[]{:S(2)}, u32[]{:S(2)}) collective-permute-start(f32[15,32]{1,0:T(8,128)S(1)} %get-tuple-element.70), channel_id=1, source_target_pairs={{4,0},{8,4},{12,8},{16,12},{20,16},{24,20},{28,24},{32,28},{36,32}... | collective-permute-start | bytes 5768 | tf_op jit(solution)/shard_map/ppermute | solution.py:25
  109.1 2.8 %collective-permute-start = (f32[15,32]{1,0:T(8,128)S(1)}, f32[15,32]{1,0:T(8,128)S(1)}, u32[]{:S(2)}, u32[]{:S(2)}) collective-permute-start(f32[15,32]{1,0:T(8,128)S(1)} %get-tuple-element.69), channel_id=1, source_target_pairs={{0,4},{4,8},{8,12},{12,16},{16,20},{20,24},{24,28},{28,32},{32,36}... | collective-permute-start | bytes 5768 | tf_op jit(solution)/shard_map/ppermute | solution.py:22
  110.5 5.4 %collective-permute-start.3 = (f32[15,32]{1,0:T(8,128)S(1)}, f32[15,32]{1,0:T(8,128)S(1)}, u32[]{:S(2)}, u32[]{:S(2)}) collective-permute-start(f32[15,32]{1,0:T(8,128)S(1)} %collective-permute-done.2), channel_id=1, source_target_pairs={{1,0},{2,1},{3,2},{5,4},{6,5},{7,6},{9,8},{10,9},{11,10},{13,12},{... | collective-permute-start | bytes 5768 | tf_op jit(solution)/shard_map/ppermute | solution.py:33
  111.9 4.8 %collective-permute-start.1 = (f32[15,32]{1,0:T(8,128)S(1)}, f32[15,32]{1,0:T(8,128)S(1)}, u32[]{:S(2)}, u32[]{:S(2)}) collective-permute-start(f32[15,32]{1,0:T(8,128)S(1)} %collective-permute-done), channel_id=1, source_target_pairs={{0,1},{1,2},{2,3},{4,5},{5,6},{6,7},{8,9},{9,10},{10,11},{12,13},{... | collective-permute-start | bytes 5768 | tf_op jit(solution)/shard_map/ppermute | solution.py:33
  119.6 17.5 %all-to-all-start.5 = ((f32[64,1,192]{2,1,0:T(1,128)}), f32[64,1,192]{2,1,0:T(1,128)S(1)}, u32[]{:S(2)}, u32[]{:S(2)}) async-start(f32[64,1,192]{2,1,0:T(1,128)} %reshape.348), calls=%async_computation.5 | async-start | bytes 131072 | tf_op jit(solution)/shard_map/all_to_all | solution.py:156
  183.3 3.1 %collective-permute-start.6 = (f32[15,32]{1,0:T(8,128)S(1)}, f32[15,32]{1,0:T(8,128)S(1)}, u32[]{:S(2)}, u32[]{:S(2)}) collective-permute-start(f32[15,32]{1,0:T(8,128)S(1)} %get-tuple-element.68), channel_id=1, source_target_pairs={{4,0},{8,4},{12,8},{16,12},{20,16},{24,20},{28,24},{32,28},{36,32}... | collective-permute-start | bytes 5768 | tf_op jit(solution)/shard_map/ppermute | solution.py:25
  183.7 4.8 %collective-permute-start.4 = (f32[15,32]{1,0:T(8,128)S(1)}, f32[15,32]{1,0:T(8,128)S(1)}, u32[]{:S(2)}, u32[]{:S(2)}) collective-permute-start(f32[15,32]{1,0:T(8,128)S(1)} %get-tuple-element.67), channel_id=1, source_target_pairs={{0,4},{4,8},{8,12},{12,16},{16,20},{20,24},{24,28},{28,32},{32,36}... | collective-permute-start | bytes 5768 | tf_op jit(solution)/shard_map/ppermute | solution.py:22
  186.4 6.1 %collective-permute-start.7 = (f32[15,32]{1,0:T(8,128)S(1)}, f32[15,32]{1,0:T(8,128)S(1)}, u32[]{:S(2)}, u32[]{:S(2)}) collective-permute-start(f32[15,32]{1,0:T(8,128)S(1)} %collective-permute-done.6), channel_id=1, source_target_pairs={{1,0},{2,1},{3,2},{5,4},{6,5},{7,6},{9,8},{10,9},{11,10},{13,12},{... | collective-permute-start | bytes 5768 | tf_op jit(solution)/shard_map/ppermute | solution.py:33
  188.6 4.8 %collective-permute-start.5 = (f32[15,32]{1,0:T(8,128)S(1)}, f32[15,32]{1,0:T(8,128)S(1)}, u32[]{:S(2)}, u32[]{:S(2)}) collective-permute-start(f32[15,32]{1,0:T(8,128)S(1)} %collective-permute-done.4), channel_id=1, source_target_pairs={{0,1},{1,2},{2,3},{4,5},{5,6},{6,7},{8,9},{9,10},{10,11},{12,13},{... | collective-permute-start | bytes 5768 | tf_op jit(solution)/shard_map/ppermute | solution.py:33
where the time goes:
time: 196 us; the launch traced here: 194 us
  starting transfers between devices  50 us (26%)
  waiting for transfers between devices  35.3 us (18%)
  local copies, waits for them, and re-layouts  34.5 us (18%)
  blocking collectives  30.4 us (16%)
  other arithmetic  27.1 us (14%)
  between operations  13.3 us (7%)
  matrix products  3.81 us (2%)
    all_to_all x2, waiting for transfers between devices, per_device(): lax.all_to_all(served, SKY, split_axis=2, concat_axis=2, tiled=True)  19.4 us
    scatter-add x2, other arithmetic, per_device(): jnp.zeros((3, BLOCK_KNOTS, blocks_here + 1), jnp.float32).at[:, :, wanted]  17.2 us
    all_to_all x2, starting transfers between devices, per_device(): lax.all_to_all(served, SKY, split_axis=2, concat_axis=2, tiled=True)  16.1 us
    all_to_all x1, blocking collectives, per_device(): lax.all_to_all(outgoing, SKY, split_axis=2, concat_axis=2, tiled=True)  15.1 us
    unnamed x43, local copies, waits for them, and re-layouts  11.4 us
    ppermute x4, starting transfers between devices, from_behind(): lax.ppermute(value, axis, [(source, source + steps) for source in range(i...  10.5 us
    all_to_all x1, waiting for transfers between devices, per_device(): lax.all_to_all(outgoing, SKY, split_axis=2, concat_axis=2, tiled=True)  9.89 us
    all_to_all x1, starting transfers between devices, turned_blocks(): out = lax.all_to_all(out, axes[k], k, k, tiled=True)  9.43 us
  transfers between devices with their start and end apart: 13, of which 8 were waited for; matrix products, arithmetic and copies ran while one was open for 2% of the time, Pallas kernels for 0%

commit v1 on v0

v1 whole, which is shorter than its diff:
```python
import jax
import jax.numpy as jnp
from jax import lax
from jax.experimental import pallas as pl
from jax.experimental.pallas import tpu as pltpu
from jax.sharding import Mesh
from jax.sharding import PartitionSpec as P

F32 = jnp.float32
BF16 = jnp.bfloat16
I32 = jnp.int32
ROWS = 128
KNOTS = 16
CROSS = 128
SKY_N = 64
CHIPS = 32
TM_N = 4
SRC_N = 1024
RUN = 512
WIDE = RUN + 128
HEAD = 64
SKY = ("x", "z", "c")
SKY_TM = ("x", "z", "c", "tm")


def iota(shape, dim):
    return lax.broadcasted_iota(I32, shape, dim)


def dot(a, b):
    return jnp.dot(a.astype(BF16), b.astype(BF16), preferred_element_type=F32)


def dot_nt(a, b):
    return lax.dot_general(
        a.astype(BF16), b.astype(BF16), (((1,), (1,)), ((), ())), preferred_element_type=F32
    )


def halves(x):
    high = x.astype(BF16)
    return high, (x - high.astype(F32)).astype(BF16)


def thirds(x):
    high = x.astype(BF16).astype(F32)
    rest = x - high
    middle = rest.astype(BF16).astype(F32)
    return high, middle, rest - middle


def dot_split(values, table):
    vh, vl = halves(values)
    th, tl = halves(table)
    return dot(jnp.concatenate([vh, vl, vh], 1), jnp.concatenate([th, th, tl], 0))


def b_spline(moment_row, knot):
    tau = 1.5 + (KNOTS - 3) * (moment_row.astype(F32) + 0.5) / ROWS
    dist = jnp.abs(tau - knot.astype(F32))
    inner = 2.0 / 3.0 - dist * dist + 0.5 * dist * dist * dist
    rest = 2.0 - dist
    outer = rest * rest * rest / 6.0
    return jnp.where(dist < 1.0, inner, jnp.where(dist < 2.0, outer, 0.0))


def spline_by_lane():
    return b_spline(iota((128, 128), 1), iota((128, 128), 0) & 15)


def spline_by_row():
    return b_spline(iota((128, 128), 0), iota((128, 128), 1) & 15)


def fold_table():
    return jnp.where((iota((128, 128), 0) & 15) == (iota((128, 128), 1) & 15), 1.0, 0.0)


def as_columns(rows):
    sub = iota((128, 128), 0)
    square = jnp.zeros((128, 128), F32)
    for i, row in enumerate(rows):
        square = jnp.where(sub == i, row.astype(F32), square)
    turned = square.T
    return [turned[:, i : i + 1].astype(I32) for i in range(len(rows))]


class Meta:
    def __init__(self, kb_ref, slot_ref):
        kb, slot = kb_ref[...], slot_ref[...]
        self.h, self.lb, self.slot = kb >> 5, kb & 31, slot
        self.hc, self.lbc, self.slotc = as_columns([self.h, self.lb, slot])
        sub, lane = iota((128, 128), 0), iota((128, 128), 1)
        same = self.hc == self.h
        self.c = jnp.sum(
            jnp.where(same & (sub < lane), 1.0, 0.0), axis=0, keepdims=True
        ).astype(I32)
        self.cc = jnp.sum(
            jnp.where(same & (lane < sub), 1.0, 0.0), axis=1, keepdims=True
        ).astype(I32)
        self.group = lane >> 4

    def ghost_rows(self, live):
        sub = iota((8, 128), 0)
        place = self.c == (sub & 3)
        after = (self.h == SKY_N - 1) & (self.lb >= 30) & (sub < 4)
        before = (self.h == 0) & (self.lb <= 1) & (sub >= 4)
        used = iota((8, 128), 1) < live
        return jnp.where(place & (after | before) & used, 1.0, 0.0)

    def source_onehot(self):
        return jnp.where(iota((128, SRC_N), 1) == self.slotc, 1.0, 0.0).astype(BF16)


def attitude_term(att_ref, masked):
    spread = dot_split(jnp.concatenate(masked, 0), spline_by_lane())
    total = jnp.zeros((CROSS, ROWS), F32)
    for a in range(3):
        total = total + att_ref[a].astype(F32) * spread[a * 128 : a * 128 + 128]
    return total


def local_normal(src_ref, resid, onehot):
    lane = iota((128, 128), 1)
    square = jnp.zeros((128, 128), F32)
    for p in range(5):
        rhs = jnp.sum(src_ref[p].astype(F32) * resid, axis=1, keepdims=True)
        square = jnp.where(lane == p, rhs, square)
    rows = square.T[0:8]
    parts = dot(jnp.concatenate(thirds(rows), 0), onehot)
    return parts[0:8] + parts[8:16] + parts[16:24]


def gather_source(values8, onehot):
    parts = dot_nt(onehot, jnp.concatenate(thirds(values8), 0))
    return [
        parts[:, p : p + 1] + parts[:, 8 + p : 9 + p] + parts[:, 16 + p : 17 + p] for p in range(5)
    ]


def padded_rows(x):
    return jnp.concatenate([x, jnp.zeros((8 - x.shape[0], x.shape[1]), F32)], 0)


def first_kernel(
    live_ref, core_ref, near_ref, far_ref, obs_ref, att_ref, src_ref, slot_ref, kb_ref, sources_ref,
    resid_ref, plain_ref, up_ref, down_ref,
):
    meta = Meta(kb_ref, slot_ref)
    live, core = live_ref[0], core_ref[0]
    place = (meta.lbc >> 3) * CHIPS + (meta.hc >> 1)
    place = place + jnp.where((meta.hc & 1) == core, 0, 128)
    onehot = jnp.where(iota((128, 256), 1) == place, 1.0, 0.0)
    tables = []
    for a in range(3):
        rows = [ref[:, a, r, :] for ref in (near_ref, far_ref) for r in range(4)]
        tables += halves(jnp.concatenate(rows, 0))
    found = dot(onehot, jnp.concatenate(tables, 1))
    mine = meta.group == (meta.lbc & 7)
    masked = []
    for a in range(3):
        whole = found[:, 256 * a : 256 * a + 128] + found[:, 256 * a + 128 : 256 * a + 256]
        masked.append(jnp.where(mine, whole, 0.0))
    att_term = attitude_term(att_ref, masked)
    by_source = meta.source_onehot()
    values = gather_source(padded_rows(sources_ref[...]), by_source)
    src_term = jnp.zeros((CROSS, ROWS), F32)
    for p in range(5):
        src_term = src_term + src_ref[p].astype(F32) * values[p]
    used = jnp.where(iota((CROSS, 1), 0) < live, 1.0, 0.0)
    resid = (obs_ref[...] - src_term - att_term) * used
    resid_ref[...] = resid
    normal = local_normal(src_ref, resid, by_source)
    for ref in (plain_ref, up_ref, down_ref):
        for j in range(8):
            ref[8 * j : 8 * j + 8, :] = normal[:, 128 * j : 128 * j + 128]
    choose = meta.ghost_rows(live)
    high, low = halves(resid)
    pieces = [att_ref[a] for a in range(3)] + [src_ref[p] for p in range(5)] + [high, low]
    ghosts = dot(choose, jnp.concatenate(pieces, 1))
    items = [ghosts[:, 128 * i : 128 * i + 128] for i in range(10)]
    slot = jnp.sum(choose * meta.slot.astype(F32), axis=1, keepdims=True)
    block = jnp.sum(choose * meta.lb.astype(F32), axis=1, keepdims=True)
    items[8] = items[8] + items[9]
    items[9] = jnp.where(iota((8, 128), 1) < 64, slot, block)
    for q in range(5):
        even, odd = items[2 * q], items[2 * q + 1]
        low_row = HEAD + 8 * q
        up_ref[low_row : low_row + 8, :] = jnp.concatenate([even[0:4], odd[0:4]], 0)
        down_ref[low_row : low_row + 8, :] = jnp.concatenate([even[4:8], odd[4:8]], 0)


def middle_kernel(
    live_ref, got_ref, resid_in_ref, att_ref, src_ref, slot_ref, kb_ref, resid_ref, send_ref
):
    meta = Meta(kb_ref, slot_ref)
    peers = jnp.where(iota((128, SKY_N), 1) == meta.hc, 1.0, 0.0)
    table = jnp.concatenate([*halves(got_ref[:, 0, :]), *halves(got_ref[:, 1, :])], 1)
    found = dot(peers, table)
    front = found[:, 0:128] + found[:, 128:256]
    back = found[:, 256:384] + found[:, 384:512]
    masked = [
        jnp.where(meta.group == meta.cc, front, 0.0),
        jnp.where(meta.group == meta.cc + 4, front, 0.0),
        jnp.where(meta.group == meta.cc, back, 0.0),
    ]
    used = jnp.where(iota((CROSS, 1), 0) < live_ref[0], 1.0, 0.0)
    resid = resid_in_ref[...] - attitude_term(att_ref, masked) * used
    resid_ref[...] = resid
    normal = local_normal(src_ref, resid, meta.source_onehot())
    for j in range(8):
        send_ref[8 * j : 8 * j + 8, :] = normal[:, 128 * j : 128 * j + 128]
    ghosts = dot(meta.ghost_rows(live_ref[0]), jnp.concatenate(halves(resid), 1))
    send_ref[HEAD : HEAD + 8, :] = ghosts[:, 0:128] + ghosts[:, 128:256]


def return_kernel(
    live_ref, tm_ref, own_ref, below_ref, above_ref, across_ref, up_ref, down_ref, inverses_ref,
    sources_in_ref, resid_in_ref, att_ref, src_ref, slot_ref, kb_ref,
    out_ref, resid_ref, sources_ref, *, second,
):
    meta = Meta(kb_ref, slot_ref)
    tm = tm_ref[0]
    total = (
        own_ref[0:HEAD, :] + across_ref[0:HEAD, :] + below_ref[0:HEAD, :] + above_ref[0:HEAD, :]
    )
    normal = jnp.concatenate([total[8 * j : 8 * j + 8] for j in range(8)], 1)
    sub8 = iota((8, SRC_N), 0)
    step = jnp.zeros((8, SRC_N), F32)
    for p in range(5):
        row = jnp.sum(inverses_ref[p] * normal[0:5], axis=0, keepdims=True)
        step = jnp.where(sub8 == p, row, step)
    sources_ref[...] = sources_in_ref[...] + step[0:5]
    ghost8 = iota((8, 128), 0)
    there = jnp.where(ghost8 < 4, jnp.where(tm > 0, 1.0, 0.0), jnp.where(tm < TM_N - 1, 1.0, 0.0))

    def item(i):
        row = HEAD + 4 * i
        return jnp.concatenate([up_ref[row : row + 4, :], down_ref[row : row + 4, :]], 0)

    facts = item(9)
    ghost_slot = facts[:, 0:1].astype(I32)
    ghost_block = facts[:, 64:65].astype(I32)
    ghost_onehot = jnp.where(iota((8, SRC_N), 1) == ghost_slot, 1.0, 0.0)
    values = gather_source(step, meta.source_onehot())
    ghost_values = gather_source(step, ghost_onehot)
    change = jnp.zeros((CROSS, ROWS), F32)
    ghost_change = jnp.zeros((8, ROWS), F32)
    for p in range(5):
        change = change + src_ref[p].astype(F32) * values[p]
        ghost_change = ghost_change + item(3 + p) * ghost_values[p]
    used = jnp.where(iota((CROSS, 1), 0) < live_ref[0], 1.0, 0.0)
    resid = resid_in_ref[...] - used * change
    resid_ref[...] = resid
    if second:
        ghost_resid = jnp.concatenate(
            [below_ref[HEAD : HEAD + 4, :], above_ref[HEAD + 4 : HEAD + 8, :]], 0
        )
    else:
        ghost_resid = item(8)
    ghost_resid = (ghost_resid - ghost_change) * there
    rows = [att_ref[a].astype(F32) * resid for a in range(3)]
    rows += [item(a) * ghost_resid for a in range(3)]
    grads = dot_split(jnp.concatenate(rows, 0), spline_by_row())
    to_row = jnp.where(
        meta.lb <= 1, meta.h - 1, jnp.where(meta.lb >= 30, meta.h + 1, jnp.full_like(meta.h, -1))
    )
    edge_group = jnp.where(meta.lbc <= 1, meta.lbc, meta.lbc - 24)
    own = meta.group == meta.cc + 2
    edge = meta.group == edge_group
    peer = iota((SKY_N, 128), 0)
    onehot = jnp.concatenate(
        [jnp.where(peer == meta.h, 1.0, 0.0), jnp.where(peer == to_row, 1.0, 0.0)], 1
    )
    top, bottom = [], []
    for a in range(3):
        g = grads[128 * a : 128 * a + 128]
        top += halves(jnp.where(own, g, 0.0))
        bottom += halves(jnp.where(edge, g, 0.0))
    if not second:
        top.append(jnp.where(own, (meta.lbc + 1).astype(F32), 0.0).astype(BF16))
        bottom.append(jnp.zeros((128, 128), BF16))
    table = jnp.concatenate([jnp.concatenate(top, 1), jnp.concatenate(bottom, 1)], 0)
    packed = dot(onehot, table)
    ghost_group = iota((8, 128), 1) >> 4
    ghost_own = ghost_group == jnp.where(ghost8[:, 0:1] < 4, ghost_block - 24, ghost_block)
    for a in range(3):
        ghost = jnp.where(ghost_own, grads[384 + 8 * a : 392 + 8 * a], 0.0)
        from_below = jnp.sum(jnp.where(ghost8 < 4, ghost, 0.0), axis=0, keepdims=True)
        from_above = jnp.sum(jnp.where(ghost8 >= 4, ghost, 0.0), axis=0, keepdims=True)
        block = packed[:, 256 * a : 256 * a + 128] + packed[:, 256 * a + 128 : 256 * a + 256]
        block = block + jnp.where(peer == 0, from_below, 0.0)
        block = block + jnp.where(peer == SKY_N - 1, from_above, 0.0)
        out_ref[:, a, :] = block
    if second:
        out_ref[:, 3, :] = jnp.zeros((SKY_N, 128), F32)
    else:
        out_ref[:, 3, :] = packed[:, 768:896]


def smooth_kernel(
    offsets_ref, got_ref, index_ref, knots_in_ref, bands_ref, before_ref, after_ref, *outs, last
):
    knots_ref = outs[0]
    lane = iota((SKY_N, 128), 1)
    index = index_ref[:, 3, :]
    square = jnp.concatenate([index, jnp.zeros((128 - SKY_N, 128), F32)], 0).T
    block32 = (iota((32, SKY_N), 0) + 1).astype(F32)
    pick = jnp.concatenate(
        [
            jnp.where(square[16 * (2 + c) : 16 * (2 + c) + 1, 0:SKY_N] == block32, 1.0, 0.0)
            for c in range(4)
        ],
        0,
    )
    got = [got_ref[:, a, :] for a in range(3)]
    table = jnp.concatenate([part for g in got for part in halves(g)], 1)
    summed = dot(pick, table)
    row128 = iota((128, 128), 0)
    group128 = iota((128, 128), 1) >> 4
    keep = group128 == (row128 >> 5) + 2
    fold = fold_table()
    stack = []
    for a in range(3):
        one = summed[:, 256 * a : 256 * a + 128] + summed[:, 256 * a + 128 : 256 * a + 256]
        one = jnp.where(keep, one, 0.0)
        stack.append(one[0:32] + one[32:64] + one[64:96] + one[96:128])
    high, low = halves(jnp.concatenate(stack, 0))
    spread = dot(jnp.concatenate([high, low], 1), jnp.concatenate([fold, fold], 0))
    in_row = (iota((8, 128), 1) >> 4) == iota((8, 128), 0)
    sub_w = iota((8, WIDE), 0)
    grad = jnp.zeros((8, WIDE), F32)
    for a in range(3):
        tiles = []
        for r in range(4):
            piece = spread[32 * a + 8 * r : 32 * a + 8 * r + 8]
            tiles.append(jnp.sum(jnp.where(in_row, piece, 0.0), axis=0, keepdims=True))
        rim = jnp.where((lane < 32) | (lane >= 96), got[a], 0.0)
        tiles.append(jnp.sum(rim, axis=0, keepdims=True))
        grad = jnp.where(sub_w == a, jnp.concatenate(tiles, 1), grad)
    lane3 = iota((3, 128), 1)

    def wide(i):
        rim = jnp.where(
            lane3 < 32,
            after_ref[3 * i : 3 * i + 3, :],
            jnp.where(lane3 >= 96, before_ref[3 * i : 3 * i + 3, :], 0.0),
        )
        return padded_rows(jnp.concatenate([bands_ref[3 * i : 3 * i + 3, :], rim], 1))

    bands = [wide(b) for b in range(3)]
    diag = wide(3) + 2.0 * (bands[0] + bands[1] + bands[2])
    diag = jnp.where(diag > 0.0, diag, 1.0)
    delta = grad / diag
    for _ in range(2):
        total = jnp.zeros((8, WIDE), F32)
        for b in range(3):
            offset = offsets_ref[b]
            upper = pltpu.roll(delta, WIDE - offset, 1)
            lower = pltpu.roll(delta, offset, 1)
            total = total + bands[b] * (upper + lower)
        delta = (grad + total) / diag
    knots_ref[...] = knots_in_ref[...] + delta[0:3, 0:RUN]
    if last:
        return
    send_ref = outs[1]
    sub8 = iota((8, 128), 0)
    tables = []
    for a in range(3):
        rows = jnp.zeros((8, 128), F32)
        for r in range(4):
            rows = jnp.where(sub8 == r, delta[a : a + 1, 128 * r : 128 * r + 128], rows)
        tables += halves(rows)
    slots = [index[:, 16 * (2 + c) : 16 * (2 + c) + 1].astype(I32) - 1 for c in range(4)]
    slot = jnp.concatenate(slots, 0)
    by_row = jnp.where(iota((4 * SKY_N, 8), 1) == (slot >> 3), 1.0, 0.0)
    found = dot(by_row, jnp.concatenate(tables, 1))
    mine = (iota((4 * SKY_N, 128), 1) >> 4) == (slot & 7)
    masked = []
    for a in range(3):
        one = found[:, 256 * a : 256 * a + 128] + found[:, 256 * a + 128 : 256 * a + 256]
        masked.append(jnp.where(mine, one, 0.0))
    high, low = halves(jnp.concatenate(masked, 0))
    spread = dot(jnp.concatenate([high, low], 1), jnp.concatenate([fold, fold], 0))
    group = lane >> 4
    front = jnp.zeros((SKY_N, 128), F32)
    back = jnp.zeros((SKY_N, 128), F32)
    for c in range(4):
        part = [
            spread[4 * SKY_N * a + SKY_N * c : 4 * SKY_N * a + SKY_N * (c + 1)] for a in range(3)
        ]
        front = jnp.where(group == c, part[0], jnp.where(group == c + 4, part[1], front))
        back = jnp.where(group == c, part[2], back)
    send_ref[:, 0, :] = front
    send_ref[:, 1, :] = back


def run_kernel(body, scalars, outs, *args, **static):
    specs = [
        pl.BlockSpec(memory_space=pltpu.SMEM if i < scalars else pltpu.VMEM)
        for i in range(len(args))
    ]

    def kernel(*refs):
        body(*refs, **static)

    return pl.pallas_call(
        kernel,
        out_shape=[jax.ShapeDtypeStruct(shape, F32) for shape in outs],
        in_specs=specs,
        out_specs=[pl.BlockSpec(memory_space=pltpu.VMEM) for _ in outs],
        compiler_params=pltpu.CompilerParams(vmem_limit_bytes=32 * 1024 * 1024),
    )(*args)


def shifts(k):
    return [(i, (i + k) % TM_N) for i in range(TM_N)]


def per_device(
    observed,
    att_partials,
    src_partials,
    src_slot,
    knot_block,
    live_count,
    sources,
    inverses,
    attitude,
    band_coef,
    extra_diag,
    band_offsets,
):
    core = lax.axis_index("c").astype(I32).reshape(1)
    tm = lax.axis_index("tm").astype(I32).reshape(1)
    slot = src_slot.reshape(1, CROSS)
    kb = knot_block.reshape(1, CROSS)
    knots = attitude[:, 0, :]
    static = jnp.concatenate([band_coef.reshape(9, RUN), extra_diag.reshape(3, RUN)], 0)
    chain = [s * TM_N + t for t in range(TM_N) for s in range(SKY_N)]
    pairs = list(zip(chain[:-1], chain[1:], strict=True))
    before = lax.ppermute(static[:, RUN - 128 :], SKY_TM, pairs)
    after = lax.ppermute(static[:, :128], SKY_TM, [(b, a) for a, b in pairs])

    dense = jnp.broadcast_to(attitude.reshape(1, 3, 4, 128), (CHIPS, 3, 4, 128))
    near = lax.all_to_all(dense, ("x", "z"), 0, 0, tiled=True)
    far = lax.ppermute(near, "c", [(0, 1), (1, 0)])
    resid, plain, up, down = run_kernel(
        first_kernel, 2, [(CROSS, ROWS), (HEAD, 128), (HEAD + 40, 128), (HEAD + 40, 128)],
        live_count, core, near, far, observed, att_partials, src_partials, slot, kb, sources,
    )
    up = lax.ppermute(up, "tm", shifts(1))
    down = lax.ppermute(down, "tm", shifts(-1))
    across = lax.ppermute(plain, "tm", shifts(2))
    back_shapes = [(SKY_N, 4, 128), (CROSS, ROWS), (5, SRC_N)]
    outgoing, resid, sources = run_kernel(
        return_kernel, 2, back_shapes,
        live_count, tm, plain, up, down, across, up, down, inverses, sources, resid,
        att_partials, src_partials, slot, kb, second=False,
    )
    first = lax.all_to_all(outgoing, SKY, 0, 0, tiled=True)
    knots, served = run_kernel(
        smooth_kernel, 1, [(3, RUN), (SKY_N, 2, 128)],
        band_offsets, first, first, knots, static, before, after, last=False,
    )
    arrived = lax.all_to_all(served, SKY, 0, 0, tiled=True)
    resid, mine = run_kernel(
        middle_kernel, 1, [(CROSS, ROWS), (HEAD + 8, 128)],
        live_count, arrived, resid, att_partials, src_partials, slot, kb,
    )
    below = lax.ppermute(mine, "tm", shifts(1))
    above = lax.ppermute(mine, "tm", shifts(-1))
    across = lax.ppermute(mine, "tm", shifts(2))
    outgoing, resid, sources = run_kernel(
        return_kernel, 2, back_shapes,
        live_count, tm, mine, below, above, across, up, down, inverses, sources, resid,
        att_partials, src_partials, slot, kb, second=True,
    )
    second = lax.all_to_all(outgoing, SKY, 0, 0, tiled=True)
    (knots,) = run_kernel(
        smooth_kernel, 1, [(3, RUN)],
        band_offsets, second, first, knots, static, before, after, last=True,
    )
    return (sources, knots[:, None, :])


def solution(mesh):
    torus = Mesh(mesh.devices.reshape(4, 8, 2, mesh.shape["tm"]), SKY_TM)
    return jax.shard_map(
        per_device,
        mesh=torus,
        in_specs=(
            P(SKY_TM, None),
            P(None, SKY_TM, None),
            P(None, SKY_TM, None),
            P(SKY_TM),
            P(SKY_TM),
            P(SKY_TM),
            P(None, SKY),
            P(None, None, SKY),
            P(None, "tm", SKY),
            P(None, None, "tm", SKY),
            P(None, "tm", SKY),
            P(),
        ),
        out_specs=(P(None, SKY), P(None, "tm", SKY)),
        check_vma=False,
    )
```

time: 196 us -> 104 us (0.53)
  local copies, waits for them, and re-layouts: 34.5 us -> 2.04 us
  other arithmetic: 27.1 us -> 0.08 us
  starting transfers between devices: 50 us -> 24.2 us
  blocking collectives: 30.4 us -> 55.2 us
  waiting for transfers between devices: 35.3 us -> 11.7 us
  between operations: 13.3 us -> 1.47 us
  Pallas kernels: 0 us -> 8.81 us
  matrix products: 3.81 us -> 0 us
    all_to_all x5 -> x1, starting transfers between devices: 35.7 us -> 6.38 us  [per_device(): first = lax.all_to_all(outgoing, SKY, 0, 0, tiled=True)]
    all_to_all x5 -> x1, waiting for transfers between devices: 32.4 us -> 3.88 us  [per_device(): first = lax.all_to_all(outgoing, SKY, 0, 0, tiled=True)]
    all_to_all x3, blocking collectives: 30.4 us -> 55.2 us  [the longest x1 21.2 us: per_device(): near = lax.all_to_all(dense, ('x', 'z'), 0, 0, tiled=True)]
    scatter-add x4 -> x0, other arithmetic: 19.5 us -> none  [the longest x2 17.2 us: per_device(): jnp.zeros((3, BLOCK_KNOTS, blocks_here + 1), jnp.float32).at[:, :, wanted]]
    unnamed x43 -> x25, local copies, waits for them, and re-layouts: 11.4 us -> 1.3 us
    scatter x3 -> x0, local copies, waits for them, and re-layouts: 9.63 us -> none  [the longest x2 8.65 us: per_device(): outgoing = jnp.zeros((3, BLOCK_KNOTS, slots_total), jnp.float32).at[:, :,...]
    pallas_call x0 -> x6, Pallas kernels: none -> 8.81 us  [run_kernel(): pl.pallas_call(kernel, out_shape=[jax.ShapeDtypeStruct(shape, F32) for sh...]
    gather x8 -> x0, local copies, waits for them, and re-layouts: 6.09 us -> none  [the longest x2 1.98 us: per_device(): served = jnp.take(jnp.transpose(own_blocks, (0, 2, 1)), wanted, axis=2)]
  transfers between devices with their start and end apart: 13 -> 10, of which waited for: 8 -> 6; matrix products, arithmetic and copies ran while one was open for 2% -> 0% of each run, Pallas kernels for 0% -> 0%
where the time goes in v1:
time: 104 us
  blocking collectives  55.2 us (53%)
  starting transfers between devices  24.2 us (23%)
  waiting for transfers between devices  11.7 us (11%)
  Pallas kernels  8.81 us (8%)
  local copies, waits for them, and re-layouts  2.04 us (2%)
  between operations  1.47 us (1%)
    all_to_all x1, blocking collectives, per_device(): near = lax.all_to_all(dense, ('x', 'z'), 0, 0, tiled=True)  21.2 us
    all_to_all x1, blocking collectives, per_device(): arrived = lax.all_to_all(served, SKY, 0, 0, tiled=True)  18.1 us
    all_to_all x1, blocking collectives, per_device(): second = lax.all_to_all(outgoing, SKY, 0, 0, tiled=True)  15.9 us
    pallas_call x6, Pallas kernels, run_kernel(): pl.pallas_call(kernel, out_shape=[jax.ShapeDtypeStruct(shape, F32) for sh...  8.81 us
    all_to_all x1, starting transfers between devices, per_device(): first = lax.all_to_all(outgoing, SKY, 0, 0, tiled=True)  6.38 us
    all_to_all x1, waiting for transfers between devices, per_device(): first = lax.all_to_all(outgoing, SKY, 0, 0, tiled=True)  3.88 us
    ppermute x1, starting transfers between devices, per_device(): before = lax.ppermute(static[:, RUN - 128:], SKY_TM, pairs)  3.2 us
    ppermute x1, starting transfers between devices, per_device(): across = lax.ppermute(mine, 'tm', shifts(2))  3.01 us
  transfers between devices with their start and end apart: 10, of which 6 were waited for; matrix products, arithmetic and copies ran while one was open for 0% of the time, Pallas kernels for 0%

profile of v1, /device:TPU:1, one launch (start us, length us, event | category | flops | bytes accessed | tf_op | source)
XLA Modules:
  0.0 103.6 jit_solution(13541353792081678731)
XLA Ops:
  0.6 0.7 broadcast_in_dim.11
  1.4 0.0 copy-start
  1.4 0.0 copy-start.1
  1.4 0.0 copy-start.3
  1.4 0.0 copy-start.4
  1.4 21.2 %all_to_all.20.refs_2_ = f32[32,3,4,128]{3,2,1,0:T(4,128)S(1)} all-to-all(f32[32,3,4,128]{3,2,1,0:T(4,128)S(1)} %broadcast_in_dim.11), channel_id=1, replica_groups=mesh['x'=4,'z'=8,'c'=2,'tm'=4] {'x','z'}, dimensions={0} | all-to-all | bytes 393216 | tf_op jit(solution)/shard_map/all_to_all | solution.py:446
  22.6 2.8 %collective-permute-start = (f32[32,3,4,128]{3,2,1,0:T(4,128)S(1)}, f32[32,3,4,128]{3,2,1,0:T(4,128)S(1)}, u32[]{:S(2)}, u32[]{:S(2)}) collective-permute-start(f32[32,3,4,128]{3,2,1,0:T(4,128)S(1)} %all_to_all.20.refs_2_), channel_id=1, source_target_pairs={{0,4},{4,0},{1,5},{5,1},{2,6},{6,2},{3,7},{7,3},{8,12},{12,8},{9,1... | collective-permute-start | bytes 589832 | tf_op jit(solution)/shard_map/ppermute | solution.py:447
  26.1 0.4 collective-permute-done.refs_3_
  26.5 0.0 copy-done
  26.5 0.0 copy-done.1
  26.5 0.0 copy-done.3
  26.5 0.0 copy-done.4
  26.5 0.6 copy-done.5
  27.2 0.0 copy-done.6
  27.2 1.4 %shard_map.131 = (f32[128,128]{1,0:T(8,128)S(1)}, f32[64,128]{1,0:T(8,128)S(1)}, f32[104,128]{1,0:T(8,128)S(1)}, f32[104,128]{1,0:T(8,128)S(1)}) custom-call(s32[1]{0:T(128)S(6)} %copy.22.refs_0_, s32[1]{0:T(128)} %bitcast.1.refs_1_, f32[32,3,4,128]{3,2,1,0:T(4,128)S(1)} %all_to_all.20.refs_2_, f32[32,3,4,128]{3,2,1,0:T(4,128)S(1)} %collective-permute-done.refs_3_, ...), custom_call_target="tpu_custom_call" | custom-call | tf_op jit(solution)/shard_map/pallas_call | solution.py:407
  28.6 1.4 %collective-permute-start.1 = (f32[104,128]{1,0:T(8,128)S(1)}, f32[104,128]{1,0:T(8,128)S(1)}, u32[]{:S(2)}, u32[]{:S(2)}) collective-permute-start(f32[104,128]{1,0:T(8,128)S(1)} %get-tuple-element.16), channel_id=1, source_target_pairs={{0,1},{1,2},{2,3},{3,0},{4,5},{5,6},{6,7},{7,4},{8,9},{9,10},{10,1... | collective-permute-start | bytes 159752 | tf_op jit(solution)/shard_map/ppermute | solution.py:452
  30.0 1.5 %collective-permute-start.2 = (f32[104,128]{1,0:T(8,128)S(1)}, f32[104,128]{1,0:T(8,128)S(1)}, u32[]{:S(2)}, u32[]{:S(2)}) collective-permute-start(f32[104,128]{1,0:T(8,128)S(1)} %get-tuple-element.17), channel_id=1, source_target_pairs={{0,3},{1,0},{2,1},{3,2},{4,7},{5,4},{6,5},{7,6},{8,11},{9,8},{10,9... | collective-permute-start | bytes 159752 | tf_op jit(solution)/shard_map/ppermute | solution.py:453
  31.5 1.6 %collective-permute-start.3 = (f32[64,128]{1,0:T(8,128)S(1)}, f32[64,128]{1,0:T(8,128)S(1)}, u32[]{:S(2)}, u32[]{:S(2)}) collective-permute-start(f32[64,128]{1,0:T(8,128)S(1)} %get-tuple-element.15.refs_2_), channel_id=1, source_target_pairs={{0,2},{1,3},{2,0},{3,1},{4,6},{5,7},{6,4},{7,5},{8,10},{9,11},{10,... | collective-permute-start | bytes 98312 | tf_op jit(solution)/shard_map/ppermute | solution.py:454
  33.1 2.7 %collective-permute-done.3.refs_5_ = f32[64,128]{1,0:T(8,128)S(1)} collective-permute-done((f32[64,128]{1,0:T(8,128)S(1)}, f32[64,128]{1,0:T(8,128)S(1)}, u32[]{:S(2)}, u32[]{:S(2)}) %collective-permute-start.3) | collective-permute-done | bytes 32800 | tf_op jit(solution)/shard_map/ppermute | solution.py:454
  35.8 0.0 collective-permute-done.1.refs_3_.refs_6_
  35.8 0.0 collective-permute-done.2.refs_4_.refs_7_
  35.8 0.0 copy-done.2
  35.8 1.7 %shard_map.132 = (f32[64,4,128]{2,1,0:T(4,128)}, f32[128,128]{1,0:T(8,128)S(1)}, f32[5,1024]{1,0:T(8,128)S(1)}) custom-call(s32[1]{0:T(128)S(6)} %copy.22.refs_0_, s32[1]{0:T(128)} %bitcast.refs_1_, f32[64,128]{1,0:T(8,128)S(1)} %get-tuple-element.15.refs_2_, f32[104,128]{1,0:T(8,128)S(1)} %collective-permute-done.1.refs_3_.refs_6_, ...), custom_call_target="tpu_custom_call" | custom-call | tf_op jit(solution)/shard_map/pallas_call | solution.py:407
  37.5 6.4 %all-to-all-start.1 = ((f32[64,4,128]{2,1,0:T(4,128)}), f32[64,4,128]{2,1,0:T(4,128)S(1)}, u32[]{:S(2)}, u32[]{:S(2)}) async-start(f32[64,4,128]{2,1,0:T(4,128)} %get-tuple-element.19), calls=%async_computation.1 | async-start | bytes 262144 | tf_op jit(solution)/shard_map/all_to_all | solution.py:461
  43.9 0.0 copy-done.10
  43.9 0.0 copy-done.9
  43.9 0.1 reduce
  44.0 2.4 %collective-permute-start.5 = (f32[12,128]{1,0:T(8,128)S(1)}, f32[12,128]{1,0:T(8,128)S(1)}, u32[]{:S(2)}, u32[]{:S(2)}) collective-permute-start(f32[12,128]{1,0:T(8,128)S(1)} %get-tuple-element.30), channel_id=1, source_target_pairs={{4,0},{8,4},{12,8},{16,12},{20,16},{24,20},{28,24},{32,28},{36,32}... | collective-permute-start | bytes 18440 | tf_op jit(solution)/shard_map/ppermute | solution.py:443
  46.4 0.0 copy-start.8
  46.4 3.2 %collective-permute-start.4 = (f32[12,128]{1,0:T(8,128)S(1)}, f32[12,128]{1,0:T(8,128)S(1)}, u32[]{:S(2)}, u32[]{:S(2)}) collective-permute-start(f32[12,128]{1,0:T(8,128)S(1)} %get-tuple-element.31), channel_id=1, source_target_pairs={{0,4},{4,8},{8,12},{12,16},{16,20},{20,24},{24,28},{28,32},{32,36}... | collective-permute-start | bytes 18440 | tf_op jit(solution)/shard_map/ppermute | solution.py:442
  49.6 0.0 copy-start.7
  49.6 0.0 collective-permute-done.5.refs_6_
  49.6 0.7 collective-permute-done.4.refs_5_
  50.4 3.9 %all-to-all-done.1.refs_1_.refs_2_ = f32[64,4,128]{2,1,0:T(4,128)S(1)} async-done(((f32[64,4,128]{2,1,0:T(4,128)}), f32[64,4,128]{2,1,0:T(4,128)S(1)}, u32[]{:S(2)}, u32[]{:S(2)}) %all-to-all-start.1) | async-done | bytes 131104 | tf_op jit(solution)/shard_map/all_to_all | solution.py:461
  54.2 0.0 copy-done.7
  54.2 1.9 %shard_map.133 = (f32[3,512]{1,0:T(4,128)S(1)}, f32[64,2,128]{2,1,0:T(2,128)S(1)}) custom-call(s32[3]{0:T(128)S(1)} %copy-done.7, f32[64,4,128]{2,1,0:T(4,128)S(1)} %all-to-all-done.1.refs_1_.refs_2_, f32[64,4,128]{2,1,0:T(4,128)S(1)} %all-to-all-done.1.refs_1_.refs_2_, f32[3,512]{1,0:T(4,128)S(1)} %bitcast.12, f32[12,512]{1,0:T(8,128)S(1)} %pad_maximum_fusion.refs_4_, ...), custom_call_target="tpu_custom_call" | custom-call | tf_op jit(solution)/shard_map/pallas_call | solution.py:407
  56.2 18.1 %all_to_all.21.refs_1_ = f32[64,2,128]{2,1,0:T(2,128)S(1)} all-to-all(f32[64,2,128]{2,1,0:T(2,128)S(1)} %get-tuple-element.20), channel_id=1, replica_groups=mesh['x'=4,'z'=8,'c'=2,'tm'=4] {'x','z','c'}, dimensions={0} | all-to-all | bytes 131072 | tf_op jit(solution)/shard_map/all_to_all | solution.py:466
  74.2 1.0 shard_map.134
  75.2 3.0 %collective-permute-start.8 = (f32[72,128]{1,0:T(8,128)S(1)}, f32[72,128]{1,0:T(8,128)S(1)}, u32[]{:S(2)}, u32[]{:S(2)}) collective-permute-start(f32[72,128]{1,0:T(8,128)S(1)} %get-tuple-element.22.refs_2_), channel_id=1, source_target_pairs={{0,2},{1,3},{2,0},{3,1},{4,6},{5,7},{6,4},{7,5},{8,10},{9,11},{10,... | collective-permute-start | bytes 110600 | tf_op jit(solution)/shard_map/ppermute | solution.py:473
  78.2 2.0 %collective-permute-start.7 = (f32[72,128]{1,0:T(8,128)S(1)}, f32[72,128]{1,0:T(8,128)S(1)}, u32[]{:S(2)}, u32[]{:S(2)}) collective-permute-start(f32[72,128]{1,0:T(8,128)S(1)} %get-tuple-element.22.refs_2_), channel_id=1, source_target_pairs={{0,3},{1,0},{2,1},{3,2},{4,7},{5,4},{6,5},{7,6},{8,11},{9,8},{10,9... | collective-permute-start | bytes 110600 | tf_op jit(solution)/shard_map/ppermute | solution.py:472
  80.2 0.0 collective-permute-start.6
  80.2 0.0 collective-permute-done.8.refs_5_
  80.2 1.1 %collective-permute-done.7.refs_4_ = f32[72,128]{1,0:T(8,128)S(1)} collective-permute-done((f32[72,128]{1,0:T(8,128)S(1)}, f32[72,128]{1,0:T(8,128)S(1)}, u32[]{:S(2)}, u32[]{:S(2)}) %collective-permute-start.7) | collective-permute-done | bytes 36896 | tf_op jit(solution)/shard_map/ppermute | solution.py:472
  81.4 2.9 %collective-permute-done.6.refs_3_ = f32[72,128]{1,0:T(8,128)S(1)} collective-permute-done((f32[72,128]{1,0:T(8,128)S(1)}, f32[72,128]{1,0:T(8,128)S(1)}, u32[]{:S(2)}, u32[]{:S(2)}) %collective-permute-start.6) | collective-permute-done | bytes 36896 | tf_op jit(solution)/shard_map/ppermute | solution.py:471
  84.3 1.4 %shard_map.135 = (f32[64,4,128]{2,1,0:T(4,128)S(1)}, f32[128,128]{1,0:T(8,128)}, f32[5,1024]{1,0:T(8,128)}) custom-call(s32[1]{0:T(128)S(6)} %copy.22.refs_0_, s32[1]{0:T(128)} %bitcast.refs_1_, f32[72,128]{1,0:T(8,128)S(1)} %get-tuple-element.22.refs_2_, f32[72,128]{1,0:T(8,128)S(1)} %collective-permute-done.6.refs_3_, ...), custom_call_target="tpu_custom_call" | custom-call | tf_op jit(solution)/shard_map/pallas_call | solution.py:407
  85.6 15.9 %all_to_all.22.refs_1_ = f32[64,4,128]{2,1,0:T(4,128)S(1)} all-to-all(f32[64,4,128]{2,1,0:T(4,128)S(1)} %get-tuple-element.26), channel_id=1, replica_groups=mesh['x'=4,'z'=8,'c'=2,'tm'=4] {'x','z','c'}, dimensions={0} | all-to-all | bytes 262144 | tf_op jit(solution)/shard_map/all_to_all | solution.py:479
  101.6 1.4 %shard_map.136 = f32[3,512]{1,0:T(4,128)S(1)} custom-call(s32[3]{0:T(128)S(1)} %copy-done.7, f32[64,4,128]{2,1,0:T(4,128)S(1)} %all_to_all.22.refs_1_, f32[64,4,128]{2,1,0:T(4,128)S(1)} %all-to-all-done.1.refs_1_.refs_2_, f32[3,512]{1,0:T(4,128)S(1)} %get-tuple-element.27.refs_3_, f32[12,512]{1,0:T(8,128)S(1)} %pad_maximum_fusion.refs_4_, ...), custom_call_target="tpu_custom_call" | custom-call | tf_op jit(solution)/shard_map/pallas_call | solution.py:407
  103.0 0.6 copy.14
  (11 shorter events, 0.1 us)
Async XLA Ops:
  1.4 25.2 %copy-start = (bf16[5,128,128]{2,1,0:T(8,128)(2,1)S(1)}, bf16[5,128,128]{2,1,0:T(8,128)(2,1)}, u32[]{:S(2)}) copy-start(bf16[5,128,128]{2,1,0:T(8,128)(2,1)} %refs_12_.3) | copy-start | bytes 491524
  1.4 25.2 %copy-start.1 = (bf16[3,128,128]{2,1,0:T(8,128)(2,1)S(1)}, bf16[3,128,128]{2,1,0:T(8,128)(2,1)}, u32[]{:S(2)}) copy-start(bf16[3,128,128]{2,1,0:T(8,128)(2,1)} %refs_11_.3) | copy-start | bytes 294916
  1.4 25.2 %copy-start.3 = (f32[5,1024]{1,0:T(8,128)S(1)}, f32[5,1024]{1,0:T(8,128)}, u32[]{:S(2)}) copy-start(f32[5,1024]{1,0:T(8,128)} %refs_9_.3) | copy-start | bytes 61444
  1.4 25.2 %copy-start.4 = (f32[128,128]{1,0:T(8,128)S(1)}, f32[128,128]{1,0:T(8,128)}, u32[]{:S(2)}) copy-start(f32[128,128]{1,0:T(8,128)} %refs_4_.2) | copy-start | bytes 196612
  22.6 3.9 %collective-permute-start = (f32[32,3,4,128]{3,2,1,0:T(4,128)S(1)}, f32[32,3,4,128]{3,2,1,0:T(4,128)S(1)}, u32[]{:S(2)}, u32[]{:S(2)}) collective-permute-start(f32[32,3,4,128]{3,2,1,0:T(4,128)S(1)} %all_to_all.20.refs_2_), channel_id=1, source_target_pairs={{0,4},{4,0},{1,5},{5,1},{2,6},{6,2},{3,7},{7,3},{8,12},{12,8},{9,1... | collective-permute-start | bytes 589832 | tf_op jit(solution)/shard_map/ppermute | solution.py:447
  26.5 0.7 copy-start.5
  26.5 0.7 copy-start.6
  27.2 8.6 %copy-start.2 = (f32[5,5,1024]{2,1,0:T(8,128)S(1)}, f32[5,5,1024]{2,1,0:T(8,128)}, u32[]{:S(2)}) copy-start(f32[5,5,1024]{2,1,0:T(8,128)} %refs_8_.3) | copy-start | bytes 307204
  28.6 7.2 %collective-permute-start.1 = (f32[104,128]{1,0:T(8,128)S(1)}, f32[104,128]{1,0:T(8,128)S(1)}, u32[]{:S(2)}, u32[]{:S(2)}) collective-permute-start(f32[104,128]{1,0:T(8,128)S(1)} %get-tuple-element.16), channel_id=1, source_target_pairs={{0,1},{1,2},{2,3},{3,0},{4,5},{5,6},{6,7},{7,4},{8,9},{9,10},{10,1... | collective-permute-start | bytes 159752 | tf_op jit(solution)/shard_map/ppermute | solution.py:452
  30.0 5.8 %collective-permute-start.2 = (f32[104,128]{1,0:T(8,128)S(1)}, f32[104,128]{1,0:T(8,128)S(1)}, u32[]{:S(2)}, u32[]{:S(2)}) collective-permute-start(f32[104,128]{1,0:T(8,128)S(1)} %get-tuple-element.17), channel_id=1, source_target_pairs={{0,3},{1,0},{2,1},{3,2},{4,7},{5,4},{6,5},{7,6},{8,11},{9,8},{10,9... | collective-permute-start | bytes 159752 | tf_op jit(solution)/shard_map/ppermute | solution.py:453
  31.5 4.3 %collective-permute-start.3 = (f32[64,128]{1,0:T(8,128)S(1)}, f32[64,128]{1,0:T(8,128)S(1)}, u32[]{:S(2)}, u32[]{:S(2)}) collective-permute-start(f32[64,128]{1,0:T(8,128)S(1)} %get-tuple-element.15.refs_2_), channel_id=1, source_target_pairs={{0,2},{1,3},{2,0},{3,1},{4,6},{5,7},{6,4},{7,5},{8,10},{9,11},{10,... | collective-permute-start | bytes 98312 | tf_op jit(solution)/shard_map/ppermute | solution.py:454
  37.5 6.4 %copy-start.10 = (f32[3,1,512]{2,1,0:T(1,128)S(1)}, f32[3,1,512]{2,1,0:T(1,128)}, u32[]{:S(2)}) copy-start(f32[3,1,512]{2,1,0:T(1,128)} %param.22) | copy-start | bytes 18436
  37.5 6.4 %copy-start.9 = (f32[3,3,1,512]{3,2,1,0:T(1,128)S(1)}, f32[3,3,1,512]{3,2,1,0:T(1,128)}, u32[]{:S(2)}) copy-start(f32[3,3,1,512]{3,2,1,0:T(1,128)} %param.21) | copy-start | bytes 55300
  37.5 16.8 %all-to-all-start.1 = ((f32[64,4,128]{2,1,0:T(4,128)}), f32[64,4,128]{2,1,0:T(4,128)S(1)}, u32[]{:S(2)}, u32[]{:S(2)}) async-start(f32[64,4,128]{2,1,0:T(4,128)} %get-tuple-element.19), calls=%async_computation.1 | async-start | bytes 262144 | tf_op jit(solution)/shard_map/all_to_all | solution.py:461
  44.0 5.6 %collective-permute-start.5 = (f32[12,128]{1,0:T(8,128)S(1)}, f32[12,128]{1,0:T(8,128)S(1)}, u32[]{:S(2)}, u32[]{:S(2)}) collective-permute-start(f32[12,128]{1,0:T(8,128)S(1)} %get-tuple-element.30), channel_id=1, source_target_pairs={{4,0},{8,4},{12,8},{16,12},{20,16},{24,20},{28,24},{32,28},{36,32}... | collective-permute-start | bytes 18440 | tf_op jit(solution)/shard_map/ppermute | solution.py:443
  46.4 3.2 %copy-start.8 = (f32[3,1,512]{2,1,0:T(1,128)S(1)}, f32[3,1,512]{2,1,0:T(1,128)}, u32[]{:S(2)}) copy-start(f32[3,1,512]{2,1,0:T(1,128)} %param.20) | copy-start | bytes 18436
  46.4 4.0 %collective-permute-start.4 = (f32[12,128]{1,0:T(8,128)S(1)}, f32[12,128]{1,0:T(8,128)S(1)}, u32[]{:S(2)}, u32[]{:S(2)}) collective-permute-start(f32[12,128]{1,0:T(8,128)S(1)} %get-tuple-element.31), channel_id=1, source_target_pairs={{0,4},{4,8},{8,12},{12,16},{16,20},{20,24},{24,28},{28,32},{32,36}... | collective-permute-start | bytes 18440 | tf_op jit(solution)/shard_map/ppermute | solution.py:442
  49.6 4.6 %copy-start.7 = (s32[3]{0:T(128)S(1)}, s32[3]{0:T(128)}, u32[]{:S(2)}) copy-start(s32[3]{0:T(128)} %refs_0_.7) | copy-start | bytes 40
  75.2 5.0 %collective-permute-start.8 = (f32[72,128]{1,0:T(8,128)S(1)}, f32[72,128]{1,0:T(8,128)S(1)}, u32[]{:S(2)}, u32[]{:S(2)}) collective-permute-start(f32[72,128]{1,0:T(8,128)S(1)} %get-tuple-element.22.refs_2_), channel_id=1, source_target_pairs={{0,2},{1,3},{2,0},{3,1},{4,6},{5,7},{6,4},{7,5},{8,10},{9,11},{10,... | collective-permute-start | bytes 110600 | tf_op jit(solution)/shard_map/ppermute | solution.py:473
  78.2 3.1 %collective-permute-start.7 = (f32[72,128]{1,0:T(8,128)S(1)}, f32[72,128]{1,0:T(8,128)S(1)}, u32[]{:S(2)}, u32[]{:S(2)}) collective-permute-start(f32[72,128]{1,0:T(8,128)S(1)} %get-tuple-element.22.refs_2_), channel_id=1, source_target_pairs={{0,3},{1,0},{2,1},{3,2},{4,7},{5,4},{6,5},{7,6},{8,11},{9,8},{10,9... | collective-permute-start | bytes 110600 | tf_op jit(solution)/shard_map/ppermute | solution.py:472
  80.2 4.0 %collective-permute-start.6 = (f32[72,128]{1,0:T(8,128)S(1)}, f32[72,128]{1,0:T(8,128)S(1)}, u32[]{:S(2)}, u32[]{:S(2)}) collective-permute-start(f32[72,128]{1,0:T(8,128)S(1)} %get-tuple-element.22.refs_2_), channel_id=1, source_target_pairs={{0,1},{1,2},{2,3},{3,0},{4,5},{5,6},{6,7},{7,4},{8,9},{9,10},{10,1... | collective-permute-start | bytes 110600 | tf_op jit(solution)/shard_map/ppermute | solution.py:471

commit v2 on v1

v2 whole, which is shorter than its diff:
```python
import jax
import jax.numpy as jnp
from jax import lax
from jax.experimental import pallas as pl
from jax.experimental.pallas import tpu as pltpu
from jax.sharding import Mesh
from jax.sharding import PartitionSpec as P

F32 = jnp.float32
BF16 = jnp.bfloat16
I32 = jnp.int32
ROWS = 128
KNOTS = 16
CROSS = 128
SKY_N = 64
CHIPS = 32
TM_N = 4
SRC_N = 1024
RUN = 512
WIDE = RUN + 128
HEAD = 40
SKY = ("x", "z", "c")
SKY_TM = ("x", "z", "c", "tm")


def iota(shape, dim):
    return lax.broadcasted_iota(I32, shape, dim)


def dot(a, b):
    return jnp.dot(a.astype(BF16), b.astype(BF16), preferred_element_type=F32)


def dot_nt(a, b):
    return lax.dot_general(
        a.astype(BF16), b.astype(BF16), (((1,), (1,)), ((), ())), preferred_element_type=F32
    )


def halves(x):
    high = x.astype(BF16)
    return high, (x - high.astype(F32)).astype(BF16)


def thirds(x):
    high = x.astype(BF16).astype(F32)
    rest = x - high
    middle = rest.astype(BF16).astype(F32)
    return high, middle, rest - middle


def b_spline(moment_row, knot):
    tau = 1.5 + (KNOTS - 3) * (moment_row.astype(F32) + 0.5) / ROWS
    dist = jnp.abs(tau - knot.astype(F32))
    inner = 2.0 / 3.0 - dist * dist + 0.5 * dist * dist * dist
    rest = 2.0 - dist
    outer = rest * rest * rest / 6.0
    return jnp.where(dist < 1.0, inner, jnp.where(dist < 2.0, outer, 0.0))


def spline_by_lane():
    return b_spline(iota((128, 128), 1), iota((128, 128), 0) & 15)


def spline_by_row():
    return b_spline(iota((128, 128), 0), iota((128, 128), 1) & 15)


def fold_table():
    return jnp.where((iota((128, 128), 0) & 15) == (iota((128, 128), 1) & 15), 1.0, 0.0)


def attitude_term(att_ref, masked, table_ref):
    high, low = halves(jnp.concatenate(masked, 0))
    spread = dot(jnp.concatenate([high, low, high], 1), table_ref[...])
    total = jnp.zeros((CROSS, ROWS), F32)
    for a in range(3):
        total = total + att_ref[a].astype(F32) * spread[a * 128 : a * 128 + 128]
    return total


def send_normal(src_ref, resid, onehot, refs):
    lane = iota((128, 128), 1)
    square = jnp.zeros((128, 128), F32)
    for p in range(5):
        rhs = jnp.sum(src_ref[p].astype(F32) * resid, axis=1, keepdims=True)
        square = jnp.where(lane == p, rhs, square)
    rows = square.T[0:8]
    parts = dot(jnp.concatenate(thirds(rows), 0), onehot)
    normal = parts[0:8] + parts[8:16] + parts[16:24]
    for ref in refs:
        for j in range(8):
            ref[pl.ds(j, 5, stride=8), :] = normal[0:5, 128 * j : 128 * j + 128]


def gather_source(values8, onehot):
    parts = dot_nt(onehot, jnp.concatenate(thirds(values8), 0))
    return [
        parts[:, p : p + 1] + parts[:, 8 + p : 9 + p] + parts[:, 16 + p : 17 + p] for p in range(5)
    ]


def padded_rows(x):
    return jnp.concatenate([x, jnp.zeros((8 - x.shape[0], x.shape[1]), F32)], 0)


def column(cols_ref, i):
    return cols_ref[:, i : i + 1].astype(I32)


def stacked_spline(table):
    high, low = halves(table)
    return jnp.concatenate([high, high, low], 0)


def prepare_kernel(
    live_ref, core_ref, obs_ref, att_ref, src_ref, slot_ref, kb_ref, sources_ref,
    cols_ref, places_ref, by_source_ref, base_ref, by_lane_ref, by_row_ref, pack_ref, index_ref,
    peers_ref, choose_ref, up_ref, down_ref,
):
    live, core = live_ref[0], core_ref[0]
    kb, slot = kb_ref[...], slot_ref[...]
    h, lb = kb >> 5, kb & 31
    sub, lane = iota((128, 128), 0), iota((128, 128), 1)
    square = jnp.zeros((128, 128), F32)
    for i, row in enumerate((h, lb, slot)):
        square = jnp.where(sub == i, row.astype(F32), square)
    turned = square.T
    hc, lbc, slotc = (turned[:, i : i + 1].astype(I32) for i in range(3))
    same = hc == h
    c = jnp.sum(jnp.where(same & (sub < lane), 1.0, 0.0), axis=0, keepdims=True).astype(I32)
    cc = jnp.sum(jnp.where(same & (lane < sub), 1.0, 0.0), axis=1, keepdims=True)
    cols_ref[...] = jnp.where(lane == 3, cc, turned)
    cc = cc.astype(I32)
    group = lane >> 4

    place = (lbc >> 3) * CHIPS + (hc >> 1) + jnp.where((hc & 1) == core, 0, 128)
    places_ref[...] = jnp.where(iota((128, 256), 1) == place, 1.0, 0.0).astype(BF16)
    by_source = jnp.where(iota((128, SRC_N), 1) == slotc, 1.0, 0.0).astype(BF16)
    by_source_ref[...] = by_source
    values = gather_source(padded_rows(sources_ref[...]), by_source)
    src_term = jnp.zeros((CROSS, ROWS), F32)
    for p in range(5):
        src_term = src_term + src_ref[p].astype(F32) * values[p]
    base_ref[...] = obs_ref[...] - src_term
    by_lane_ref[...] = stacked_spline(spline_by_lane())
    by_row_ref[...] = stacked_spline(spline_by_row())

    peer = iota((SKY_N, 128), 0)
    to_row = jnp.where(lb <= 1, h - 1, jnp.where(lb >= 30, h + 1, jnp.full_like(h, -1)))
    own = jnp.where(peer == h, 1.0, 0.0)
    pack_ref[...] = jnp.concatenate([own, jnp.where(peer == to_row, 1.0, 0.0)], 1).astype(BF16)
    index_ref[...] = dot(own, jnp.where(group == cc + 2, (lbc + 1).astype(F32), 0.0))
    peers_ref[...] = jnp.where(iota((128, SKY_N), 1) == hc, 1.0, 0.0).astype(BF16)

    sub8 = iota((8, 128), 0)
    after = (h == SKY_N - 1) & (lb >= 30) & (sub8 < 4)
    before = (h == 0) & (lb <= 1) & (sub8 >= 4)
    chosen = (c == (sub8 & 3)) & (after | before) & (iota((8, 128), 1) < live)
    choose = jnp.where(chosen, 1.0, 0.0)
    choose_ref[...] = choose
    pieces = [att_ref[a] for a in range(3)] + [src_ref[p] for p in range(5)]
    ghosts = dot(choose, jnp.concatenate(pieces, 1))
    items = [ghosts[:, 128 * i : 128 * i + 128] for i in range(8)]
    ghost_slot = jnp.sum(choose * slot.astype(F32), axis=1, keepdims=True)
    ghost_block = jnp.sum(choose * lb.astype(F32), axis=1, keepdims=True)
    items.append(jnp.zeros((8, 128), F32))
    items.append(jnp.where(iota((8, 128), 1) < 64, ghost_slot, ghost_block))
    for q in range(5):
        even, odd = items[2 * q], items[2 * q + 1]
        up_ref[8 * q : 8 * q + 8, :] = jnp.concatenate([even[0:4], odd[0:4]], 0)
        down_ref[8 * q : 8 * q + 8, :] = jnp.concatenate([even[4:8], odd[4:8]], 0)


def widen_kernel(bands_ref, extra_ref, before_ref, after_ref, wide_ref):
    sub, lane = iota((8, RUN), 0), iota((8, 128), 1)

    def wide(i):
        core = jnp.zeros((8, RUN), F32)
        for a in range(3):
            rows = bands_ref[i, a] if i < 3 else extra_ref[a]
            core = jnp.where(sub == a, jnp.concatenate([rows[r : r + 1] for r in range(4)], 1), core)
        after = padded_rows(after_ref[3 * i : 3 * i + 3, :])
        before = padded_rows(before_ref[3 * i : 3 * i + 3, :])
        rim = jnp.where(lane < 32, after, jnp.where(lane >= 96, before, 0.0))
        return jnp.concatenate([core, rim], 1)

    bands = [wide(b) for b in range(3)]
    diag = wide(3) + 2.0 * (bands[0] + bands[1] + bands[2])
    for b in range(3):
        wide_ref[8 * b : 8 * b + 8, :] = bands[b]
    wide_ref[24:32, :] = 1.0 / jnp.where(diag > 0.0, diag, 1.0)


def first_kernel(
    live_ref, near_ref, far_ref, att_ref, src_ref, cols_ref, places_ref, by_source_ref, base_ref,
    by_lane_ref, choose_ref, up_in_ref, down_in_ref,
    resid_ref, plain_ref, up_ref, down_ref,
):
    tables = []
    for a in range(3):
        rows = [ref[:, a, r, :] for ref in (near_ref, far_ref) for r in range(4)]
        tables += halves(jnp.concatenate(rows, 0))
    found = dot(places_ref[...], jnp.concatenate(tables, 1))
    mine = (iota((128, 128), 1) >> 4) == (column(cols_ref, 1) & 7)
    masked = []
    for a in range(3):
        whole = found[:, 256 * a : 256 * a + 128] + found[:, 256 * a + 128 : 256 * a + 256]
        masked.append(jnp.where(mine, whole, 0.0))
    used = jnp.where(iota((CROSS, 1), 0) < live_ref[0], 1.0, 0.0)
    resid = (base_ref[...] - attitude_term(att_ref, masked, by_lane_ref)) * used
    resid_ref[...] = resid
    send_normal(src_ref, resid, by_source_ref[...], (plain_ref, up_ref, down_ref))
    ghosts = dot(choose_ref[...], jnp.concatenate(halves(resid), 1))
    ghosts = ghosts[:, 0:128] + ghosts[:, 128:256]
    up_ref[HEAD : HEAD + 40, :] = up_in_ref[...]
    down_ref[HEAD : HEAD + 40, :] = down_in_ref[...]
    up_ref[HEAD + 32 : HEAD + 36, :] = ghosts[0:4]
    down_ref[HEAD + 32 : HEAD + 36, :] = ghosts[4:8]


def middle_kernel(
    live_ref, got_ref, resid_in_ref, att_ref, src_ref, cols_ref, peers_ref, by_source_ref,
    by_lane_ref, choose_ref, resid_ref, send_ref,
):
    table = jnp.concatenate([*halves(got_ref[:, 0, :]), *halves(got_ref[:, 1, :])], 1)
    found = dot(peers_ref[...], table)
    front = found[:, 0:128] + found[:, 128:256]
    back = found[:, 256:384] + found[:, 384:512]
    group, cc = iota((128, 128), 1) >> 4, column(cols_ref, 3)
    masked = [
        jnp.where(group == cc, front, 0.0),
        jnp.where(group == cc + 4, front, 0.0),
        jnp.where(group == cc, back, 0.0),
    ]
    used = jnp.where(iota((CROSS, 1), 0) < live_ref[0], 1.0, 0.0)
    resid = resid_in_ref[...] - attitude_term(att_ref, masked, by_lane_ref) * used
    resid_ref[...] = resid
    send_normal(src_ref, resid, by_source_ref[...], (send_ref,))
    ghosts = dot(choose_ref[...], jnp.concatenate(halves(resid), 1))
    send_ref[HEAD : HEAD + 8, :] = ghosts[:, 0:128] + ghosts[:, 128:256]


def return_kernel(
    live_ref, tm_ref, own_ref, below_ref, above_ref, across_ref, up_ref, down_ref, inverses_ref,
    sources_in_ref, resid_in_ref, att_ref, src_ref, cols_ref, by_source_ref, by_row_ref, pack_ref,
    index_ref, out_ref, resid_ref, sources_ref, total_ref, *, second,
):
    tm = tm_ref[0]
    total_ref[...] = (
        own_ref[0:HEAD, :] + across_ref[0:HEAD, :] + below_ref[0:HEAD, :] + above_ref[0:HEAD, :]
    )
    normal = jnp.concatenate([total_ref[pl.ds(j, 5, stride=8), :] for j in range(8)], 1)
    sub8 = iota((8, SRC_N), 0)
    step = jnp.zeros((8, SRC_N), F32)
    for p in range(5):
        row = jnp.sum(inverses_ref[p] * normal, axis=0, keepdims=True)
        step = jnp.where(sub8 == p, row, step)
    sources_ref[...] = step[0:5] if second else sources_in_ref[...] + step[0:5]
    ghost8 = iota((8, 128), 0)
    there = jnp.where(ghost8 < 4, jnp.where(tm > 0, 1.0, 0.0), jnp.where(tm < TM_N - 1, 1.0, 0.0))

    def item(i):
        row = HEAD + 4 * i
        return jnp.concatenate([up_ref[row : row + 4, :], down_ref[row : row + 4, :]], 0)

    facts = item(9)
    ghost_slot = facts[:, 0:1].astype(I32)
    ghost_block = facts[:, 64:65].astype(I32)
    ghost_onehot = jnp.where(iota((8, SRC_N), 1) == ghost_slot, 1.0, 0.0)
    values = gather_source(step, by_source_ref[...])
    ghost_values = gather_source(step, ghost_onehot)
    change = jnp.zeros((CROSS, ROWS), F32)
    ghost_change = jnp.zeros((8, ROWS), F32)
    for p in range(5):
        change = change + src_ref[p].astype(F32) * values[p]
        ghost_change = ghost_change + item(3 + p) * ghost_values[p]
    used = jnp.where(iota((CROSS, 1), 0) < live_ref[0], 1.0, 0.0)
    resid = resid_in_ref[...] - used * change
    resid_ref[...] = resid
    if second:
        ghost_resid = jnp.concatenate(
            [below_ref[HEAD : HEAD + 4, :], above_ref[HEAD + 4 : HEAD + 8, :]], 0
        )
    else:
        ghost_resid = item(8)
    ghost_resid = (ghost_resid - ghost_change) * there
    rows = [att_ref[a].astype(F32) * resid for a in range(3)]
    rows += [item(a) * ghost_resid for a in range(3)]
    high, low = halves(jnp.concatenate(rows, 0))
    grads = dot(jnp.concatenate([high, low, high], 1), by_row_ref[...])
    lbc, cc = column(cols_ref, 1), column(cols_ref, 3)
    group = iota((128, 128), 1) >> 4
    edge_group = jnp.where(lbc <= 1, lbc, lbc - 24)
    own = group == cc + 2
    edge = group == edge_group
    top, bottom = [], []
    for a in range(3):
        g = grads[128 * a : 128 * a + 128]
        top += halves(jnp.where(own, g, 0.0))
        bottom += halves(jnp.where(edge, g, 0.0))
    table = jnp.concatenate([jnp.concatenate(top, 1), jnp.concatenate(bottom, 1)], 0)
    packed = dot(pack_ref[...], table)
    peer = iota((SKY_N, 128), 0)
    ghost_group = iota((8, 128), 1) >> 4
    ghost_own = ghost_group == jnp.where(ghost8[:, 0:1] < 4, ghost_block - 24, ghost_block)
    for a in range(3):
        ghost = jnp.where(ghost_own, grads[384 + 8 * a : 392 + 8 * a], 0.0)
        from_below = jnp.sum(jnp.where(ghost8 < 4, ghost, 0.0), axis=0, keepdims=True)
        from_above = jnp.sum(jnp.where(ghost8 >= 4, ghost, 0.0), axis=0, keepdims=True)
        block = packed[:, 256 * a : 256 * a + 128] + packed[:, 256 * a + 128 : 256 * a + 256]
        block = block + jnp.where(peer == 0, from_below, 0.0)
        block = block + jnp.where(peer == SKY_N - 1, from_above, 0.0)
        out_ref[:, a, :] = block
    out_ref[:, 3, :] = index_ref[...]


def smooth_kernel(
    offsets_ref, got_ref, pick_in_ref, knots_in_ref, wide_ref, sources_in_ref, step_ref, *outs, last
):
    knots_ref = outs[0]
    lane = iota((SKY_N, 128), 1)
    if last:
        pick = pick_in_ref[...]
    else:
        index = got_ref[:, 3, :]
        square = jnp.concatenate([index, jnp.zeros((128 - SKY_N, 128), F32)], 0).T
        block32 = (iota((32, SKY_N), 0) + 1).astype(F32)
        pick = jnp.concatenate(
            [
                jnp.where(square[16 * (2 + c) : 16 * (2 + c) + 1, 0:SKY_N] == block32, 1.0, 0.0)
                for c in range(4)
            ],
            0,
        ).astype(BF16)
        outs[2][...] = pick
    got = [got_ref[:, a, :] for a in range(3)]
    table = jnp.concatenate([part for g in got for part in halves(g)], 1)
    summed = dot(pick, table)
    row128 = iota((128, 128), 0)
    group128 = iota((128, 128), 1) >> 4
    keep = group128 == (row128 >> 5) + 2
    fold = fold_table()
    stack = []
    for a in range(3):
        one = summed[:, 256 * a : 256 * a + 128] + summed[:, 256 * a + 128 : 256 * a + 256]
        one = jnp.where(keep, one, 0.0)
        stack.append(one[0:32] + one[32:64] + one[64:96] + one[96:128])
    high, low = halves(jnp.concatenate(stack, 0))
    spread = dot(jnp.concatenate([high, low], 1), jnp.concatenate([fold, fold], 0))
    in_row = (iota((8, 128), 1) >> 4) == iota((8, 128), 0)
    sub_w = iota((8, WIDE), 0)
    grad = jnp.zeros((8, WIDE), F32)
    for a in range(3):
        tiles = []
        for r in range(4):
            piece = spread[32 * a + 8 * r : 32 * a + 8 * r + 8]
            tiles.append(jnp.sum(jnp.where(in_row, piece, 0.0), axis=0, keepdims=True))
        rim = jnp.where((lane < 32) | (lane >= 96), got[a], 0.0)
        tiles.append(jnp.sum(rim, axis=0, keepdims=True))
        grad = jnp.where(sub_w == a, jnp.concatenate(tiles, 1), grad)
    bands = [wide_ref[8 * b : 8 * b + 8, :] for b in range(3)]
    scale = wide_ref[24:32, :]
    delta = grad * scale
    for _ in range(2):
        total = jnp.zeros((8, WIDE), F32)
        for b in range(3):
            offset = offsets_ref[b]
            upper = pltpu.roll(delta, WIDE - offset, 1)
            lower = pltpu.roll(delta, offset, 1)
            total = total + bands[b] * (upper + lower)
        delta = (grad + total) * scale
    for a in range(3):
        for r in range(4):
            tile = delta[a : a + 1, 128 * r : 128 * r + 128]
            knots_ref[a, r : r + 1, :] = knots_in_ref[a, r : r + 1, :] + tile
    if last:
        outs[1][...] = sources_in_ref[...] + step_ref[...]
        return
    send_ref = outs[1]
    spreads = []
    for a in range(3):
        for r in range(4):
            tile = delta[a : a + 1, 128 * r : 128 * r + 128]
            spreads.append(jnp.where(in_row, tile, 0.0))
    high, low = halves(jnp.concatenate(spreads, 0))
    blocks = dot(jnp.concatenate([high, low], 1), jnp.concatenate([fold, fold], 0))
    tables = [part for a in range(3) for part in halves(blocks[32 * a : 32 * a + 32])]
    slots = [index[:, 16 * (2 + c) : 16 * (2 + c) + 1].astype(I32) - 1 for c in range(4)]
    slot = jnp.concatenate(slots, 0)
    by_block = jnp.where(iota((4 * SKY_N, 32), 1) == slot, 1.0, 0.0)
    found = dot(by_block, jnp.concatenate(tables, 1))
    group = lane >> 4
    front = jnp.zeros((SKY_N, 128), F32)
    back = jnp.zeros((SKY_N, 128), F32)
    for c in range(4):
        rows = found[SKY_N * c : SKY_N * (c + 1)]
        part = [
            rows[:, 256 * a : 256 * a + 128] + rows[:, 256 * a + 128 : 256 * a + 256]
            for a in range(3)
        ]
        front = jnp.where(group == c, part[0], jnp.where(group == c + 4, part[1], front))
        back = jnp.where(group == c, part[2], back)
    send_ref[:, 0, :] = front
    send_ref[:, 1, :] = back


def run_kernel(body, scalars, outs, *args, scratch=(), flops=10_000_000, **static):
    specs = [
        pl.BlockSpec(memory_space=pltpu.SMEM if i < scalars else pltpu.VMEM)
        for i in range(len(args))
    ]
    shapes = [o if isinstance(o, jax.ShapeDtypeStruct) else jax.ShapeDtypeStruct(o, F32) for o in outs]

    def kernel(*refs):
        body(*refs, **static)

    return pl.pallas_call(
        kernel,
        out_shape=shapes,
        in_specs=specs,
        out_specs=[pl.BlockSpec(memory_space=pltpu.VMEM) for _ in outs],
        scratch_shapes=[pltpu.VMEM(shape, F32) for shape in scratch],
        cost_estimate=pl.CostEstimate(flops=flops, bytes_accessed=2_000_000, transcendentals=0),
        compiler_params=pltpu.CompilerParams(vmem_limit_bytes=32 * 1024 * 1024),
    )(*args)


def half(*shape):
    return jax.ShapeDtypeStruct(shape, BF16)


def shifts(k):
    return [(i, (i + k) % TM_N) for i in range(TM_N)]


def per_device(
    observed,
    att_partials,
    src_partials,
    src_slot,
    knot_block,
    live_count,
    sources,
    inverses,
    attitude,
    band_coef,
    extra_diag,
    band_offsets,
):
    core = lax.axis_index("c").astype(I32).reshape(1)
    tm = lax.axis_index("tm").astype(I32).reshape(1)
    slot = src_slot.reshape(1, CROSS)
    kb = knot_block.reshape(1, CROSS)
    static = jnp.concatenate([band_coef.reshape(9, RUN), extra_diag.reshape(3, RUN)], 0)

    dense = jnp.broadcast_to(attitude.reshape(1, 3, 4, 128), (CHIPS, 3, 4, 128))
    near = lax.all_to_all(dense, ("x", "z"), 0, 0, tiled=True)
    chain = [s * TM_N + t for t in range(TM_N) for s in range(SKY_N)]
    pairs = list(zip(chain[:-1], chain[1:], strict=True))
    after = lax.ppermute(static[:, :128], SKY_TM, [(b, a) for a, b in pairs])
    (
        cols, places, by_source, base, by_lane, by_row, pack, index, peers, choose, up, down,
    ) = run_kernel(
        prepare_kernel, 2,
        [
            (128, 128), half(128, 256), half(128, SRC_N), (CROSS, ROWS), half(384, 128),
            half(384, 128), half(SKY_N, 256), (SKY_N, 128), half(128, SKY_N), (8, 128), (40, 128),
            (40, 128),
        ],
        live_count, core, observed, att_partials, src_partials, slot, kb, sources,
    )
    near, after, cols = lax.optimization_barrier((near, after, cols))
    far = lax.ppermute(near, "c", [(0, 1), (1, 0)])
    resid, plain, up, down = run_kernel(
        first_kernel, 1, [(CROSS, ROWS), (HEAD, 128), (HEAD + 40, 128), (HEAD + 40, 128)],
        live_count, near, far, att_partials, src_partials, cols, places, by_source, base, by_lane,
        choose, up, down,
    )
    across = lax.ppermute(plain, "tm", shifts(2))
    up = lax.ppermute(up, "tm", shifts(1))
    down = lax.ppermute(down, "tm", shifts(-1))
    back_shapes = [(SKY_N, 4, 128), (CROSS, ROWS), (5, SRC_N)]
    last_run, cols = lax.optimization_barrier((static[:, RUN - 128 :], cols))
    before = lax.ppermute(last_run, SKY_TM, pairs)
    (wide,) = run_kernel(
        widen_kernel, 0, [(32, WIDE)],
        band_coef.reshape(3, 3, 4, 128), extra_diag.reshape(3, 4, 128), before, after,
    )
    outgoing, resid, sources = run_kernel(
        return_kernel, 2, back_shapes,
        live_count, tm, plain, up, down, across, up, down, inverses, sources, resid,
        att_partials, src_partials, cols, by_source, by_row, pack, index,
        scratch=[(HEAD, 128)], second=False,
    )
    got = lax.all_to_all(outgoing, SKY, 0, 0, tiled=True)
    knots, served, pick = run_kernel(
        smooth_kernel, 1, [(3, 4, 128), (SKY_N, 2, 128), half(128, SKY_N)],
        band_offsets, got, pack, attitude.reshape(3, 4, 128), wide, choose, choose, last=False,
    )
    arrived = lax.all_to_all(served, SKY, 0, 0, tiled=True)
    resid, mine = run_kernel(
        middle_kernel, 1, [(CROSS, ROWS), (HEAD + 8, 128)],
        live_count, arrived, resid, att_partials, src_partials, cols, peers, by_source, by_lane,
        choose,
    )
    across = lax.ppermute(mine, "tm", shifts(2))
    below = lax.ppermute(mine, "tm", shifts(1))
    above = lax.ppermute(mine, "tm", shifts(-1))
    outgoing, resid, step = run_kernel(
        return_kernel, 2, back_shapes,
        live_count, tm, mine, below, above, across, up, down, inverses, sources, resid,
        att_partials, src_partials, cols, by_source, by_row, pack, index,
        scratch=[(HEAD, 128)], second=True,
    )
    got = lax.all_to_all(outgoing, SKY, 0, 0, tiled=True)
    knots, sources = run_kernel(
        smooth_kernel, 1, [(3, 4, 128), (5, SRC_N)],
        band_offsets, got, pick, knots, wide, sources, step, last=True,
    )
    return (sources, knots.reshape(3, 1, RUN))


def solution(mesh):
    torus = Mesh(mesh.devices.reshape(4, 8, 2, mesh.shape["tm"]), SKY_TM)
    return jax.shard_map(
        per_device,
        mesh=torus,
        in_specs=(
            P(SKY_TM, None),
            P(None, SKY_TM, None),
            P(None, SKY_TM, None),
            P(SKY_TM),
            P(SKY_TM),
            P(SKY_TM),
            P(None, SKY),
            P(None, None, SKY),
            P(None, "tm", SKY),
            P(None, None, "tm", SKY),
            P(None, "tm", SKY),
            P(),
        ),
        out_specs=(P(None, SKY), P(None, "tm", SKY)),
        check_vma=False,
    )
```

time: 104 us -> 99 us (0.952)
  blocking collectives: 55.2 us -> 32.3 us
  starting transfers between devices: 24.2 us -> 35.2 us
  waiting for transfers between devices: 11.7 us -> 18.5 us
    all_to_all x2 -> x1, blocking collectives: 37.1 us -> 15.9 us  [per_device(): got = lax.all_to_all(outgoing, SKY, 0, 0, tiled=True)]
    all_to_all x1 -> x2, starting transfers between devices: 6.38 us -> 18.3 us  [the longest x1 12 us: per_device(): near = lax.all_to_all(dense, ('x', 'z'), 0, 0, tiled=True)]
    all_to_all x1 -> x2, waiting for transfers between devices: 3.88 us -> 8.69 us  [the longest x1 6 us: per_device(): got = lax.all_to_all(outgoing, SKY, 0, 0, tiled=True)]
    ppermute x1, waiting for transfers between devices: 0.01 us -> 2.97 us  [per_device(): across = lax.ppermute(mine, 'tm', shifts(2))]
    ppermute x1, starting transfers between devices: 3.01 us -> 0.49 us  [per_device(): across = lax.ppermute(mine, 'tm', shifts(2))]
    ppermute x1, waiting for transfers between devices: 2.88 us -> 0.72 us  [per_device(): below = lax.ppermute(mine, 'tm', shifts(1))]
    ppermute x1, waiting for transfers between devices: 0.01 us -> 1.68 us  [per_device(): after = lax.ppermute(static[:, :128], SKY_TM, [(b, a) for a, b in pairs])]
    all_to_all x1, blocking collectives: 18.1 us -> 16.4 us  [per_device(): arrived = lax.all_to_all(served, SKY, 0, 0, tiled=True)]
  transfers between devices with their start and end apart: 10 -> 11, of which waited for: 6 -> 8; matrix products, arithmetic and copies ran while one was open for 0% -> 0% of each run, Pallas kernels for 0% -> 1%
where the time goes in v2:
time: 99 us; the launch traced here: 98.6 us
  starting transfers between devices  35.2 us (36%)
  blocking collectives  32.3 us (33%)
  waiting for transfers between devices  18.5 us (19%)
  Pallas kernels  8.94 us (9%)
  local copies, waits for them, and re-layouts  2.08 us (2%)
  between operations  1.46 us (1%)
    all_to_all x1, blocking collectives, per_device(): arrived = lax.all_to_all(served, SKY, 0, 0, tiled=True)  16.4 us
    all_to_all x1, blocking collectives, per_device(): got = lax.all_to_all(outgoing, SKY, 0, 0, tiled=True)  15.9 us
    all_to_all x1, starting transfers between devices, per_device(): near = lax.all_to_all(dense, ('x', 'z'), 0, 0, tiled=True)  12 us
    pallas_call x8, Pallas kernels, run_kernel(): pl.pallas_call(kernel, out_shape=shapes, in_specs=specs, out_specs=[pl.Bl...  8.94 us
    all_to_all x1, starting transfers between devices, per_device(): got = lax.all_to_all(outgoing, SKY, 0, 0, tiled=True)  6.28 us
    all_to_all x1, waiting for transfers between devices, per_device(): got = lax.all_to_all(outgoing, SKY, 0, 0, tiled=True)  6 us
    ppermute x1, starting transfers between devices, per_device(): before = lax.ppermute(last_run, SKY_TM, pairs)  3.54 us
    ppermute x1, waiting for transfers between devices, per_device(): across = lax.ppermute(mine, 'tm', shifts(2))  2.97 us
  transfers between devices with their start and end apart: 11, of which 8 were waited for; matrix products, arithmetic and copies ran while one was open for 0% of the time, Pallas kernels for 1%

profile of v2, /device:TPU:1, one launch (start us, length us, event | category | flops | bytes accessed | tf_op | source)
XLA Modules:
  0.0 98.6 jit_solution(2687323015419947335)
XLA Ops:
  0.6 1.4 %broadcast_in_dim.8 = f32[32,3,4,128]{3,2,1,0:T(4,128)} broadcast(f32[3,4,128]{2,1,0:T(4,128)} %bitcast.12), dimensions={1,2,3} | broadcast | bytes 202752 | tf_op jit(solution)/shard_map/broadcast_in_dim | solution.py:457
  2.0 0.0 copy-start.5
  2.1 12.0 %all-to-all-start = ((f32[32,3,4,128]{3,2,1,0:T(4,128)}), f32[32,3,4,128]{3,2,1,0:T(4,128)S(1)}, u32[]{:S(2)}, u32[]{:S(2)}) async-start(f32[32,3,4,128]{3,2,1,0:T(4,128)} %broadcast_in_dim.8), calls=%async_computation | async-start | bytes 393216 | tf_op jit(solution)/shard_map/all_to_all | solution.py:458
  14.1 0.0 copy-done.4
  14.1 0.0 copy-start
  14.1 0.1 reduce
  14.2 0.0 copy-done.7
  14.2 2.9 %collective-permute-start = (f32[12,128]{1,0:T(8,128)S(1)}, f32[12,128]{1,0:T(8,128)S(1)}, u32[]{:S(2)}, u32[]{:S(2)}) collective-permute-start(f32[12,128]{1,0:T(8,128)S(1)} %get-tuple-element.73), channel_id=1, source_target_pairs={{4,0},{8,4},{12,8},{16,12},{20,16},{24,20},{28,24},{32,28},{36,32}... | collective-permute-start | bytes 18440 | tf_op jit(solution)/shard_map/ppermute | solution.py:461
  17.7 0.0 copy-start.9
  17.7 0.0 copy-start.10
  17.8 0.0 copy-done.1
  17.8 0.0 copy-done.3
  17.8 0.0 copy-done.5
  17.8 0.0 copy-done
  17.8 0.6 copy-done.9
  18.4 0.0 copy-done.10
  18.4 0.7 shard_map.131
  19.1 1.7 %collective-permute-done.refs_3_ = f32[12,128]{1,0:T(8,128)S(1)} collective-permute-done((f32[12,128]{1,0:T(8,128)S(1)}, f32[12,128]{1,0:T(8,128)S(1)}, u32[]{:S(2)}, u32[]{:S(2)}) %collective-permute-start) | collective-permute-done | bytes 6176 | tf_op jit(solution)/shard_map/ppermute | solution.py:461
  20.8 2.7 %all-to-all-done.refs_1_ = f32[32,3,4,128]{3,2,1,0:T(4,128)S(1)} async-done(((f32[32,3,4,128]{3,2,1,0:T(4,128)}), f32[32,3,4,128]{3,2,1,0:T(4,128)S(1)}, u32[]{:S(2)}, u32[]{:S(2)}) %all-to-all-start) | async-done | bytes 196640 | tf_op jit(solution)/shard_map/all_to_all | solution.py:458
  23.5 2.8 %collective-permute-start.1 = (f32[32,3,4,128]{3,2,1,0:T(4,128)S(1)}, f32[32,3,4,128]{3,2,1,0:T(4,128)S(1)}, u32[]{:S(2)}, u32[]{:S(2)}) collective-permute-start(f32[32,3,4,128]{3,2,1,0:T(4,128)S(1)} %all-to-all-done.refs_1_), channel_id=1, source_target_pairs={{0,4},{4,0},{1,5},{5,1},{2,6},{6,2},{3,7},{7,3},{8,12},{12,8},{9,1... | collective-permute-start | bytes 589832 | tf_op jit(solution)/shard_map/ppermute | solution.py:474
  26.3 1.1 %collective-permute-done.1.refs_2_ = f32[32,3,4,128]{3,2,1,0:T(4,128)S(1)} collective-permute-done((f32[32,3,4,128]{3,2,1,0:T(4,128)S(1)}, f32[32,3,4,128]{3,2,1,0:T(4,128)S(1)}, u32[]{:S(2)}, u32[]{:S(2)}) %collective-permute-start.1) | collective-permute-done | bytes 196640 | tf_op jit(solution)/shard_map/ppermute | solution.py:474
  27.4 0.9 shard_map.132
  28.3 1.4 %collective-permute-start.2 = (f32[80,128]{1,0:T(8,128)S(1)}, f32[80,128]{1,0:T(8,128)S(1)}, u32[]{:S(2)}, u32[]{:S(2)}) collective-permute-start(f32[80,128]{1,0:T(8,128)S(1)} %get-tuple-element.46), channel_id=1, source_target_pairs={{0,1},{1,2},{2,3},{3,0},{4,5},{5,6},{6,7},{7,4},{8,9},{9,10},{10,1... | collective-permute-start | bytes 122888 | tf_op jit(solution)/shard_map/ppermute | solution.py:481
  29.6 1.5 %collective-permute-start.3 = (f32[80,128]{1,0:T(8,128)S(1)}, f32[80,128]{1,0:T(8,128)S(1)}, u32[]{:S(2)}, u32[]{:S(2)}) collective-permute-start(f32[80,128]{1,0:T(8,128)S(1)} %get-tuple-element.47), channel_id=1, source_target_pairs={{0,3},{1,0},{2,1},{3,2},{4,7},{5,4},{6,5},{7,6},{8,11},{9,8},{10,9... | collective-permute-start | bytes 122888 | tf_op jit(solution)/shard_map/ppermute | solution.py:482
  31.2 1.6 %collective-permute-start.4 = (f32[40,128]{1,0:T(8,128)S(1)}, f32[40,128]{1,0:T(8,128)S(1)}, u32[]{:S(2)}, u32[]{:S(2)}) collective-permute-start(f32[40,128]{1,0:T(8,128)S(1)} %get-tuple-element.45.refs_2_), channel_id=1, source_target_pairs={{0,2},{1,3},{2,0},{3,1},{4,6},{5,7},{6,4},{7,5},{8,10},{9,11},{10,... | collective-permute-start | bytes 61448 | tf_op jit(solution)/shard_map/ppermute | solution.py:480
  32.7 2.6 %collective-permute-done.4.refs_5_ = f32[40,128]{1,0:T(8,128)S(1)} collective-permute-done((f32[40,128]{1,0:T(8,128)S(1)}, f32[40,128]{1,0:T(8,128)S(1)}, u32[]{:S(2)}, u32[]{:S(2)}) %collective-permute-start.4) | collective-permute-done | bytes 20512 | tf_op jit(solution)/shard_map/ppermute | solution.py:480
  35.3 0.0 collective-permute-done.2.refs_3_.refs_6_
  35.3 0.0 collective-permute-done.3.refs_4_.refs_7_
  35.3 0.0 copy-done.2
  35.3 1.6 %shard_map.133 = (f32[64,4,128]{2,1,0:T(4,128)}, f32[128,128]{1,0:T(8,128)S(1)}, f32[5,1024]{1,0:T(8,128)S(1)}) custom-call(s32[1]{0:T(128)S(6)} %copy.20.refs_0_, s32[1]{0:T(128)} %bitcast.refs_1_, f32[40,128]{1,0:T(8,128)S(1)} %get-tuple-element.45.refs_2_, f32[80,128]{1,0:T(8,128)S(1)} %collective-permute-done.2.refs_3_.refs_6_, ...), custom_call_target="tpu_custom_call" | custom-call | flops 10000000 | bytes 2000000 | tf_op jit(solution)/shard_map/pallas_call | solution.py:418
  36.9 6.3 %all-to-all-start.1 = ((f32[64,4,128]{2,1,0:T(4,128)}), f32[64,4,128]{2,1,0:T(4,128)S(1)}, u32[]{:S(2)}, u32[]{:S(2)}) async-start(f32[64,4,128]{2,1,0:T(4,128)} %get-tuple-element.53), calls=%async_computation.1 | async-start | bytes 262144 | tf_op jit(solution)/shard_map/all_to_all | solution.py:496
  43.2 3.5 %collective-permute-start.5 = (f32[12,128]{1,0:T(8,128)S(1)}, f32[12,128]{1,0:T(8,128)S(1)}, u32[]{:S(2)}, u32[]{:S(2)}) collective-permute-start(f32[12,128]{1,0:T(8,128)S(1)} %get-tuple-element.54), channel_id=1, source_target_pairs={{0,4},{4,8},{8,12},{12,16},{16,20},{20,24},{24,28},{28,32},{32,36}... | collective-permute-start | bytes 18440 | tf_op jit(solution)/shard_map/ppermute | solution.py:485
  46.7 0.8 collective-permute-done.5.refs_2_
  47.5 6.0 %all-to-all-done.1.refs_1_ = f32[64,4,128]{2,1,0:T(4,128)S(1)} async-done(((f32[64,4,128]{2,1,0:T(4,128)}), f32[64,4,128]{2,1,0:T(4,128)S(1)}, u32[]{:S(2)}, u32[]{:S(2)}) %all-to-all-start.1) | async-done | bytes 131104 | tf_op jit(solution)/shard_map/all_to_all | solution.py:496
  53.5 0.0 copy-done.6
  53.5 0.0 copy-done.8
  53.6 1.8 %shard_map.135 = (f32[3,4,128]{2,1,0:T(4,128)S(1)}, f32[64,2,128]{2,1,0:T(2,128)S(1)}, bf16[128,64]{1,0:T(8,128)(2,1)S(1)}) custom-call(s32[3]{0:T(128)S(1)} %copy-done.8, f32[64,4,128]{2,1,0:T(4,128)S(1)} %all-to-all-done.1.refs_1_, bf16[64,256]{1,0:T(8,128)(2,1)S(1)} %get-tuple-element.51.refs_16_.refs_2_, f32[3,4,128]{2,1,0:T(4,128)S(1)} %bitcast.13, ...), custom_call_target="tpu_custom_call" | custom-call | flops 10000000 | bytes 2000000 | tf_op jit(solution)/shard_map/pallas_call | solution.py:418
  55.4 16.4 %all_to_all.20.refs_1_ = f32[64,2,128]{2,1,0:T(2,128)S(1)} all-to-all(f32[64,2,128]{2,1,0:T(2,128)S(1)} %get-tuple-element.56), channel_id=1, replica_groups=mesh['x'=4,'z'=8,'c'=2,'tm'=4] {'x','z','c'}, dimensions={0} | all-to-all | bytes 131072 | tf_op jit(solution)/shard_map/all_to_all | solution.py:501
  71.8 0.9 shard_map.136
  72.6 0.2 collective-permute-start.6
  72.8 2.6 %collective-permute-start.7 = (f32[48,128]{1,0:T(8,128)S(1)}, f32[48,128]{1,0:T(8,128)S(1)}, u32[]{:S(2)}, u32[]{:S(2)}) collective-permute-start(f32[48,128]{1,0:T(8,128)S(1)} %get-tuple-element.59.refs_2_), channel_id=1, source_target_pairs={{0,3},{1,0},{2,1},{3,2},{4,7},{5,4},{6,5},{7,6},{8,11},{9,8},{10,9... | collective-permute-start | bytes 73736 | tf_op jit(solution)/shard_map/ppermute | solution.py:509
  75.4 0.5 collective-permute-start.8
  75.9 0.7 collective-permute-done.6.refs_3_
  76.6 0.0 collective-permute-done.7.refs_4_
  76.6 3.0 %collective-permute-done.8.refs_5_ = f32[48,128]{1,0:T(8,128)S(1)} collective-permute-done((f32[48,128]{1,0:T(8,128)S(1)}, f32[48,128]{1,0:T(8,128)S(1)}, u32[]{:S(2)}, u32[]{:S(2)}) %collective-permute-start.8) | collective-permute-done | bytes 24608 | tf_op jit(solution)/shard_map/ppermute | solution.py:507
  79.6 1.2 %shard_map.137 = (f32[64,4,128]{2,1,0:T(4,128)S(1)}, f32[128,128]{1,0:T(8,128)}, f32[5,1024]{1,0:T(8,128)S(1)}) custom-call(s32[1]{0:T(128)S(6)} %copy.20.refs_0_, s32[1]{0:T(128)} %bitcast.refs_1_, f32[48,128]{1,0:T(8,128)S(1)} %get-tuple-element.59.refs_2_, f32[48,128]{1,0:T(8,128)S(1)} %collective-permute-done.6.refs_3_, ...), custom_call_target="tpu_custom_call" | custom-call | flops 10000000 | bytes 2000000 | tf_op jit(solution)/shard_map/pallas_call | solution.py:418
  80.7 15.9 %all_to_all.21.refs_1_ = f32[64,4,128]{2,1,0:T(4,128)S(1)} all-to-all(f32[64,4,128]{2,1,0:T(4,128)S(1)} %get-tuple-element.62), channel_id=1, replica_groups=mesh['x'=4,'z'=8,'c'=2,'tm'=4] {'x','z','c'}, dimensions={0} | all-to-all | bytes 262144 | tf_op jit(solution)/shard_map/all_to_all | solution.py:516
  96.6 1.9 %shard_map.138 = (f32[3,4,128]{2,1,0:T(4,128)}, f32[5,1024]{1,0:T(8,128)}) custom-call(s32[3]{0:T(128)S(1)} %copy-done.8, f32[64,4,128]{2,1,0:T(4,128)S(1)} %all_to_all.21.refs_1_, bf16[128,64]{1,0:T(8,128)(2,1)S(1)} %get-tuple-element.63.refs_2_, f32[3,4,128]{2,1,0:T(4,128)S(1)} %get-tuple-element.64.refs_3_, f32[32,640]{1,0:T(8,128)S(1)} %shard_map.134.refs_4_, ...), custom_call_target="tpu_custom_call" | custom-call | flops 10000000 | bytes 2000000 | tf_op jit(solution)/shard_map/pallas_call | solution.py:418
  (11 shorter events, 0.1 us)
Async XLA Ops:
  2.0 12.0 %copy-start.4 = (f32[3,3,1,512]{3,2,1,0:T(1,128)S(1)}, f32[3,3,1,512]{3,2,1,0:T(1,128)}, u32[]{:S(2)}) copy-start(f32[3,3,1,512]{3,2,1,0:T(1,128)} %param.21) | copy-start | bytes 55300
  2.0 12.1 %copy-start.7 = (f32[3,1,512]{2,1,0:T(1,128)S(1)}, f32[3,1,512]{2,1,0:T(1,128)}, u32[]{:S(2)}) copy-start(f32[3,1,512]{2,1,0:T(1,128)} %param.22) | copy-start | bytes 18436
  2.0 15.7 %copy-start.1 = (bf16[3,128,128]{2,1,0:T(8,128)(2,1)S(1)}, bf16[3,128,128]{2,1,0:T(8,128)(2,1)}, u32[]{:S(2)}) copy-start(bf16[3,128,128]{2,1,0:T(8,128)(2,1)} %refs_11_.3) | copy-start | bytes 294916
  2.0 15.7 %copy-start.3 = (f32[5,1024]{1,0:T(8,128)S(1)}, f32[5,1024]{1,0:T(8,128)}, u32[]{:S(2)}) copy-start(f32[5,1024]{1,0:T(8,128)} %refs_9_.1) | copy-start | bytes 61444
  2.0 15.7 %copy-start.5 = (f32[128,128]{1,0:T(8,128)S(1)}, f32[128,128]{1,0:T(8,128)}, u32[]{:S(2)}) copy-start(f32[128,128]{1,0:T(8,128)} %refs_2_.1) | copy-start | bytes 196612
  2.1 21.4 %all-to-all-start = ((f32[32,3,4,128]{3,2,1,0:T(4,128)}), f32[32,3,4,128]{3,2,1,0:T(4,128)S(1)}, u32[]{:S(2)}, u32[]{:S(2)}) async-start(f32[32,3,4,128]{3,2,1,0:T(4,128)} %broadcast_in_dim.8), calls=%async_computation | async-start | bytes 393216 | tf_op jit(solution)/shard_map/all_to_all | solution.py:458
  14.1 3.7 %copy-start = (bf16[5,128,128]{2,1,0:T(8,128)(2,1)S(1)}, bf16[5,128,128]{2,1,0:T(8,128)(2,1)}, u32[]{:S(2)}) copy-start(bf16[5,128,128]{2,1,0:T(8,128)(2,1)} %refs_12_.3) | copy-start | bytes 491524
  14.2 6.6 %collective-permute-start = (f32[12,128]{1,0:T(8,128)S(1)}, f32[12,128]{1,0:T(8,128)S(1)}, u32[]{:S(2)}, u32[]{:S(2)}) collective-permute-start(f32[12,128]{1,0:T(8,128)S(1)} %get-tuple-element.73), channel_id=1, source_target_pairs={{4,0},{8,4},{12,8},{16,12},{20,16},{24,20},{28,24},{32,28},{36,32}... | collective-permute-start | bytes 18440 | tf_op jit(solution)/shard_map/ppermute | solution.py:461
  17.7 0.7 copy-start.9
  17.7 0.7 copy-start.10
  23.5 3.9 %collective-permute-start.1 = (f32[32,3,4,128]{3,2,1,0:T(4,128)S(1)}, f32[32,3,4,128]{3,2,1,0:T(4,128)S(1)}, u32[]{:S(2)}, u32[]{:S(2)}) collective-permute-start(f32[32,3,4,128]{3,2,1,0:T(4,128)S(1)} %all-to-all-done.refs_1_), channel_id=1, source_target_pairs={{0,4},{4,0},{1,5},{5,1},{2,6},{6,2},{3,7},{7,3},{8,12},{12,8},{9,1... | collective-permute-start | bytes 589832 | tf_op jit(solution)/shard_map/ppermute | solution.py:474
  27.4 7.9 %copy-start.2 = (f32[5,5,1024]{2,1,0:T(8,128)S(1)}, f32[5,5,1024]{2,1,0:T(8,128)}, u32[]{:S(2)}) copy-start(f32[5,5,1024]{2,1,0:T(8,128)} %refs_8_.3) | copy-start | bytes 307204
  28.3 7.0 %collective-permute-start.2 = (f32[80,128]{1,0:T(8,128)S(1)}, f32[80,128]{1,0:T(8,128)S(1)}, u32[]{:S(2)}, u32[]{:S(2)}) collective-permute-start(f32[80,128]{1,0:T(8,128)S(1)} %get-tuple-element.46), channel_id=1, source_target_pairs={{0,1},{1,2},{2,3},{3,0},{4,5},{5,6},{6,7},{7,4},{8,9},{9,10},{10,1... | collective-permute-start | bytes 122888 | tf_op jit(solution)/shard_map/ppermute | solution.py:481
  29.6 5.7 %collective-permute-start.3 = (f32[80,128]{1,0:T(8,128)S(1)}, f32[80,128]{1,0:T(8,128)S(1)}, u32[]{:S(2)}, u32[]{:S(2)}) collective-permute-start(f32[80,128]{1,0:T(8,128)S(1)} %get-tuple-element.47), channel_id=1, source_target_pairs={{0,3},{1,0},{2,1},{3,2},{4,7},{5,4},{6,5},{7,6},{8,11},{9,8},{10,9... | collective-permute-start | bytes 122888 | tf_op jit(solution)/shard_map/ppermute | solution.py:482
  31.2 4.1 %collective-permute-start.4 = (f32[40,128]{1,0:T(8,128)S(1)}, f32[40,128]{1,0:T(8,128)S(1)}, u32[]{:S(2)}, u32[]{:S(2)}) collective-permute-start(f32[40,128]{1,0:T(8,128)S(1)} %get-tuple-element.45.refs_2_), channel_id=1, source_target_pairs={{0,2},{1,3},{2,0},{3,1},{4,6},{5,7},{6,4},{7,5},{8,10},{9,11},{10,... | collective-permute-start | bytes 61448 | tf_op jit(solution)/shard_map/ppermute | solution.py:480
  36.9 16.7 %all-to-all-start.1 = ((f32[64,4,128]{2,1,0:T(4,128)}), f32[64,4,128]{2,1,0:T(4,128)S(1)}, u32[]{:S(2)}, u32[]{:S(2)}) async-start(f32[64,4,128]{2,1,0:T(4,128)} %get-tuple-element.53), calls=%async_computation.1 | async-start | bytes 262144 | tf_op jit(solution)/shard_map/all_to_all | solution.py:496
  43.2 4.3 %collective-permute-start.5 = (f32[12,128]{1,0:T(8,128)S(1)}, f32[12,128]{1,0:T(8,128)S(1)}, u32[]{:S(2)}, u32[]{:S(2)}) collective-permute-start(f32[12,128]{1,0:T(8,128)S(1)} %get-tuple-element.54), channel_id=1, source_target_pairs={{0,4},{4,8},{8,12},{12,16},{16,20},{20,24},{24,28},{28,32},{32,36}... | collective-permute-start | bytes 18440 | tf_op jit(solution)/shard_map/ppermute | solution.py:485
  47.5 6.0 %copy-start.6 = (f32[3,1,512]{2,1,0:T(1,128)S(1)}, f32[3,1,512]{2,1,0:T(1,128)}, u32[]{:S(2)}) copy-start(f32[3,1,512]{2,1,0:T(1,128)} %param.20) | copy-start | bytes 18436
  47.5 6.0 %copy-start.8 = (s32[3]{0:T(128)S(1)}, s32[3]{0:T(128)}, u32[]{:S(2)}) copy-start(s32[3]{0:T(128)} %refs_0_.8) | copy-start | bytes 40
  72.6 4.0 %collective-permute-start.6 = (f32[48,128]{1,0:T(8,128)S(1)}, f32[48,128]{1,0:T(8,128)S(1)}, u32[]{:S(2)}, u32[]{:S(2)}) collective-permute-start(f32[48,128]{1,0:T(8,128)S(1)} %get-tuple-element.59.refs_2_), channel_id=1, source_target_pairs={{0,1},{1,2},{2,3},{3,0},{4,5},{5,6},{6,7},{7,4},{8,9},{9,10},{10,1... | collective-permute-start | bytes 73736 | tf_op jit(solution)/shard_map/ppermute | solution.py:508
  72.8 3.8 %collective-permute-start.7 = (f32[48,128]{1,0:T(8,128)S(1)}, f32[48,128]{1,0:T(8,128)S(1)}, u32[]{:S(2)}, u32[]{:S(2)}) collective-permute-start(f32[48,128]{1,0:T(8,128)S(1)} %get-tuple-element.59.refs_2_), channel_id=1, source_target_pairs={{0,3},{1,0},{2,1},{3,2},{4,7},{5,4},{6,5},{7,6},{8,11},{9,8},{10,9... | collective-permute-start | bytes 73736 | tf_op jit(solution)/shard_map/ppermute | solution.py:509
  75.4 4.2 %collective-permute-start.8 = (f32[48,128]{1,0:T(8,128)S(1)}, f32[48,128]{1,0:T(8,128)S(1)}, u32[]{:S(2)}, u32[]{:S(2)}) collective-permute-start(f32[48,128]{1,0:T(8,128)S(1)} %get-tuple-element.59.refs_2_), channel_id=1, source_target_pairs={{0,2},{1,3},{2,0},{3,1},{4,6},{5,7},{6,4},{7,5},{8,10},{9,11},{10,... | collective-permute-start | bytes 73736 | tf_op jit(solution)/shard_map/ppermute | solution.py:507

commit v3 on v2

--- a/solution.py
+++ b/solution.py
@@ -114,11 +114,14 @@
 
 
 def prepare_kernel(
-    live_ref, core_ref, obs_ref, att_ref, src_ref, slot_ref, kb_ref, sources_ref,
+    live_ref, core_ref, offsets_in_ref, obs_ref, att_ref, src_ref, slot_ref, kb_ref, sources_ref,
+    bands_ref, extra_ref,
     cols_ref, places_ref, by_source_ref, base_ref, by_lane_ref, by_row_ref, pack_ref, index_ref,
-    peers_ref, choose_ref, up_ref, down_ref,
+    peers_ref, choose_ref, up_ref, down_ref, wide_ref, offsets_ref,
 ):
     live, core = live_ref[0], core_ref[0]
+    for b in range(3):
+        offsets_ref[b] = offsets_in_ref[b]
     kb, slot = kb_ref[...], slot_ref[...]
     h, lb = kb >> 5, kb & 31
     sub, lane = iota((128, 128), 0), iota((128, 128), 1)
@@ -171,31 +174,81 @@
         up_ref[8 * q : 8 * q + 8, :] = jnp.concatenate([even[0:4], odd[0:4]], 0)
         down_ref[8 * q : 8 * q + 8, :] = jnp.concatenate([even[4:8], odd[4:8]], 0)
 
-
-def widen_kernel(bands_ref, extra_ref, before_ref, after_ref, wide_ref):
-    sub, lane = iota((8, RUN), 0), iota((8, 128), 1)
-
-    def wide(i):
-        core = jnp.zeros((8, RUN), F32)
-        for a in range(3):
-            rows = bands_ref[i, a] if i < 3 else extra_ref[a]
-            core = jnp.where(sub == a, jnp.concatenate([rows[r : r + 1] for r in range(4)], 1), core)
-        after = padded_rows(after_ref[3 * i : 3 * i + 3, :])
-        before = padded_rows(before_ref[3 * i : 3 * i + 3, :])
-        rim = jnp.where(lane < 32, after, jnp.where(lane >= 96, before, 0.0))
-        return jnp.concatenate([core, rim], 1)
-
-    bands = [wide(b) for b in range(3)]
-    diag = wide(3) + 2.0 * (bands[0] + bands[1] + bands[2])
+    bands = [axis_rows(bands_ref[b]) for b in range(3)]
+    diag = axis_rows(extra_ref) + 2.0 * (bands[0] + bands[1] + bands[2])
     for b in range(3):
         wide_ref[8 * b : 8 * b + 8, :] = bands[b]
     wide_ref[24:32, :] = 1.0 / jnp.where(diag > 0.0, diag, 1.0)
 
 
+def axis_rows(tiles):
+    sub = iota((8, RUN), 0)
+    out = jnp.zeros((8, RUN), F32)
+    for a in range(3):
+        out = jnp.where(sub == a, jnp.concatenate([tiles[a][r : r + 1] for r in range(4)], 1), out)
+    return out
+
+
+def payload_kernel(knots_hbm, bands_hbm, extra_hbm, out_ref, knots_ref, bands_ref, extra_ref, sems):
+    copies = [
+        pltpu.make_async_copy(source, target, sems.at[i])
+        for i, (source, target) in enumerate(
+            ((bands_hbm, bands_ref), (extra_hbm, extra_ref), (knots_hbm, knots_ref))
+        )
+    ]
+    for copy in copies:
+        copy.start()
+    for copy in copies:
+        copy.wait()
+    lane = iota((1, 128), 1)
+
+    def ends(tiles, width):
+        low, high = tiles[0:1], tiles[3:4]
+        return jnp.where(lane < width, low, jnp.where(lane >= 128 - width, high, 0.0))
+
+    rows = []
+    for a in range(3):
+        bands = [bands_ref[b, a] for b in range(3)]
+        diag = extra_ref[a] + 2.0 * (bands[0] + bands[1] + bands[2])
+        row = ends(diag, 32) + pltpu.roll(ends(bands[0], 16), 48, 1)
+        rows.append(row + pltpu.roll(ends(bands[1], 16), 80, 1))
+    third = [ends(bands_ref[2, a], 16) for a in range(3)]
+    rows.append(third[0] + pltpu.roll(third[1], 48, 1) + pltpu.roll(third[2], 80, 1))
+    sub = iota((4, 128), 0)
+    edge = jnp.zeros((4, 128), F32)
+    for i, row in enumerate(rows):
+        edge = jnp.where(sub == i, row, edge)
+    for chip in range(CHIPS):
+        out_ref[chip, 0:3] = knots_ref[...]
+        out_ref[chip, 3] = edge
+
+
+def rim_tiles(before, after):
+    sub, lane = iota((8, 128), 0), iota((8, 128), 1)
+
+    def tile(sources, width):
+        out = jnp.zeros((8, 128), F32)
+        for a, (row, turn) in enumerate(sources):
+            both = [e[row : row + 1] for e in (after, before)]
+            if turn:
+                both = [pltpu.roll(e, 128 - turn, 1) for e in both]
+            one = jnp.where(lane < width, both[0], jnp.where(lane >= 128 - width, both[1], 0.0))
+            out = jnp.where(sub == a, one, out)
+        return out
+
+    bands = [
+        tile([(a, 48) for a in range(3)], 16),
+        tile([(a, 80) for a in range(3)], 16),
+        tile([(3, 0), (3, 48), (3, 80)], 16),
+    ]
+    diag = tile([(a, 0) for a in range(3)], 32)
+    return bands + [1.0 / jnp.where(diag > 0.0, diag, 1.0)]
+
+
 def first_kernel(
-    live_ref, near_ref, far_ref, att_ref, src_ref, cols_ref, places_ref, by_source_ref, base_ref,
-    by_lane_ref, choose_ref, up_in_ref, down_in_ref,
-    resid_ref, plain_ref, up_ref, down_ref,
+    live_ref, core_ref, chip_ref, near_ref, far_ref, att_ref, src_ref, cols_ref, places_ref,
+    by_source_ref, base_ref, by_lane_ref, choose_ref, up_in_ref, down_in_ref,
+    resid_ref, plain_ref, up_ref, down_ref, sides_ref,
 ):
     tables = []
     for a in range(3):
@@ -217,6 +270,16 @@
     down_ref[HEAD : HEAD + 40, :] = down_in_ref[...]
     up_ref[HEAD + 32 : HEAD + 36, :] = ghosts[0:4]
     down_ref[HEAD + 32 : HEAD + 36, :] = ghosts[4:8]
+    core, chip = core_ref[0], chip_ref[0]
+    before = jnp.where(core == 0, jnp.maximum(chip - 1, 0), chip)
+    after = jnp.where(core == 0, chip, jnp.minimum(chip + 1, CHIPS - 1))
+    sides_ref[0:4, :] = far_ref[before, 3]
+    sides_ref[4:8, :] = far_ref[after, 3]
+    empty = jnp.zeros((4, 128), F32)
+    final = jnp.where(core == 1, near_ref[CHIPS - 1, 3], far_ref[CHIPS - 1, 3])
+    initial = jnp.where(core == 0, near_ref[0, 3], far_ref[0, 3])
+    up_ref[HEAD + 40 : HEAD + 48, :] = jnp.concatenate([final, empty], 0)
+    down_ref[HEAD + 40 : HEAD + 48, :] = jnp.concatenate([initial, empty], 0)
 
 
 def middle_kernel(
@@ -242,7 +305,7 @@
 
 
 def return_kernel(
-    live_ref, tm_ref, own_ref, below_ref, above_ref, across_ref, up_ref, down_ref, inverses_ref,
+    live_ref, tm_ref, across_ref, own_ref, below_ref, above_ref, up_ref, down_ref, inverses_ref,
     sources_in_ref, resid_in_ref, att_ref, src_ref, cols_ref, by_source_ref, by_row_ref, pack_ref,
     index_ref, out_ref, resid_ref, sources_ref, total_ref, *, second,
 ):
@@ -316,13 +379,25 @@
 
 
 def smooth_kernel(
-    offsets_ref, got_ref, pick_in_ref, knots_in_ref, wide_ref, sources_in_ref, step_ref, *outs, last
+    offsets_ref, chip_ref, core_ref, tm_ref, got_ref, knots_in_ref, wide_ref, one_ref, two_ref,
+    three_ref, four_ref, *outs, last,
 ):
     knots_ref = outs[0]
     lane = iota((SKY_N, 128), 1)
     if last:
-        pick = pick_in_ref[...]
+        sources_in_ref, step_ref, pick_ref, rims_ref = one_ref, two_ref, three_ref, four_ref
+        pick = pick_ref[...]
+        rims = [rims_ref[8 * i : 8 * i + 8, :] for i in range(4)]
     else:
+        sides_ref, up_ref, down_ref = one_ref, two_ref, three_ref
+        place, tm = chip_ref[0] * 2 + core_ref[0], tm_ref[0]
+        below = jnp.where(tm > 0, up_ref[HEAD + 40 : HEAD + 44, :], 0.0)
+        above = jnp.where(tm < TM_N - 1, down_ref[HEAD + 40 : HEAD + 44, :], 0.0)
+        before = jnp.where(place == 0, below, sides_ref[0:4, :])
+        after = jnp.where(place == SKY_N - 1, above, sides_ref[4:8, :])
+        rims = rim_tiles(before, after)
+        for i in range(4):
+            outs[3][8 * i : 8 * i + 8, :] = rims[i]
         index = got_ref[:, 3, :]
         square = jnp.concatenate([index, jnp.zeros((128 - SKY_N, 128), F32)], 0).T
         block32 = (iota((32, SKY_N), 0) + 1).astype(F32)
@@ -359,8 +434,9 @@
         rim = jnp.where((lane < 32) | (lane >= 96), got[a], 0.0)
         tiles.append(jnp.sum(rim, axis=0, keepdims=True))
         grad = jnp.where(sub_w == a, jnp.concatenate(tiles, 1), grad)
-    bands = [wide_ref[8 * b : 8 * b + 8, :] for b in range(3)]
-    scale = wide_ref[24:32, :]
+    *bands, scale = (
+        jnp.concatenate([wide_ref[8 * i : 8 * i + 8, :], rims[i]], 1) for i in range(4)
+    )
     delta = grad * scale
     for _ in range(2):
         total = jnp.zeros((8, WIDE), F32)
@@ -419,7 +495,9 @@
         kernel,
         out_shape=shapes,
         in_specs=specs,
-        out_specs=[pl.BlockSpec(memory_space=pltpu.VMEM) for _ in outs],
+        out_specs=[
+            pl.BlockSpec(memory_space=pltpu.SMEM if s.dtype == I32 else pltpu.VMEM) for s in shapes
+        ],
         scratch_shapes=[pltpu.VMEM(shape, F32) for shape in scratch],
         cost_estimate=pl.CostEstimate(flops=flops, bytes_accessed=2_000_000, transcendentals=0),
         compiler_params=pltpu.CompilerParams(vmem_limit_bytes=32 * 1024 * 1024),
@@ -452,51 +530,59 @@
     tm = lax.axis_index("tm").astype(I32).reshape(1)
     slot = src_slot.reshape(1, CROSS)
     kb = knot_block.reshape(1, CROSS)
-    static = jnp.concatenate([band_coef.reshape(9, RUN), extra_diag.reshape(3, RUN)], 0)
-
-    dense = jnp.broadcast_to(attitude.reshape(1, 3, 4, 128), (CHIPS, 3, 4, 128))
+    chip = lax.axis_index(("x", "z")).astype(I32).reshape(1)
+    knots = attitude.reshape(3, 4, 128)
+    bands = band_coef.reshape(3, 3, 4, 128)
+    extra = extra_diag.reshape(3, 4, 128)
+
+    dense = pl.pallas_call(
+        payload_kernel,
+        out_shape=jax.ShapeDtypeStruct((CHIPS, 4, 4, 128), F32),
+        in_specs=[pl.BlockSpec(memory_space=pl.ANY)] * 3,
+        out_specs=pl.BlockSpec(memory_space=pltpu.VMEM),
+        scratch_shapes=[
+            pltpu.VMEM((3, 4, 128), F32),
+            pltpu.VMEM((3, 3, 4, 128), F32),
+            pltpu.VMEM((3, 4, 128), F32),
+            pltpu.SemaphoreType.DMA((3,)),
+        ],
+        compiler_params=pltpu.CompilerParams(vmem_limit_bytes=56 * 1024 * 1024),
+    )(knots, bands, extra)
     near = lax.all_to_all(dense, ("x", "z"), 0, 0, tiled=True)
-    chain = [s * TM_N + t for t in range(TM_N) for s in range(SKY_N)]
-    pairs = list(zip(chain[:-1], chain[1:], strict=True))
-    after = lax.ppermute(static[:, :128], SKY_TM, [(b, a) for a, b in pairs])
     (
-        cols, places, by_source, base, by_lane, by_row, pack, index, peers, choose, up, down,
+        cols, places, by_source, base, by_lane, by_row, pack, index, peers, choose, up, down, wide,
+        offsets,
     ) = run_kernel(
-        prepare_kernel, 2,
+        prepare_kernel, 3,
         [
             (128, 128), half(128, 256), half(128, SRC_N), (CROSS, ROWS), half(384, 128),
             half(384, 128), half(SKY_N, 256), (SKY_N, 128), half(128, SKY_N), (8, 128), (40, 128),
-            (40, 128),
+            (40, 128), (32, RUN), jax.ShapeDtypeStruct((3,), I32),
         ],
-        live_count, core, observed, att_partials, src_partials, slot, kb, sources,
-    )
-    near, after, cols = lax.optimization_barrier((near, after, cols))
+        live_count, core, band_offsets, observed, att_partials, src_partials, slot, kb, sources, bands, extra,
+    )
+    near, cols = lax.optimization_barrier((near, cols))
     far = lax.ppermute(near, "c", [(0, 1), (1, 0)])
-    resid, plain, up, down = run_kernel(
-        first_kernel, 1, [(CROSS, ROWS), (HEAD, 128), (HEAD + 40, 128), (HEAD + 40, 128)],
-        live_count, near, far, att_partials, src_partials, cols, places, by_source, base, by_lane,
-        choose, up, down,
+    resid, plain, up, down, sides = run_kernel(
+        first_kernel, 3,
+        [(CROSS, ROWS), (HEAD, 128), (HEAD + 48, 128), (HEAD + 48, 128), (8, 128)],
+        live_count, core, chip, near, far, att_partials, src_partials, cols, places, by_source,
+        base, by_lane, choose, up, down,
     )
     across = lax.ppermute(plain, "tm", shifts(2))
     up = lax.ppermute(up, "tm", shifts(1))
     down = lax.ppermute(down, "tm", shifts(-1))
     back_shapes = [(SKY_N, 4, 128), (CROSS, ROWS), (5, SRC_N)]
-    last_run, cols = lax.optimization_barrier((static[:, RUN - 128 :], cols))
-    before = lax.ppermute(last_run, SKY_TM, pairs)
-    (wide,) = run_kernel(
-        widen_kernel, 0, [(32, WIDE)],
-        band_coef.reshape(3, 3, 4, 128), extra_diag.reshape(3, 4, 128), before, after,
-    )
     outgoing, resid, sources = run_kernel(
         return_kernel, 2, back_shapes,
-        live_count, tm, plain, up, down, across, up, down, inverses, sources, resid,
+        live_count, tm, across, plain, up, down, up, down, inverses, sources, resid,
         att_partials, src_partials, cols, by_source, by_row, pack, index,
         scratch=[(HEAD, 128)], second=False,
     )
     got = lax.all_to_all(outgoing, SKY, 0, 0, tiled=True)
-    knots, served, pick = run_kernel(
-        smooth_kernel, 1, [(3, 4, 128), (SKY_N, 2, 128), half(128, SKY_N)],
-        band_offsets, got, pack, attitude.reshape(3, 4, 128), wide, choose, choose, last=False,
+    knots, served, pick, rims = run_kernel(
+        smooth_kernel, 4, [(3, 4, 128), (SKY_N, 2, 128), half(128, SKY_N), (32, 128)],
+        offsets, chip, core, tm, got, knots, wide, sides, up, down, choose, last=False,
     )
     arrived = lax.all_to_all(served, SKY, 0, 0, tiled=True)
     resid, mine = run_kernel(
@@ -509,14 +595,14 @@
     above = lax.ppermute(mine, "tm", shifts(-1))
     outgoing, resid, step = run_kernel(
         return_kernel, 2, back_shapes,
-        live_count, tm, mine, below, above, across, up, down, inverses, sources, resid,
+        live_count, tm, across, mine, below, above, up, down, inverses, sources, resid,
         att_partials, src_partials, cols, by_source, by_row, pack, index,
         scratch=[(HEAD, 128)], second=True,
     )
     got = lax.all_to_all(outgoing, SKY, 0, 0, tiled=True)
     knots, sources = run_kernel(
-        smooth_kernel, 1, [(3, 4, 128), (5, SRC_N)],
-        band_offsets, got, pick, knots, wide, sources, step, last=True,
+        smooth_kernel, 4, [(3, 4, 128), (5, SRC_N)],
+        offsets, chip, core, tm, got, knots, wide, sources, step, pick, rims, last=True,
     )
     return (sources, knots.reshape(3, 1, RUN))
 

time: 99 us -> 96.7 us (0.977)
  blocking collectives: 32.3 us -> 46.9 us
  starting transfers between devices: 35.2 us -> 23.4 us
  waiting for transfers between devices: 18.5 us -> 13.1 us
  Pallas kernels: 8.94 us -> 10.7 us
  local copies, waits for them, and re-layouts: 2.08 us -> 0.65 us
    all_to_all x1 -> x2, blocking collectives: 15.9 us -> 32.4 us  [per_device(): got = lax.all_to_all(outgoing, SKY, 0, 0, tiled=True)]
    ppermute x2 -> x0, starting transfers between devices: 6.4 us -> none  [the longest x1 3.54 us: per_device(): before = lax.ppermute(last_run, SKY_TM, pairs)]
    all_to_all x1 -> x0, starting transfers between devices: 6.28 us -> none  [per_device(): got = lax.all_to_all(outgoing, SKY, 0, 0, tiled=True)]
    all_to_all x1 -> x0, waiting for transfers between devices: 6 us -> none  [per_device(): got = lax.all_to_all(outgoing, SKY, 0, 0, tiled=True)]
    all_to_all x1, waiting for transfers between devices: 2.69 us -> 6.71 us  [per_device(): near = lax.all_to_all(dense, ('x', 'z'), 0, 0, tiled=True)]
    ppermute x1, waiting for transfers between devices: 2.97 us -> 0.36 us  [per_device(): across = lax.ppermute(mine, 'tm', shifts(2))]
    ppermute x2 -> x0, waiting for transfers between devices: 2.45 us -> none  [the longest x1 1.68 us: per_device(): after = lax.ppermute(static[:, :128], SKY_TM, [(b, a) for a, b in pairs])]
    all_to_all x1, blocking collectives: 16.4 us -> 14.5 us  [per_device(): arrived = lax.all_to_all(served, SKY, 0, 0, tiled=True)]
  transfers between devices with their start and end apart: 11 -> 8, of which waited for: 8 -> 5; matrix products, arithmetic and copies ran while one was open for 0% -> 0% of each run, Pallas kernels for 1% -> 2%
where the time goes in v3:
time: 96.7 us; the launch traced here: 96.3 us
  blocking collectives  46.9 us (49%)
  starting transfers between devices  23.4 us (24%)
  waiting for transfers between devices  13.1 us (14%)
  Pallas kernels  10.7 us (11%)
  between operations  1.48 us (2%)
    all_to_all x2, blocking collectives, per_device(): got = lax.all_to_all(outgoing, SKY, 0, 0, tiled=True)  32.4 us
    all_to_all x1, blocking collectives, per_device(): arrived = lax.all_to_all(served, SKY, 0, 0, tiled=True)  14.5 us
    all_to_all x1, starting transfers between devices, per_device(): near = lax.all_to_all(dense, ('x', 'z'), 0, 0, tiled=True)  12 us
    pallas_call x7, Pallas kernels, run_kernel(): pl.pallas_call(kernel, out_shape=shapes, in_specs=specs, out_specs=[pl.Bl...  9.19 us
    all_to_all x1, waiting for transfers between devices, per_device(): near = lax.all_to_all(dense, ('x', 'z'), 0, 0, tiled=True)  6.71 us
    ppermute x1, starting transfers between devices, per_device(): far = lax.ppermute(near, 'c', [(0, 1), (1, 0)])  3.72 us
    ppermute x1, waiting for transfers between devices, per_device(): across = lax.ppermute(plain, 'tm', shifts(2))  2.58 us
    ppermute x1, waiting for transfers between devices, per_device(): below = lax.ppermute(mine, 'tm', shifts(1))  2.24 us
  transfers between devices with their start and end apart: 8, of which 5 were waited for; matrix products, arithmetic and copies ran while one was open for 0% of the time, Pallas kernels for 2%

profile of v3, /device:TPU:1, one launch (start us, length us, event | category | flops | bytes accessed | tf_op | source)
XLA Modules:
  0.0 96.3 jit_solution(9210112877486528865)
XLA Ops:
  0.6 1.5 %shard_map.132 = f32[32,4,4,128]{3,2,1,0:T(4,128)} custom-call(f32[3,4,128]{2,1,0:T(4,128)} %bitcast.13, f32[3,3,4,128]{3,2,1,0:T(4,128)} %bitcast.9, f32[3,4,128]{2,1,0:T(4,128)} %bitcast.11), custom_call_target="tpu_custom_call" | custom-call | tf_op jit(solution)/shard_map/pallas_call | solution.py:538
  2.2 0.0 copy-start
  2.2 0.0 copy-start.1
  2.2 0.0 copy-start.3
  2.2 0.0 copy-start.4
  2.2 0.0 copy-start.5
  2.2 12.0 %all-to-all-start = ((f32[32,4,4,128]{3,2,1,0:T(4,128)}), f32[32,4,4,128]{3,2,1,0:T(4,128)S(1)}, u32[]{:S(2)}, u32[]{:S(2)}) async-start(f32[32,4,4,128]{3,2,1,0:T(4,128)} %shard_map.132), calls=%async_computation | async-start | bytes 524288 | tf_op jit(solution)/shard_map/all_to_all | solution.py:551
  14.3 0.0 copy-start.6
  14.9 0.0 copy-start.8
  14.9 0.0 copy-start.9
  15.0 0.0 copy-start.10
  15.0 0.0 copy-done
  15.0 0.0 copy-done.1
  15.0 0.0 copy-done.3
  15.0 0.0 copy-done.4
  15.0 0.0 copy-done.5
  15.0 0.0 copy-done.6
  15.0 0.6 copy-done.8
  15.6 0.0 copy-done.9
  15.6 0.0 copy-done.10
  15.6 1.6 %shard_map.131 = (f32[128,128]{1,0:T(8,128)S(1)}, bf16[128,256]{1,0:T(8,128)(2,1)S(1)}, bf16[128,1024]{1,0:T(8,128)(2,1)S(1)}, f32[128,128]{1,0:T(8,128)S(1)}, b...) custom-call(s32[1]{0:T(128)S(6)} %copy.16.refs_0_, ...), custom_call_target="tpu_custom_call" | custom-call | flops 10000000 | bytes 2000000 | tf_op jit(solution)/shard_map/pallas_call | solution.py:494
  17.2 6.7 %all-to-all-done.refs_3_ = f32[32,4,4,128]{3,2,1,0:T(4,128)S(1)} async-done(((f32[32,4,4,128]{3,2,1,0:T(4,128)}), f32[32,4,4,128]{3,2,1,0:T(4,128)S(1)}, u32[]{:S(2)}, u32[]{:S(2)}) %all-to-all-start) | async-done | bytes 262176 | tf_op jit(solution)/shard_map/all_to_all | solution.py:551
  23.9 3.7 %collective-permute-start = (f32[32,4,4,128]{3,2,1,0:T(4,128)S(1)}, f32[32,4,4,128]{3,2,1,0:T(4,128)S(1)}, u32[]{:S(2)}, u32[]{:S(2)}) collective-permute-start(f32[32,4,4,128]{3,2,1,0:T(4,128)S(1)} %all-to-all-done.refs_3_), channel_id=1, source_target_pairs={{0,4},{4,0},{1,5},{5,1},{2,6},{6,2},{3,7},{7,3},{8,12},{12,8},{9,1... | collective-permute-start | bytes 786440 | tf_op jit(solution)/shard_map/ppermute | solution.py:565
  27.7 1.2 %collective-permute-done.refs_4_ = f32[32,4,4,128]{3,2,1,0:T(4,128)S(1)} collective-permute-done((f32[32,4,4,128]{3,2,1,0:T(4,128)S(1)}, f32[32,4,4,128]{3,2,1,0:T(4,128)S(1)}, u32[]{:S(2)}, u32[]{:S(2)}) %collective-permute-start) | collective-permute-done | bytes 262176 | tf_op jit(solution)/shard_map/ppermute | solution.py:565
  28.8 0.9 shard_map.133
  29.7 1.4 %collective-permute-start.2 = (f32[88,128]{1,0:T(8,128)S(1)}, f32[88,128]{1,0:T(8,128)S(1)}, u32[]{:S(2)}, u32[]{:S(2)}) collective-permute-start(f32[88,128]{1,0:T(8,128)S(1)} %get-tuple-element.48), channel_id=1, source_target_pairs={{0,1},{1,2},{2,3},{3,0},{4,5},{5,6},{6,7},{7,4},{8,9},{9,10},{10,1... | collective-permute-start | bytes 135176 | tf_op jit(solution)/shard_map/ppermute | solution.py:573
  31.1 1.5 %collective-permute-start.3 = (f32[88,128]{1,0:T(8,128)S(1)}, f32[88,128]{1,0:T(8,128)S(1)}, u32[]{:S(2)}, u32[]{:S(2)}) collective-permute-start(f32[88,128]{1,0:T(8,128)S(1)} %get-tuple-element.49), channel_id=1, source_target_pairs={{0,3},{1,0},{2,1},{3,2},{4,7},{5,4},{6,5},{7,6},{8,11},{9,8},{10,9... | collective-permute-start | bytes 135176 | tf_op jit(solution)/shard_map/ppermute | solution.py:574
  32.6 1.6 %collective-permute-start.1 = (f32[40,128]{1,0:T(8,128)S(1)}, f32[40,128]{1,0:T(8,128)S(1)}, u32[]{:S(2)}, u32[]{:S(2)}) collective-permute-start(f32[40,128]{1,0:T(8,128)S(1)} %get-tuple-element.47.refs_3_), channel_id=1, source_target_pairs={{0,2},{1,3},{2,0},{3,1},{4,6},{5,7},{6,4},{7,5},{8,10},{9,11},{10,... | collective-permute-start | bytes 61448 | tf_op jit(solution)/shard_map/ppermute | solution.py:572
  34.2 2.6 %collective-permute-done.1.refs_2_ = f32[40,128]{1,0:T(8,128)S(1)} collective-permute-done((f32[40,128]{1,0:T(8,128)S(1)}, f32[40,128]{1,0:T(8,128)S(1)}, u32[]{:S(2)}, u32[]{:S(2)}) %collective-permute-start.1) | collective-permute-done | bytes 20512 | tf_op jit(solution)/shard_map/ppermute | solution.py:572
  36.7 0.0 collective-permute-done.2.refs_4_.refs_6_.refs_8_
  36.8 0.0 collective-permute-done.3.refs_5_.refs_7_.refs_9_
  36.8 0.0 copy-done.2
  36.8 0.9 shard_map.134
  37.7 0.0 copy-start.7
  37.7 16.7 %all_to_all.20.refs_4_ = f32[64,4,128]{2,1,0:T(4,128)S(1)} all-to-all(f32[64,4,128]{2,1,0:T(4,128)S(1)} %get-tuple-element.54), channel_id=1, replica_groups=mesh['x'=4,'z'=8,'c'=2,'tm'=4] {'x','z','c'}, dimensions={0} | all-to-all | bytes 262144 | tf_op jit(solution)/shard_map/all_to_all | solution.py:582
  54.4 0.0 copy-done.7
  54.4 1.8 %shard_map.135 = (f32[3,4,128]{2,1,0:T(4,128)S(1)}, f32[64,2,128]{2,1,0:T(2,128)S(1)}, bf16[128,64]{1,0:T(8,128)(2,1)S(1)}, f32[32,128]{1,0:T(8,128)S(1)}) custom-call(s32[3]{0:T(128)S(1)} %get-tuple-element.36.refs_0_, s32[1]{0:T(128)} %bitcast.5.refs_2_.refs_1_, s32[1]{0:T(128)} %bitcast.refs_1_.refs_2_, s32[1]{0:T(128)} %bitcast.6.refs_1_.refs_3_, ...), custom_call_target="tpu_custom_call" | custom-call | flops 10000000 | bytes 2000000 | tf_op jit(solution)/shard_map/pallas_call | solution.py:494
  56.2 14.5 %all_to_all.21.refs_1_ = f32[64,2,128]{2,1,0:T(2,128)S(1)} all-to-all(f32[64,2,128]{2,1,0:T(2,128)S(1)} %get-tuple-element.57), channel_id=1, replica_groups=mesh['x'=4,'z'=8,'c'=2,'tm'=4] {'x','z','c'}, dimensions={0} | all-to-all | bytes 131072 | tf_op jit(solution)/shard_map/all_to_all | solution.py:587
  70.6 0.9 shard_map.136
  71.5 1.6 %collective-permute-start.6 = (f32[48,128]{1,0:T(8,128)S(1)}, f32[48,128]{1,0:T(8,128)S(1)}, u32[]{:S(2)}, u32[]{:S(2)}) collective-permute-start(f32[48,128]{1,0:T(8,128)S(1)} %get-tuple-element.60.refs_3_), channel_id=1, source_target_pairs={{0,3},{1,0},{2,1},{3,2},{4,7},{5,4},{6,5},{7,6},{8,11},{9,8},{10,9... | collective-permute-start | bytes 73736 | tf_op jit(solution)/shard_map/ppermute | solution.py:595
  73.1 0.0 collective-permute-start.5
  73.1 1.6 %collective-permute-start.4 = (f32[48,128]{1,0:T(8,128)S(1)}, f32[48,128]{1,0:T(8,128)S(1)}, u32[]{:S(2)}, u32[]{:S(2)}) collective-permute-start(f32[48,128]{1,0:T(8,128)S(1)} %get-tuple-element.60.refs_3_), channel_id=1, source_target_pairs={{0,2},{1,3},{2,0},{3,1},{4,6},{5,7},{6,4},{7,5},{8,10},{9,11},{10,... | collective-permute-start | bytes 73736 | tf_op jit(solution)/shard_map/ppermute | solution.py:593
  74.8 0.0 collective-permute-done.6.refs_5_
  74.8 2.2 %collective-permute-done.5.refs_4_ = f32[48,128]{1,0:T(8,128)S(1)} collective-permute-done((f32[48,128]{1,0:T(8,128)S(1)}, f32[48,128]{1,0:T(8,128)S(1)}, u32[]{:S(2)}, u32[]{:S(2)}) %collective-permute-start.5) | collective-permute-done | bytes 24608 | tf_op jit(solution)/shard_map/ppermute | solution.py:594
  77.0 0.4 collective-permute-done.4.refs_2_
  77.4 1.2 %shard_map.137 = (f32[64,4,128]{2,1,0:T(4,128)S(1)}, f32[128,128]{1,0:T(8,128)}, f32[5,1024]{1,0:T(8,128)S(1)}) custom-call(s32[1]{0:T(128)S(6)} %copy.16.refs_0_, s32[1]{0:T(128)} %bitcast.6.refs_1_.refs_3_, f32[48,128]{1,0:T(8,128)S(1)} %collective-permute-done.4.refs_2_, f32[48,128]{1,0:T(8,128)S(1)} %get-tuple-element.60.refs_3_, ...), custom_call_target="tpu_custom_call" | custom-call | flops 10000000 | bytes 2000000 | tf_op jit(solution)/shard_map/pallas_call | solution.py:494
  78.5 15.8 %all_to_all.22.refs_4_ = f32[64,4,128]{2,1,0:T(4,128)S(1)} all-to-all(f32[64,4,128]{2,1,0:T(4,128)S(1)} %get-tuple-element.63), channel_id=1, replica_groups=mesh['x'=4,'z'=8,'c'=2,'tm'=4] {'x','z','c'}, dimensions={0} | all-to-all | bytes 262144 | tf_op jit(solution)/shard_map/all_to_all | solution.py:602
  94.3 2.0 %shard_map.138 = (f32[3,4,128]{2,1,0:T(4,128)}, f32[5,1024]{1,0:T(8,128)}) custom-call(s32[3]{0:T(128)S(1)} %get-tuple-element.36.refs_0_, s32[1]{0:T(128)} %bitcast.5.refs_2_.refs_1_, s32[1]{0:T(128)} %bitcast.refs_1_.refs_2_, s32[1]{0:T(128)} %bitcast.6.refs_1_.refs_3_, f32[64,4,128]{2,1,0:T(4,128)S(1)} %all_to_all.22.refs_4_, ...), custom_call_target="tpu_custom_call" | custom-call | flops 10000000 | bytes 2000000 | tf_op jit(solution)/shard_map/pallas_call | solution.py:494
  (1 shorter events, 0.0 us)
Async XLA Ops:
  2.2 12.8 %copy-start = (bf16[5,128,128]{2,1,0:T(8,128)(2,1)S(1)}, bf16[5,128,128]{2,1,0:T(8,128)(2,1)}, u32[]{:S(2)}) copy-start(bf16[5,128,128]{2,1,0:T(8,128)(2,1)} %refs_12_.3) | copy-start | bytes 491524
  2.2 12.8 %copy-start.1 = (bf16[3,128,128]{2,1,0:T(8,128)(2,1)S(1)}, bf16[3,128,128]{2,1,0:T(8,128)(2,1)}, u32[]{:S(2)}) copy-start(bf16[3,128,128]{2,1,0:T(8,128)(2,1)} %refs_11_.3) | copy-start | bytes 294916
  2.2 12.8 %copy-start.3 = (f32[5,1024]{1,0:T(8,128)S(1)}, f32[5,1024]{1,0:T(8,128)}, u32[]{:S(2)}) copy-start(f32[5,1024]{1,0:T(8,128)} %refs_9_.1) | copy-start | bytes 61444
  2.2 12.8 %copy-start.4 = (f32[3,3,1,512]{3,2,1,0:T(1,128)S(1)}, f32[3,3,1,512]{3,2,1,0:T(1,128)}, u32[]{:S(2)}) copy-start(f32[3,3,1,512]{3,2,1,0:T(1,128)} %param.21) | copy-start | bytes 55300
  2.2 12.8 %copy-start.5 = (f32[128,128]{1,0:T(8,128)S(1)}, f32[128,128]{1,0:T(8,128)}, u32[]{:S(2)}) copy-start(f32[128,128]{1,0:T(8,128)} %refs_3_.2) | copy-start | bytes 196612
  2.2 21.7 %all-to-all-start = ((f32[32,4,4,128]{3,2,1,0:T(4,128)}), f32[32,4,4,128]{3,2,1,0:T(4,128)S(1)}, u32[]{:S(2)}, u32[]{:S(2)}) async-start(f32[32,4,4,128]{3,2,1,0:T(4,128)} %shard_map.132), calls=%async_computation | async-start | bytes 524288 | tf_op jit(solution)/shard_map/all_to_all | solution.py:551
  14.3 0.8 copy-start.6
  14.9 0.7 copy-start.8
  14.9 0.7 copy-start.9
  15.0 0.7 copy-start.10
  23.9 4.9 %collective-permute-start = (f32[32,4,4,128]{3,2,1,0:T(4,128)S(1)}, f32[32,4,4,128]{3,2,1,0:T(4,128)S(1)}, u32[]{:S(2)}, u32[]{:S(2)}) collective-permute-start(f32[32,4,4,128]{3,2,1,0:T(4,128)S(1)} %all-to-all-done.refs_3_), channel_id=1, source_target_pairs={{0,4},{4,0},{1,5},{5,1},{2,6},{6,2},{3,7},{7,3},{8,12},{12,8},{9,1... | collective-permute-start | bytes 786440 | tf_op jit(solution)/shard_map/ppermute | solution.py:565
  28.8 7.9 %copy-start.2 = (f32[5,5,1024]{2,1,0:T(8,128)S(1)}, f32[5,5,1024]{2,1,0:T(8,128)}, u32[]{:S(2)}) copy-start(f32[5,5,1024]{2,1,0:T(8,128)} %refs_8_.5) | copy-start | bytes 307204
  29.7 7.0 %collective-permute-start.2 = (f32[88,128]{1,0:T(8,128)S(1)}, f32[88,128]{1,0:T(8,128)S(1)}, u32[]{:S(2)}, u32[]{:S(2)}) collective-permute-start(f32[88,128]{1,0:T(8,128)S(1)} %get-tuple-element.48), channel_id=1, source_target_pairs={{0,1},{1,2},{2,3},{3,0},{4,5},{5,6},{6,7},{7,4},{8,9},{9,10},{10,1... | collective-permute-start | bytes 135176 | tf_op jit(solution)/shard_map/ppermute | solution.py:573
  31.1 5.7 %collective-permute-start.3 = (f32[88,128]{1,0:T(8,128)S(1)}, f32[88,128]{1,0:T(8,128)S(1)}, u32[]{:S(2)}, u32[]{:S(2)}) collective-permute-start(f32[88,128]{1,0:T(8,128)S(1)} %get-tuple-element.49), channel_id=1, source_target_pairs={{0,3},{1,0},{2,1},{3,2},{4,7},{5,4},{6,5},{7,6},{8,11},{9,8},{10,9... | collective-permute-start | bytes 135176 | tf_op jit(solution)/shard_map/ppermute | solution.py:574
  32.6 4.1 %collective-permute-start.1 = (f32[40,128]{1,0:T(8,128)S(1)}, f32[40,128]{1,0:T(8,128)S(1)}, u32[]{:S(2)}, u32[]{:S(2)}) collective-permute-start(f32[40,128]{1,0:T(8,128)S(1)} %get-tuple-element.47.refs_3_), channel_id=1, source_target_pairs={{0,2},{1,3},{2,0},{3,1},{4,6},{5,7},{6,4},{7,5},{8,10},{9,11},{10,... | collective-permute-start | bytes 61448 | tf_op jit(solution)/shard_map/ppermute | solution.py:572
  37.7 16.7 %copy-start.7 = (f32[3,1,512]{2,1,0:T(1,128)S(1)}, f32[3,1,512]{2,1,0:T(1,128)}, u32[]{:S(2)}) copy-start(f32[3,1,512]{2,1,0:T(1,128)} %param.20) | copy-start | bytes 18436
  71.5 3.2 %collective-permute-start.6 = (f32[48,128]{1,0:T(8,128)S(1)}, f32[48,128]{1,0:T(8,128)S(1)}, u32[]{:S(2)}, u32[]{:S(2)}) collective-permute-start(f32[48,128]{1,0:T(8,128)S(1)} %get-tuple-element.60.refs_3_), channel_id=1, source_target_pairs={{0,3},{1,0},{2,1},{3,2},{4,7},{5,4},{6,5},{7,6},{8,11},{9,8},{10,9... | collective-permute-start | bytes 73736 | tf_op jit(solution)/shard_map/ppermute | solution.py:595
  73.1 3.9 %collective-permute-start.5 = (f32[48,128]{1,0:T(8,128)S(1)}, f32[48,128]{1,0:T(8,128)S(1)}, u32[]{:S(2)}, u32[]{:S(2)}) collective-permute-start(f32[48,128]{1,0:T(8,128)S(1)} %get-tuple-element.60.refs_3_), channel_id=1, source_target_pairs={{0,1},{1,2},{2,3},{3,0},{4,5},{5,6},{6,7},{7,4},{8,9},{9,10},{10,1... | collective-permute-start | bytes 73736 | tf_op jit(solution)/shard_map/ppermute | solution.py:594
  73.1 4.2 %collective-permute-start.4 = (f32[48,128]{1,0:T(8,128)S(1)}, f32[48,128]{1,0:T(8,128)S(1)}, u32[]{:S(2)}, u32[]{:S(2)}) collective-permute-start(f32[48,128]{1,0:T(8,128)S(1)} %get-tuple-element.60.refs_3_), channel_id=1, source_target_pairs={{0,2},{1,3},{2,0},{3,1},{4,6},{5,7},{6,4},{7,5},{8,10},{9,11},{10,... | collective-permute-start | bytes 73736 | tf_op jit(solution)/shard_map/ppermute | solution.py:593

commit v4 on v3

--- a/solution.py
+++ b/solution.py
@@ -17,7 +17,6 @@
 TM_N = 4
 SRC_N = 1024
 RUN = 512
-WIDE = RUN + 128
 HEAD = 40
 SKY = ("x", "z", "c")
 SKY_TM = ("x", "z", "c", "tm")
@@ -40,6 +39,10 @@
 def halves(x):
     high = x.astype(BF16)
     return high, (x - high.astype(F32)).astype(BF16)
+
+
+def split_dot(twice, values):
+    return dot(twice, jnp.concatenate(halves(values), 0))
 
 
 def thirds(x):
@@ -152,9 +155,10 @@
     peer = iota((SKY_N, 128), 0)
     to_row = jnp.where(lb <= 1, h - 1, jnp.where(lb >= 30, h + 1, jnp.full_like(h, -1)))
     own = jnp.where(peer == h, 1.0, 0.0)
-    pack_ref[...] = jnp.concatenate([own, jnp.where(peer == to_row, 1.0, 0.0)], 1).astype(BF16)
+    edge = jnp.where(peer == to_row, 1.0, 0.0)
+    pack_ref[...] = jnp.concatenate([own, edge, own, edge], 1).astype(BF16)
     index_ref[...] = dot(own, jnp.where(group == cc + 2, (lbc + 1).astype(F32), 0.0))
-    peers_ref[...] = jnp.where(iota((128, SKY_N), 1) == hc, 1.0, 0.0).astype(BF16)
+    peers_ref[...] = jnp.where((iota((128, 128), 1) & 63) == hc, 1.0, 0.0).astype(BF16)
 
     sub8 = iota((8, 128), 0)
     after = (h == SKY_N - 1) & (lb >= 30) & (sub8 < 4)
@@ -286,10 +290,8 @@
     live_ref, got_ref, resid_in_ref, att_ref, src_ref, cols_ref, peers_ref, by_source_ref,
     by_lane_ref, choose_ref, resid_ref, send_ref,
 ):
-    table = jnp.concatenate([*halves(got_ref[:, 0, :]), *halves(got_ref[:, 1, :])], 1)
-    found = dot(peers_ref[...], table)
-    front = found[:, 0:128] + found[:, 128:256]
-    back = found[:, 256:384] + found[:, 384:512]
+    found = split_dot(peers_ref[...], jnp.concatenate([got_ref[:, 0, :], got_ref[:, 1, :]], 1))
+    front, back = found[:, 0:128], found[:, 128:256]
     group, cc = iota((128, 128), 1) >> 4, column(cols_ref, 3)
     masked = [
         jnp.where(group == cc, front, 0.0),
@@ -307,9 +309,9 @@
 def return_kernel(
     live_ref, tm_ref, across_ref, own_ref, below_ref, above_ref, up_ref, down_ref, inverses_ref,
     sources_in_ref, resid_in_ref, att_ref, src_ref, cols_ref, by_source_ref, by_row_ref, pack_ref,
-    index_ref, out_ref, resid_ref, sources_ref, total_ref, *, second,
+    index_ref, out_ref, sources_ref, *rest, second,
 ):
-    tm = tm_ref[0]
+    tm, total_ref = tm_ref[0], rest[-1]
     total_ref[...] = (
         own_ref[0:HEAD, :] + across_ref[0:HEAD, :] + below_ref[0:HEAD, :] + above_ref[0:HEAD, :]
     )
@@ -340,7 +342,8 @@
         ghost_change = ghost_change + item(3 + p) * ghost_values[p]
     used = jnp.where(iota((CROSS, 1), 0) < live_ref[0], 1.0, 0.0)
     resid = resid_in_ref[...] - used * change
-    resid_ref[...] = resid
+    if not second:
+        rest[0][...] = resid
     if second:
         ghost_resid = jnp.concatenate(
             [below_ref[HEAD : HEAD + 4, :], above_ref[HEAD + 4 : HEAD + 8, :]], 0
@@ -357,13 +360,12 @@
     edge_group = jnp.where(lbc <= 1, lbc, lbc - 24)
     own = group == cc + 2
     edge = group == edge_group
-    top, bottom = [], []
-    for a in range(3):
-        g = grads[128 * a : 128 * a + 128]
-        top += halves(jnp.where(own, g, 0.0))
-        bottom += halves(jnp.where(edge, g, 0.0))
-    table = jnp.concatenate([jnp.concatenate(top, 1), jnp.concatenate(bottom, 1)], 0)
-    packed = dot(pack_ref[...], table)
+    whole = jnp.concatenate([grads[128 * a : 128 * a + 128] for a in range(3)], 1)
+    high, low = halves(whole)
+    own3, edge3 = jnp.concatenate([own] * 3, 1), jnp.concatenate([edge] * 3, 1)
+    none = jnp.zeros_like(high)
+    table = [jnp.where(mask, part, none) for part in (high, low) for mask in (own3, edge3)]
+    packed = dot(pack_ref[...], jnp.concatenate(table, 0))
     peer = iota((SKY_N, 128), 0)
     ghost_group = iota((8, 128), 1) >> 4
     ghost_own = ghost_group == jnp.where(ghost8[:, 0:1] < 4, ghost_block - 24, ghost_block)
@@ -371,11 +373,11 @@
         ghost = jnp.where(ghost_own, grads[384 + 8 * a : 392 + 8 * a], 0.0)
         from_below = jnp.sum(jnp.where(ghost8 < 4, ghost, 0.0), axis=0, keepdims=True)
         from_above = jnp.sum(jnp.where(ghost8 >= 4, ghost, 0.0), axis=0, keepdims=True)
-        block = packed[:, 256 * a : 256 * a + 128] + packed[:, 256 * a + 128 : 256 * a + 256]
+        block = packed[:, 128 * a : 128 * a + 128]
         block = block + jnp.where(peer == 0, from_below, 0.0)
         block = block + jnp.where(peer == SKY_N - 1, from_above, 0.0)
         out_ref[:, a, :] = block
-    out_ref[:, 3, :] = index_ref[...]
+    out_ref[:, 3, :] = jnp.zeros((SKY_N, 128), F32) if second else index_ref[...]
 
 
 def smooth_kernel(
@@ -399,56 +401,67 @@
         for i in range(4):
             outs[3][8 * i : 8 * i + 8, :] = rims[i]
         index = got_ref[:, 3, :]
-        square = jnp.concatenate([index, jnp.zeros((128 - SKY_N, 128), F32)], 0).T
-        block32 = (iota((32, SKY_N), 0) + 1).astype(F32)
+        square = jnp.concatenate([index, index], 0).T
+        block32 = (iota((32, 128), 0) + 1).astype(F32)
         pick = jnp.concatenate(
             [
-                jnp.where(square[16 * (2 + c) : 16 * (2 + c) + 1, 0:SKY_N] == block32, 1.0, 0.0)
+                jnp.where(square[16 * (2 + c) : 16 * (2 + c) + 1, :] == block32, 1.0, 0.0)
                 for c in range(4)
             ],
             0,
         ).astype(BF16)
         outs[2][...] = pick
     got = [got_ref[:, a, :] for a in range(3)]
-    table = jnp.concatenate([part for g in got for part in halves(g)], 1)
-    summed = dot(pick, table)
+    summed = split_dot(pick, jnp.concatenate(got, 1))
     row128 = iota((128, 128), 0)
     group128 = iota((128, 128), 1) >> 4
     keep = group128 == (row128 >> 5) + 2
     fold = fold_table()
     stack = []
     for a in range(3):
-        one = summed[:, 256 * a : 256 * a + 128] + summed[:, 256 * a + 128 : 256 * a + 256]
-        one = jnp.where(keep, one, 0.0)
+        one = jnp.where(keep, summed[:, 128 * a : 128 * a + 128], 0.0)
         stack.append(one[0:32] + one[32:64] + one[64:96] + one[96:128])
     high, low = halves(jnp.concatenate(stack, 0))
     spread = dot(jnp.concatenate([high, low], 1), jnp.concatenate([fold, fold], 0))
     in_row = (iota((8, 128), 1) >> 4) == iota((8, 128), 0)
-    sub_w = iota((8, WIDE), 0)
-    grad = jnp.zeros((8, WIDE), F32)
-    for a in range(3):
-        tiles = []
+    sub8, lane8 = iota((8, 128), 0), iota((8, 128), 1)
+    grad = [jnp.zeros((8, 128), F32)] * 5
+    for a in range(3):
+        for r in range(5):
+            if r < 4:
+                piece = jnp.where(in_row, spread[32 * a + 8 * r : 32 * a + 8 * r + 8], 0.0)
+            else:
+                piece = jnp.where((lane < 32) | (lane >= 96), got[a], 0.0)
+            grad[r] = jnp.where(sub8 == a, jnp.sum(piece, axis=0, keepdims=True), grad[r])
+    bands, scale = [], None
+    for i in range(4):
+        tiles = [wide_ref[8 * i : 8 * i + 8, 128 * r : 128 * r + 128] for r in range(4)]
+        if i < 3:
+            bands.append([*tiles, rims[i]])
+        else:
+            scale = [*tiles, rims[i]]
+    offsets = [offsets_ref[b] for b in range(3)]
+    wraps = [(lane8 < offset, lane8 >= 128 - offset) for offset in offsets]
+    delta = [g * f for g, f in zip(grad, scale, strict=True)]
+    for _ in range(2):
+        total = grad
+        for b in range(3):
+            low = [pltpu.roll(d, offsets[b], 1) for d in delta]
+            high = [pltpu.roll(d, 128 - offsets[b], 1) for d in delta]
+            first, final = wraps[b]
+            total = [
+                total[r]
+                + bands[b][r]
+                * (
+                    jnp.where(first, low[(r + 4) % 5], low[r])
+                    + jnp.where(final, high[(r + 1) % 5], high[r])
+                )
+                for r in range(5)
+            ]
+        delta = [t * f for t, f in zip(total, scale, strict=True)]
+    for a in range(3):
         for r in range(4):
-            piece = spread[32 * a + 8 * r : 32 * a + 8 * r + 8]
-            tiles.append(jnp.sum(jnp.where(in_row, piece, 0.0), axis=0, keepdims=True))
-        rim = jnp.where((lane < 32) | (lane >= 96), got[a], 0.0)
-        tiles.append(jnp.sum(rim, axis=0, keepdims=True))
-        grad = jnp.where(sub_w == a, jnp.concatenate(tiles, 1), grad)
-    *bands, scale = (
-        jnp.concatenate([wide_ref[8 * i : 8 * i + 8, :], rims[i]], 1) for i in range(4)
-    )
-    delta = grad * scale
-    for _ in range(2):
-        total = jnp.zeros((8, WIDE), F32)
-        for b in range(3):
-            offset = offsets_ref[b]
-            upper = pltpu.roll(delta, WIDE - offset, 1)
-            lower = pltpu.roll(delta, offset, 1)
-            total = total + bands[b] * (upper + lower)
-        delta = (grad + total) * scale
-    for a in range(3):
-        for r in range(4):
-            tile = delta[a : a + 1, 128 * r : 128 * r + 128]
+            tile = delta[r][a : a + 1]
             knots_ref[a, r : r + 1, :] = knots_in_ref[a, r : r + 1, :] + tile
     if last:
         outs[1][...] = sources_in_ref[...] + step_ref[...]
@@ -457,24 +470,21 @@
     spreads = []
     for a in range(3):
         for r in range(4):
-            tile = delta[a : a + 1, 128 * r : 128 * r + 128]
+            tile = delta[r][a : a + 1]
             spreads.append(jnp.where(in_row, tile, 0.0))
     high, low = halves(jnp.concatenate(spreads, 0))
     blocks = dot(jnp.concatenate([high, low], 1), jnp.concatenate([fold, fold], 0))
-    tables = [part for a in range(3) for part in halves(blocks[32 * a : 32 * a + 32])]
+    table = jnp.concatenate([blocks[32 * a : 32 * a + 32] for a in range(3)], 1)
     slots = [index[:, 16 * (2 + c) : 16 * (2 + c) + 1].astype(I32) - 1 for c in range(4)]
     slot = jnp.concatenate(slots, 0)
-    by_block = jnp.where(iota((4 * SKY_N, 32), 1) == slot, 1.0, 0.0)
-    found = dot(by_block, jnp.concatenate(tables, 1))
+    by_block = jnp.where((iota((4 * SKY_N, 64), 1) & 31) == slot, 1.0, 0.0)
+    found = split_dot(by_block, table)
     group = lane >> 4
     front = jnp.zeros((SKY_N, 128), F32)
     back = jnp.zeros((SKY_N, 128), F32)
     for c in range(4):
         rows = found[SKY_N * c : SKY_N * (c + 1)]
-        part = [
-            rows[:, 256 * a : 256 * a + 128] + rows[:, 256 * a + 128 : 256 * a + 256]
-            for a in range(3)
-        ]
+        part = [rows[:, 128 * a : 128 * a + 128] for a in range(3)]
         front = jnp.where(group == c, part[0], jnp.where(group == c + 4, part[1], front))
         back = jnp.where(group == c, part[2], back)
     send_ref[:, 0, :] = front
@@ -556,7 +566,7 @@
         prepare_kernel, 3,
         [
             (128, 128), half(128, 256), half(128, SRC_N), (CROSS, ROWS), half(384, 128),
-            half(384, 128), half(SKY_N, 256), (SKY_N, 128), half(128, SKY_N), (8, 128), (40, 128),
+            half(384, 128), half(SKY_N, 512), (SKY_N, 128), half(128, 128), (8, 128), (40, 128),
             (40, 128), (32, RUN), jax.ShapeDtypeStruct((3,), I32),
         ],
         live_count, core, band_offsets, observed, att_partials, src_partials, slot, kb, sources, bands, extra,
@@ -572,16 +582,16 @@
     across = lax.ppermute(plain, "tm", shifts(2))
     up = lax.ppermute(up, "tm", shifts(1))
     down = lax.ppermute(down, "tm", shifts(-1))
-    back_shapes = [(SKY_N, 4, 128), (CROSS, ROWS), (5, SRC_N)]
-    outgoing, resid, sources = run_kernel(
-        return_kernel, 2, back_shapes,
+    back_shapes = [(SKY_N, 4, 128), (5, SRC_N)]
+    outgoing, sources, resid = run_kernel(
+        return_kernel, 2, [*back_shapes, (CROSS, ROWS)],
         live_count, tm, across, plain, up, down, up, down, inverses, sources, resid,
         att_partials, src_partials, cols, by_source, by_row, pack, index,
         scratch=[(HEAD, 128)], second=False,
     )
     got = lax.all_to_all(outgoing, SKY, 0, 0, tiled=True)
     knots, served, pick, rims = run_kernel(
-        smooth_kernel, 4, [(3, 4, 128), (SKY_N, 2, 128), half(128, SKY_N), (32, 128)],
+        smooth_kernel, 4, [(3, 4, 128), (SKY_N, 2, 128), half(128, 128), (32, 128)],
         offsets, chip, core, tm, got, knots, wide, sides, up, down, choose, last=False,
     )
     arrived = lax.all_to_all(served, SKY, 0, 0, tiled=True)
@@ -593,7 +603,7 @@
     across = lax.ppermute(mine, "tm", shifts(2))
     below = lax.ppermute(mine, "tm", shifts(1))
     above = lax.ppermute(mine, "tm", shifts(-1))
-    outgoing, resid, step = run_kernel(
+    outgoing, step = run_kernel(
         return_kernel, 2, back_shapes,
         live_count, tm, across, mine, below, above, up, down, inverses, sources, resid,
         att_partials, src_partials, cols, by_source, by_row, pack, index,

time: 96.7 us -> 95.8 us (level)
  no operation moved by 1% of the time
where the time goes in v4:
time: 95.8 us; the launch traced here: 95.3 us
  blocking collectives  46.9 us (49%)
  starting transfers between devices  23.4 us (24%)
  waiting for transfers between devices  13.1 us (14%)
  Pallas kernels  9.79 us (10%)
  between operations  1.48 us (2%)
    all_to_all x2, blocking collectives, per_device(): got = lax.all_to_all(outgoing, SKY, 0, 0, tiled=True)  32.5 us
    all_to_all x1, blocking collectives, per_device(): arrived = lax.all_to_all(served, SKY, 0, 0, tiled=True)  14.5 us
    all_to_all x1, starting transfers between devices, per_device(): near = lax.all_to_all(dense, ('x', 'z'), 0, 0, tiled=True)  12 us
    pallas_call x7, Pallas kernels, run_kernel(): pl.pallas_call(kernel, out_shape=shapes, in_specs=specs, out_specs=[pl.Bl...  8.24 us
    all_to_all x1, waiting for transfers between devices, per_device(): near = lax.all_to_all(dense, ('x', 'z'), 0, 0, tiled=True)  6.71 us
    ppermute x1, starting transfers between devices, per_device(): far = lax.ppermute(near, 'c', [(0, 1), (1, 0)])  3.72 us
    ppermute x1, waiting for transfers between devices, per_device(): across = lax.ppermute(plain, 'tm', shifts(2))  2.58 us
    ppermute x1, waiting for transfers between devices, per_device(): below = lax.ppermute(mine, 'tm', shifts(1))  2.24 us
  transfers between devices with their start and end apart: 8, of which 5 were waited for; matrix products, arithmetic and copies ran while one was open for 0% of the time, Pallas kernels for 2%

profile of v4, /device:TPU:1, one launch (start us, length us, event | category | flops | bytes accessed | tf_op | source)
XLA Modules:
  0.0 95.3 jit_solution(14129659394488912730)
XLA Ops:
  0.6 1.5 %shard_map.132 = f32[32,4,4,128]{3,2,1,0:T(4,128)} custom-call(f32[3,4,128]{2,1,0:T(4,128)} %bitcast.13, f32[3,3,4,128]{3,2,1,0:T(4,128)} %bitcast.9, f32[3,4,128]{2,1,0:T(4,128)} %bitcast.11), custom_call_target="tpu_custom_call" | custom-call | tf_op jit(solution)/shard_map/pallas_call | solution.py:548
  2.2 0.0 copy-start
  2.2 0.0 copy-start.1
  2.2 0.0 copy-start.3
  2.2 0.0 copy-start.4
  2.2 0.0 copy-start.5
  2.2 12.0 %all-to-all-start = ((f32[32,4,4,128]{3,2,1,0:T(4,128)}), f32[32,4,4,128]{3,2,1,0:T(4,128)S(1)}, u32[]{:S(2)}, u32[]{:S(2)}) async-start(f32[32,4,4,128]{3,2,1,0:T(4,128)} %shard_map.132), calls=%async_computation | async-start | bytes 524288 | tf_op jit(solution)/shard_map/all_to_all | solution.py:561
  14.3 0.0 copy-start.6
  14.9 0.0 copy-start.8
  14.9 0.0 copy-start.9
  15.0 0.0 copy-start.10
  15.0 0.0 copy-done
  15.0 0.0 copy-done.1
  15.0 0.0 copy-done.3
  15.0 0.0 copy-done.4
  15.0 0.0 copy-done.5
  15.0 0.0 copy-done.6
  15.0 0.6 copy-done.8
  15.6 0.0 copy-done.9
  15.6 0.0 copy-done.10
  15.6 1.6 %shard_map.131 = (f32[128,128]{1,0:T(8,128)S(1)}, bf16[128,256]{1,0:T(8,128)(2,1)S(1)}, bf16[128,1024]{1,0:T(8,128)(2,1)S(1)}, f32[128,128]{1,0:T(8,128)S(1)}, b...) custom-call(s32[1]{0:T(128)S(6)} %copy.16.refs_0_, ...), custom_call_target="tpu_custom_call" | custom-call | flops 10000000 | bytes 2000000 | tf_op jit(solution)/shard_map/pallas_call | solution.py:504
  17.2 6.7 %all-to-all-done.refs_3_ = f32[32,4,4,128]{3,2,1,0:T(4,128)S(1)} async-done(((f32[32,4,4,128]{3,2,1,0:T(4,128)}), f32[32,4,4,128]{3,2,1,0:T(4,128)S(1)}, u32[]{:S(2)}, u32[]{:S(2)}) %all-to-all-start) | async-done | bytes 262176 | tf_op jit(solution)/shard_map/all_to_all | solution.py:561
  23.9 3.7 %collective-permute-start = (f32[32,4,4,128]{3,2,1,0:T(4,128)S(1)}, f32[32,4,4,128]{3,2,1,0:T(4,128)S(1)}, u32[]{:S(2)}, u32[]{:S(2)}) collective-permute-start(f32[32,4,4,128]{3,2,1,0:T(4,128)S(1)} %all-to-all-done.refs_3_), channel_id=1, source_target_pairs={{0,4},{4,0},{1,5},{5,1},{2,6},{6,2},{3,7},{7,3},{8,12},{12,8},{9,1... | collective-permute-start | bytes 786440 | tf_op jit(solution)/shard_map/ppermute | solution.py:575
  27.7 1.2 %collective-permute-done.refs_4_ = f32[32,4,4,128]{3,2,1,0:T(4,128)S(1)} collective-permute-done((f32[32,4,4,128]{3,2,1,0:T(4,128)S(1)}, f32[32,4,4,128]{3,2,1,0:T(4,128)S(1)}, u32[]{:S(2)}, u32[]{:S(2)}) %collective-permute-start) | collective-permute-done | bytes 262176 | tf_op jit(solution)/shard_map/ppermute | solution.py:575
  28.8 0.9 shard_map.133
  29.7 1.4 %collective-permute-start.2 = (f32[88,128]{1,0:T(8,128)S(1)}, f32[88,128]{1,0:T(8,128)S(1)}, u32[]{:S(2)}, u32[]{:S(2)}) collective-permute-start(f32[88,128]{1,0:T(8,128)S(1)} %get-tuple-element.48), channel_id=1, source_target_pairs={{0,1},{1,2},{2,3},{3,0},{4,5},{5,6},{6,7},{7,4},{8,9},{9,10},{10,1... | collective-permute-start | bytes 135176 | tf_op jit(solution)/shard_map/ppermute | solution.py:583
  31.1 1.5 %collective-permute-start.3 = (f32[88,128]{1,0:T(8,128)S(1)}, f32[88,128]{1,0:T(8,128)S(1)}, u32[]{:S(2)}, u32[]{:S(2)}) collective-permute-start(f32[88,128]{1,0:T(8,128)S(1)} %get-tuple-element.49), channel_id=1, source_target_pairs={{0,3},{1,0},{2,1},{3,2},{4,7},{5,4},{6,5},{7,6},{8,11},{9,8},{10,9... | collective-permute-start | bytes 135176 | tf_op jit(solution)/shard_map/ppermute | solution.py:584
  32.6 1.6 %collective-permute-start.1 = (f32[40,128]{1,0:T(8,128)S(1)}, f32[40,128]{1,0:T(8,128)S(1)}, u32[]{:S(2)}, u32[]{:S(2)}) collective-permute-start(f32[40,128]{1,0:T(8,128)S(1)} %get-tuple-element.47.refs_3_), channel_id=1, source_target_pairs={{0,2},{1,3},{2,0},{3,1},{4,6},{5,7},{6,4},{7,5},{8,10},{9,11},{10,... | collective-permute-start | bytes 61448 | tf_op jit(solution)/shard_map/ppermute | solution.py:582
  34.2 2.6 %collective-permute-done.1.refs_2_ = f32[40,128]{1,0:T(8,128)S(1)} collective-permute-done((f32[40,128]{1,0:T(8,128)S(1)}, f32[40,128]{1,0:T(8,128)S(1)}, u32[]{:S(2)}, u32[]{:S(2)}) %collective-permute-start.1) | collective-permute-done | bytes 20512 | tf_op jit(solution)/shard_map/ppermute | solution.py:582
  36.7 0.0 collective-permute-done.2.refs_4_.refs_6_.refs_8_
  36.8 0.0 collective-permute-done.3.refs_5_.refs_7_.refs_9_
  36.8 0.0 copy-done.2
  36.8 1.0 %shard_map.134 = (f32[64,4,128]{2,1,0:T(4,128)S(1)}, f32[5,1024]{1,0:T(8,128)S(1)}, f32[128,128]{1,0:T(8,128)S(1)}) custom-call(s32[1]{0:T(128)S(6)} %copy.16.refs_0_, s32[1]{0:T(128)} %bitcast.6.refs_1_.refs_3_, f32[40,128]{1,0:T(8,128)S(1)} %collective-permute-done.1.refs_2_, f32[40,128]{1,0:T(8,128)S(1)} %get-tuple-element.47.refs_3_, ...), custom_call_target="tpu_custom_call" | custom-call | flops 10000000 | bytes 2000000 | tf_op jit(solution)/shard_map/pallas_call | solution.py:504
  37.7 0.0 copy-start.7
  37.7 16.7 %all_to_all.20.refs_4_ = f32[64,4,128]{2,1,0:T(4,128)S(1)} all-to-all(f32[64,4,128]{2,1,0:T(4,128)S(1)} %get-tuple-element.54), channel_id=1, replica_groups=mesh['x'=4,'z'=8,'c'=2,'tm'=4] {'x','z','c'}, dimensions={0} | all-to-all | bytes 262144 | tf_op jit(solution)/shard_map/all_to_all | solution.py:592
  54.4 0.0 copy-done.7
  54.4 1.5 %shard_map.135 = (f32[3,4,128]{2,1,0:T(4,128)S(1)}, f32[64,2,128]{2,1,0:T(2,128)S(1)}, bf16[128,128]{1,0:T(8,128)(2,1)S(1)}, f32[32,128]{1,0:T(8,128)S(1)}) custom-call(s32[3]{0:T(128)S(1)} %get-tuple-element.36.refs_0_, s32[1]{0:T(128)} %bitcast.5.refs_2_.refs_1_, s32[1]{0:T(128)} %bitcast.refs_1_.refs_2_, s32[1]{0:T(128)} %bitcast.6.refs_1_.refs_3_, ...), custom_call_target="tpu_custom_call" | custom-call | flops 10000000 | bytes 2000000 | tf_op jit(solution)/shard_map/pallas_call | solution.py:504
  55.9 14.5 %all_to_all.21.refs_1_ = f32[64,2,128]{2,1,0:T(2,128)S(1)} all-to-all(f32[64,2,128]{2,1,0:T(2,128)S(1)} %get-tuple-element.57), channel_id=1, replica_groups=mesh['x'=4,'z'=8,'c'=2,'tm'=4] {'x','z','c'}, dimensions={0} | all-to-all | bytes 131072 | tf_op jit(solution)/shard_map/all_to_all | solution.py:597
  70.3 0.7 shard_map.136
  71.1 1.6 %collective-permute-start.6 = (f32[48,128]{1,0:T(8,128)S(1)}, f32[48,128]{1,0:T(8,128)S(1)}, u32[]{:S(2)}, u32[]{:S(2)}) collective-permute-start(f32[48,128]{1,0:T(8,128)S(1)} %get-tuple-element.60.refs_3_), channel_id=1, source_target_pairs={{0,3},{1,0},{2,1},{3,2},{4,7},{5,4},{6,5},{7,6},{8,11},{9,8},{10,9... | collective-permute-start | bytes 73736 | tf_op jit(solution)/shard_map/ppermute | solution.py:605
  72.7 0.0 collective-permute-start.5
  72.7 1.6 %collective-permute-start.4 = (f32[48,128]{1,0:T(8,128)S(1)}, f32[48,128]{1,0:T(8,128)S(1)}, u32[]{:S(2)}, u32[]{:S(2)}) collective-permute-start(f32[48,128]{1,0:T(8,128)S(1)} %get-tuple-element.60.refs_3_), channel_id=1, source_target_pairs={{0,2},{1,3},{2,0},{3,1},{4,6},{5,7},{6,4},{7,5},{8,10},{9,11},{10,... | collective-permute-start | bytes 73736 | tf_op jit(solution)/shard_map/ppermute | solution.py:603
  74.3 0.0 collective-permute-done.6.refs_5_
  74.3 2.2 %collective-permute-done.5.refs_4_ = f32[48,128]{1,0:T(8,128)S(1)} collective-permute-done((f32[48,128]{1,0:T(8,128)S(1)}, f32[48,128]{1,0:T(8,128)S(1)}, u32[]{:S(2)}, u32[]{:S(2)}) %collective-permute-start.5) | collective-permute-done | bytes 24608 | tf_op jit(solution)/shard_map/ppermute | solution.py:604
  76.6 0.4 collective-permute-done.4.refs_2_
  76.9 0.9 shard_map.137
  77.9 15.8 %all_to_all.22.refs_4_ = f32[64,4,128]{2,1,0:T(4,128)S(1)} all-to-all(f32[64,4,128]{2,1,0:T(4,128)S(1)} %get-tuple-element.63), channel_id=1, replica_groups=mesh['x'=4,'z'=8,'c'=2,'tm'=4] {'x','z','c'}, dimensions={0} | all-to-all | bytes 262144 | tf_op jit(solution)/shard_map/all_to_all | solution.py:612
  93.7 1.7 %shard_map.138 = (f32[3,4,128]{2,1,0:T(4,128)}, f32[5,1024]{1,0:T(8,128)}) custom-call(s32[3]{0:T(128)S(1)} %get-tuple-element.36.refs_0_, s32[1]{0:T(128)} %bitcast.5.refs_2_.refs_1_, s32[1]{0:T(128)} %bitcast.refs_1_.refs_2_, s32[1]{0:T(128)} %bitcast.6.refs_1_.refs_3_, f32[64,4,128]{2,1,0:T(4,128)S(1)} %all_to_all.22.refs_4_, ...), custom_call_target="tpu_custom_call" | custom-call | flops 10000000 | bytes 2000000 | tf_op jit(solution)/shard_map/pallas_call | solution.py:504
  (1 shorter events, 0.0 us)
Async XLA Ops:
  2.2 12.8 %copy-start = (bf16[5,128,128]{2,1,0:T(8,128)(2,1)S(1)}, bf16[5,128,128]{2,1,0:T(8,128)(2,1)}, u32[]{:S(2)}) copy-start(bf16[5,128,128]{2,1,0:T(8,128)(2,1)} %refs_12_.3) | copy-start | bytes 491524
  2.2 12.8 %copy-start.1 = (bf16[3,128,128]{2,1,0:T(8,128)(2,1)S(1)}, bf16[3,128,128]{2,1,0:T(8,128)(2,1)}, u32[]{:S(2)}) copy-start(bf16[3,128,128]{2,1,0:T(8,128)(2,1)} %refs_11_.3) | copy-start | bytes 294916
  2.2 12.8 %copy-start.3 = (f32[5,1024]{1,0:T(8,128)S(1)}, f32[5,1024]{1,0:T(8,128)}, u32[]{:S(2)}) copy-start(f32[5,1024]{1,0:T(8,128)} %refs_9_.1) | copy-start | bytes 61444
  2.2 12.8 %copy-start.4 = (f32[3,3,1,512]{3,2,1,0:T(1,128)S(1)}, f32[3,3,1,512]{3,2,1,0:T(1,128)}, u32[]{:S(2)}) copy-start(f32[3,3,1,512]{3,2,1,0:T(1,128)} %param.21) | copy-start | bytes 55300
  2.2 12.8 %copy-start.5 = (f32[128,128]{1,0:T(8,128)S(1)}, f32[128,128]{1,0:T(8,128)}, u32[]{:S(2)}) copy-start(f32[128,128]{1,0:T(8,128)} %refs_3_.2) | copy-start | bytes 196612
  2.2 21.7 %all-to-all-start = ((f32[32,4,4,128]{3,2,1,0:T(4,128)}), f32[32,4,4,128]{3,2,1,0:T(4,128)S(1)}, u32[]{:S(2)}, u32[]{:S(2)}) async-start(f32[32,4,4,128]{3,2,1,0:T(4,128)} %shard_map.132), calls=%async_computation | async-start | bytes 524288 | tf_op jit(solution)/shard_map/all_to_all | solution.py:561
  14.3 0.8 copy-start.6
  14.9 0.7 copy-start.8
  14.9 0.7 copy-start.9
  15.0 0.7 copy-start.10
  23.9 4.9 %collective-permute-start = (f32[32,4,4,128]{3,2,1,0:T(4,128)S(1)}, f32[32,4,4,128]{3,2,1,0:T(4,128)S(1)}, u32[]{:S(2)}, u32[]{:S(2)}) collective-permute-start(f32[32,4,4,128]{3,2,1,0:T(4,128)S(1)} %all-to-all-done.refs_3_), channel_id=1, source_target_pairs={{0,4},{4,0},{1,5},{5,1},{2,6},{6,2},{3,7},{7,3},{8,12},{12,8},{9,1... | collective-permute-start | bytes 786440 | tf_op jit(solution)/shard_map/ppermute | solution.py:575
  28.8 7.9 %copy-start.2 = (f32[5,5,1024]{2,1,0:T(8,128)S(1)}, f32[5,5,1024]{2,1,0:T(8,128)}, u32[]{:S(2)}) copy-start(f32[5,5,1024]{2,1,0:T(8,128)} %refs_8_.5) | copy-start | bytes 307204
  29.7 7.0 %collective-permute-start.2 = (f32[88,128]{1,0:T(8,128)S(1)}, f32[88,128]{1,0:T(8,128)S(1)}, u32[]{:S(2)}, u32[]{:S(2)}) collective-permute-start(f32[88,128]{1,0:T(8,128)S(1)} %get-tuple-element.48), channel_id=1, source_target_pairs={{0,1},{1,2},{2,3},{3,0},{4,5},{5,6},{6,7},{7,4},{8,9},{9,10},{10,1... | collective-permute-start | bytes 135176 | tf_op jit(solution)/shard_map/ppermute | solution.py:583
  31.1 5.7 %collective-permute-start.3 = (f32[88,128]{1,0:T(8,128)S(1)}, f32[88,128]{1,0:T(8,128)S(1)}, u32[]{:S(2)}, u32[]{:S(2)}) collective-permute-start(f32[88,128]{1,0:T(8,128)S(1)} %get-tuple-element.49), channel_id=1, source_target_pairs={{0,3},{1,0},{2,1},{3,2},{4,7},{5,4},{6,5},{7,6},{8,11},{9,8},{10,9... | collective-permute-start | bytes 135176 | tf_op jit(solution)/shard_map/ppermute | solution.py:584
  32.6 4.1 %collective-permute-start.1 = (f32[40,128]{1,0:T(8,128)S(1)}, f32[40,128]{1,0:T(8,128)S(1)}, u32[]{:S(2)}, u32[]{:S(2)}) collective-permute-start(f32[40,128]{1,0:T(8,128)S(1)} %get-tuple-element.47.refs_3_), channel_id=1, source_target_pairs={{0,2},{1,3},{2,0},{3,1},{4,6},{5,7},{6,4},{7,5},{8,10},{9,11},{10,... | collective-permute-start | bytes 61448 | tf_op jit(solution)/shard_map/ppermute | solution.py:582
  37.7 16.7 %copy-start.7 = (f32[3,1,512]{2,1,0:T(1,128)S(1)}, f32[3,1,512]{2,1,0:T(1,128)}, u32[]{:S(2)}) copy-start(f32[3,1,512]{2,1,0:T(1,128)} %param.20) | copy-start | bytes 18436
  71.1 3.2 %collective-permute-start.6 = (f32[48,128]{1,0:T(8,128)S(1)}, f32[48,128]{1,0:T(8,128)S(1)}, u32[]{:S(2)}, u32[]{:S(2)}) collective-permute-start(f32[48,128]{1,0:T(8,128)S(1)} %get-tuple-element.60.refs_3_), channel_id=1, source_target_pairs={{0,3},{1,0},{2,1},{3,2},{4,7},{5,4},{6,5},{7,6},{8,11},{9,8},{10,9... | collective-permute-start | bytes 73736 | tf_op jit(solution)/shard_map/ppermute | solution.py:605
  72.7 3.9 %collective-permute-start.5 = (f32[48,128]{1,0:T(8,128)S(1)}, f32[48,128]{1,0:T(8,128)S(1)}, u32[]{:S(2)}, u32[]{:S(2)}) collective-permute-start(f32[48,128]{1,0:T(8,128)S(1)} %get-tuple-element.60.refs_3_), channel_id=1, source_target_pairs={{0,1},{1,2},{2,3},{3,0},{4,5},{5,6},{6,7},{7,4},{8,9},{9,10},{10,1... | collective-permute-start | bytes 73736 | tf_op jit(solution)/shard_map/ppermute | solution.py:604
  72.7 4.3 %collective-permute-start.4 = (f32[48,128]{1,0:T(8,128)S(1)}, f32[48,128]{1,0:T(8,128)S(1)}, u32[]{:S(2)}, u32[]{:S(2)}) collective-permute-start(f32[48,128]{1,0:T(8,128)S(1)} %get-tuple-element.60.refs_3_), channel_id=1, source_target_pairs={{0,2},{1,3},{2,0},{3,1},{4,6},{5,7},{6,4},{7,5},{8,10},{9,11},{10,... | collective-permute-start | bytes 73736 | tf_op jit(solution)/shard_map/ppermute | solution.py:603

commit v5 on v4

--- a/solution.py
+++ b/solution.py
@@ -73,22 +73,32 @@
     return jnp.where((iota((128, 128), 0) & 15) == (iota((128, 128), 1) & 15), 1.0, 0.0)
 
 
-def attitude_term(att_ref, masked, table_ref):
+def table_of(table):
+    return table if isinstance(table, jax.Array) else table[...]
+
+
+def attitude_term(att, masked, table_ref):
+    count = masked[0].shape[0]
     high, low = halves(jnp.concatenate(masked, 0))
-    spread = dot(jnp.concatenate([high, low, high], 1), table_ref[...])
-    total = jnp.zeros((CROSS, ROWS), F32)
-    for a in range(3):
-        total = total + att_ref[a].astype(F32) * spread[a * 128 : a * 128 + 128]
-    return total
-
-
-def send_normal(src_ref, resid, onehot, refs):
+    spread = dot(jnp.concatenate([high, low, high], 1), table_of(table_ref))
+    return sum(att[a].astype(F32) * spread[a * count : (a + 1) * count] for a in range(3))
+
+
+def products_sum(products_ref, masked):
     lane = iota((128, 128), 1)
     square = jnp.zeros((128, 128), F32)
     for p in range(5):
-        rhs = jnp.sum(src_ref[p].astype(F32) * resid, axis=1, keepdims=True)
-        square = jnp.where(lane == p, rhs, square)
-    rows = square.T[0:8]
+        terms = [
+            products_ref[128 * (3 * p + a) : 128 * (3 * p + a) + 128, :] * masked[a]
+            for a in range(3)
+        ]
+        row = jnp.sum(terms[0] + terms[1] + terms[2], axis=1, keepdims=True)
+        square = jnp.where(lane == p, row, square)
+    return square
+
+
+def send_normal(rhs, onehot, refs):
+    rows = rhs.T[0:8]
     parts = dot(jnp.concatenate(thirds(rows), 0), onehot)
     normal = parts[0:8] + parts[8:16] + parts[16:24]
     for ref in refs:
@@ -96,6 +106,11 @@
             ref[pl.ds(j, 5, stride=8), :] = normal[0:5, 128 * j : 128 * j + 128]
 
 
+def gradients(att, resid, table_ref):
+    high, low = halves(jnp.concatenate([att[a].astype(F32) * resid for a in range(3)], 0))
+    return dot(jnp.concatenate([high, low, high], 1), table_of(table_ref))
+
+
 def gather_source(values8, onehot):
     parts = dot_nt(onehot, jnp.concatenate(thirds(values8), 0))
     return [
@@ -118,11 +133,13 @@
 
 def prepare_kernel(
     live_ref, core_ref, offsets_in_ref, obs_ref, att_ref, src_ref, slot_ref, kb_ref, sources_ref,
-    bands_ref, extra_ref,
+    bands_ref, extra_ref, knots_in_ref,
     cols_ref, places_ref, by_source_ref, base_ref, by_lane_ref, by_row_ref, pack_ref, index_ref,
-    peers_ref, choose_ref, up_ref, down_ref, wide_ref, offsets_ref,
+    peers_ref, choose_ref, up_ref, down_ref, wide_ref, ghost_ref, products_ref, normals_ref, rhs_ref,
+    knots_ref, offsets_ref,
 ):
     live, core = live_ref[0], core_ref[0]
+    knots_ref[...] = knots_in_ref[...]
     for b in range(3):
         offsets_ref[b] = offsets_in_ref[b]
     kb, slot = kb_ref[...], slot_ref[...]
@@ -141,16 +158,32 @@
     group = lane >> 4
 
     place = (lbc >> 3) * CHIPS + (hc >> 1) + jnp.where((hc & 1) == core, 0, 128)
-    places_ref[...] = jnp.where(iota((128, 256), 1) == place, 1.0, 0.0).astype(BF16)
+    places = jnp.where(iota((128, 256), 1) == place, 1.0, 0.0)
     by_source = jnp.where(iota((128, SRC_N), 1) == slotc, 1.0, 0.0).astype(BF16)
     by_source_ref[...] = by_source
     values = gather_source(padded_rows(sources_ref[...]), by_source)
     src_term = jnp.zeros((CROSS, ROWS), F32)
     for p in range(5):
         src_term = src_term + src_ref[p].astype(F32) * values[p]
-    base_ref[...] = obs_ref[...] - src_term
+    used = jnp.where(iota((CROSS, 1), 0) < live, 1.0, 0.0)
+    base = (obs_ref[...] - src_term) * used
+    base_ref[...] = base
+    by_row = stacked_spline(spline_by_row())
+    rhs = jnp.zeros((128, 128), F32)
+    normals = [jnp.zeros((128, 128), F32)] * 5
+    for p in range(5):
+        one = src_ref[p].astype(F32) * used
+        rhs = jnp.where(lane == p, jnp.sum(one * base, axis=1, keepdims=True), rhs)
+        products_ref[384 * p : 384 * p + 384, :] = gradients(att_ref, one, by_row)
+        for q in range(p + 1):
+            both = jnp.sum(one * src_ref[q].astype(F32), axis=1, keepdims=True)
+            normals[q] = jnp.where(lane == p, both, normals[q])
+            normals[p] = jnp.where(lane == q, both, normals[p])
+    rhs_ref[...] = rhs
+    for q in range(5):
+        normals_ref[128 * q : 128 * q + 128, :] = normals[q]
     by_lane_ref[...] = stacked_spline(spline_by_lane())
-    by_row_ref[...] = stacked_spline(spline_by_row())
+    by_row_ref[...] = by_row
 
     peer = iota((SKY_N, 128), 0)
     to_row = jnp.where(lb <= 1, h - 1, jnp.where(lb >= 30, h + 1, jnp.full_like(h, -1)))
@@ -158,7 +191,7 @@
     edge = jnp.where(peer == to_row, 1.0, 0.0)
     pack_ref[...] = jnp.concatenate([own, edge, own, edge], 1).astype(BF16)
     index_ref[...] = dot(own, jnp.where(group == cc + 2, (lbc + 1).astype(F32), 0.0))
-    peers_ref[...] = jnp.where((iota((128, 128), 1) & 63) == hc, 1.0, 0.0).astype(BF16)
+    peers = jnp.where((iota((128, 128), 1) & 63) == hc, 1.0, 0.0)
 
     sub8 = iota((8, 128), 0)
     after = (h == SKY_N - 1) & (lb >= 30) & (sub8 < 4)
@@ -167,12 +200,20 @@
     choose = jnp.where(chosen, 1.0, 0.0)
     choose_ref[...] = choose
     pieces = [att_ref[a] for a in range(3)] + [src_ref[p] for p in range(5)]
+    pieces += [*halves(base), places.astype(BF16), peers.astype(BF16)]
     ghosts = dot(choose, jnp.concatenate(pieces, 1))
     items = [ghosts[:, 128 * i : 128 * i + 128] for i in range(8)]
+    empty = jnp.zeros((8, 256), F32)
+    places_ref[...] = jnp.concatenate([places, ghosts[:, 1280:1536], empty], 0).astype(BF16)
+    peers_ref[...] = jnp.concatenate([peers, ghosts[:, 1536:1664], empty[:, 0:128]], 0).astype(BF16)
     ghost_slot = jnp.sum(choose * slot.astype(F32), axis=1, keepdims=True)
     ghost_block = jnp.sum(choose * lb.astype(F32), axis=1, keepdims=True)
     items.append(jnp.zeros((8, 128), F32))
     items.append(jnp.where(iota((8, 128), 1) < 64, ghost_slot, ghost_block))
+    for a in range(3):
+        ghost_ref[8 * a : 8 * a + 8, :] = items[a]
+    ghost_ref[24:32, :] = ghosts[:, 1024:1152] + ghosts[:, 1152:1280]
+    ghost_ref[32:40, :] = items[9]
     for q in range(5):
         even, odd = items[2 * q], items[2 * q + 1]
         up_ref[8 * q : 8 * q + 8, :] = jnp.concatenate([even[0:4], odd[0:4]], 0)
@@ -250,9 +291,9 @@
 
 
 def first_kernel(
-    live_ref, core_ref, chip_ref, near_ref, far_ref, att_ref, src_ref, cols_ref, places_ref,
-    by_source_ref, base_ref, by_lane_ref, choose_ref, up_in_ref, down_in_ref,
-    resid_ref, plain_ref, up_ref, down_ref, sides_ref,
+    core_ref, chip_ref, near_ref, far_ref, cols_ref, places_ref, by_source_ref, by_lane_ref,
+    up_in_ref, down_in_ref, ghost_ref, products_ref, rhs_in_ref,
+    masked_ref, rhs_ref, plain_ref, up_ref, down_ref, sides_ref,
 ):
     tables = []
     for a in range(3):
@@ -260,16 +301,19 @@
         tables += halves(jnp.concatenate(rows, 0))
     found = dot(places_ref[...], jnp.concatenate(tables, 1))
     mine = (iota((128, 128), 1) >> 4) == (column(cols_ref, 1) & 7)
-    masked = []
+    facts = ghost_ref[32:40, :]
+    ghost_mine = (iota((8, 128), 1) >> 4) == (facts[:, 64:65].astype(I32) & 7)
+    masked, ghost_masked = [], []
     for a in range(3):
         whole = found[:, 256 * a : 256 * a + 128] + found[:, 256 * a + 128 : 256 * a + 256]
-        masked.append(jnp.where(mine, whole, 0.0))
-    used = jnp.where(iota((CROSS, 1), 0) < live_ref[0], 1.0, 0.0)
-    resid = (base_ref[...] - attitude_term(att_ref, masked, by_lane_ref)) * used
-    resid_ref[...] = resid
-    send_normal(src_ref, resid, by_source_ref[...], (plain_ref, up_ref, down_ref))
-    ghosts = dot(choose_ref[...], jnp.concatenate(halves(resid), 1))
-    ghosts = ghosts[:, 0:128] + ghosts[:, 128:256]
+        masked.append(jnp.where(mine, whole[0:128], 0.0))
+        ghost_masked.append(jnp.where(ghost_mine, whole[128:136], 0.0))
+        masked_ref[128 * a : 128 * a + 128, :] = masked[a]
+    rhs = rhs_in_ref[...] - products_sum(products_ref, masked)
+    rhs_ref[...] = rhs
+    send_normal(rhs, by_source_ref[...], (plain_ref, up_ref, down_ref))
+    ghost_att = [ghost_ref[8 * a : 8 * a + 8, :] for a in range(3)]
+    ghosts = ghost_ref[24:32, :] - attitude_term(ghost_att, ghost_masked, by_lane_ref)
     up_ref[HEAD : HEAD + 40, :] = up_in_ref[...]
     down_ref[HEAD : HEAD + 40, :] = down_in_ref[...]
     up_ref[HEAD + 32 : HEAD + 36, :] = ghosts[0:4]
@@ -286,31 +330,50 @@
     down_ref[HEAD + 40 : HEAD + 48, :] = jnp.concatenate([initial, empty], 0)
 
 
+def beside_kernel(
+    live_ref, masked_ref, resid_in_ref, att_ref, by_lane_ref, by_row_ref, grads_ref, *rest
+):
+    masked = [masked_ref[128 * a : 128 * a + 128, :] for a in range(3)]
+    used = jnp.where(iota((CROSS, 1), 0) < live_ref[0], 1.0, 0.0)
+    resid = resid_in_ref[...] - attitude_term(att_ref, masked, by_lane_ref) * used
+    grads_ref[...] = gradients(att_ref, resid, by_row_ref)
+    for ref in rest:
+        ref[...] = resid
+
+
 def middle_kernel(
-    live_ref, got_ref, resid_in_ref, att_ref, src_ref, cols_ref, peers_ref, by_source_ref,
-    by_lane_ref, choose_ref, resid_ref, send_ref,
+    got_ref, resid_ref, rhs_in_ref, cols_ref, peers_ref, by_source_ref, by_lane_ref, choose_ref,
+    ghost_ref, products_ref, masked_ref, send_ref,
 ):
     found = split_dot(peers_ref[...], jnp.concatenate([got_ref[:, 0, :], got_ref[:, 1, :]], 1))
-    front, back = found[:, 0:128], found[:, 128:256]
-    group, cc = iota((128, 128), 1) >> 4, column(cols_ref, 3)
+    group = iota((136, 128), 1) >> 4
+    cc = jnp.concatenate([column(cols_ref, 3), iota((8, 1), 0) & 3], 0)
+    front, back = found[0:136, 0:128], found[0:136, 128:256]
     masked = [
         jnp.where(group == cc, front, 0.0),
         jnp.where(group == cc + 4, front, 0.0),
         jnp.where(group == cc, back, 0.0),
     ]
-    used = jnp.where(iota((CROSS, 1), 0) < live_ref[0], 1.0, 0.0)
-    resid = resid_in_ref[...] - attitude_term(att_ref, masked, by_lane_ref) * used
-    resid_ref[...] = resid
-    send_normal(src_ref, resid, by_source_ref[...], (send_ref,))
-    ghosts = dot(choose_ref[...], jnp.concatenate(halves(resid), 1))
-    send_ref[HEAD : HEAD + 8, :] = ghosts[:, 0:128] + ghosts[:, 128:256]
+    for a in range(3):
+        masked_ref[128 * a : 128 * a + 128, :] = masked[a][0:128]
+    rhs = rhs_in_ref[...] - products_sum(products_ref, [m[0:128] for m in masked])
+    send_normal(rhs, by_source_ref[...], (send_ref,))
+    ghost_att = [ghost_ref[8 * a : 8 * a + 8, :] for a in range(3)]
+    term = attitude_term(ghost_att, [m[128:136] for m in masked], by_lane_ref)
+    ghosts = dot(choose_ref[...], jnp.concatenate(halves(resid_ref[...]), 1))
+    send_ref[HEAD : HEAD + 8, :] = ghosts[:, 0:128] + ghosts[:, 128:256] - term
 
 
 def return_kernel(
     live_ref, tm_ref, across_ref, own_ref, below_ref, above_ref, up_ref, down_ref, inverses_ref,
-    sources_in_ref, resid_in_ref, att_ref, src_ref, cols_ref, by_source_ref, by_row_ref, pack_ref,
-    index_ref, out_ref, sources_ref, *rest, second,
+    sources_in_ref, grads_ref, products_ref, cols_ref, by_source_ref, by_row_ref, pack_ref,
+    *rest, second,
 ):
+    if second:
+        out_ref, sources_ref = rest[:2]
+    else:
+        index_ref, resid_in_ref, src_ref, normals_ref, rhs_in_ref = rest[:5]
+        out_ref, sources_ref, resid_ref, rhs_ref = rest[5:9]
     tm, total_ref = tm_ref[0], rest[-1]
     total_ref[...] = (
         own_ref[0:HEAD, :] + across_ref[0:HEAD, :] + below_ref[0:HEAD, :] + above_ref[0:HEAD, :]
@@ -335,33 +398,38 @@
     ghost_onehot = jnp.where(iota((8, SRC_N), 1) == ghost_slot, 1.0, 0.0)
     values = gather_source(step, by_source_ref[...])
     ghost_values = gather_source(step, ghost_onehot)
-    change = jnp.zeros((CROSS, ROWS), F32)
     ghost_change = jnp.zeros((8, ROWS), F32)
     for p in range(5):
-        change = change + src_ref[p].astype(F32) * values[p]
         ghost_change = ghost_change + item(3 + p) * ghost_values[p]
-    used = jnp.where(iota((CROSS, 1), 0) < live_ref[0], 1.0, 0.0)
-    resid = resid_in_ref[...] - used * change
-    if not second:
-        rest[0][...] = resid
     if second:
         ghost_resid = jnp.concatenate(
             [below_ref[HEAD : HEAD + 4, :], above_ref[HEAD + 4 : HEAD + 8, :]], 0
         )
     else:
         ghost_resid = item(8)
+        used = jnp.where(iota((CROSS, 1), 0) < live_ref[0], 1.0, 0.0)
+        change = jnp.zeros((CROSS, ROWS), F32)
+        rhs = rhs_in_ref[...]
+        for p in range(5):
+            change = change + src_ref[p].astype(F32) * values[p]
+            rhs = rhs - normals_ref[128 * p : 128 * p + 128, :] * values[p]
+        resid_ref[...] = resid_in_ref[...] - used * change
+        rhs_ref[...] = rhs
     ghost_resid = (ghost_resid - ghost_change) * there
-    rows = [att_ref[a].astype(F32) * resid for a in range(3)]
-    rows += [item(a) * ghost_resid for a in range(3)]
-    high, low = halves(jnp.concatenate(rows, 0))
-    grads = dot(jnp.concatenate([high, low, high], 1), by_row_ref[...])
+    ghost_grads = gradients([item(a) for a in range(3)], ghost_resid, by_row_ref)
+    parts = []
+    for a in range(3):
+        part = grads_ref[128 * a : 128 * a + 128, :]
+        for p in range(5):
+            low_row = 128 * (3 * p + a)
+            part = part - products_ref[low_row : low_row + 128, :] * values[p]
+        parts.append(part)
     lbc, cc = column(cols_ref, 1), column(cols_ref, 3)
     group = iota((128, 128), 1) >> 4
     edge_group = jnp.where(lbc <= 1, lbc, lbc - 24)
     own = group == cc + 2
     edge = group == edge_group
-    whole = jnp.concatenate([grads[128 * a : 128 * a + 128] for a in range(3)], 1)
-    high, low = halves(whole)
+    high, low = halves(jnp.concatenate(parts, 1))
     own3, edge3 = jnp.concatenate([own] * 3, 1), jnp.concatenate([edge] * 3, 1)
     none = jnp.zeros_like(high)
     table = [jnp.where(mask, part, none) for part in (high, low) for mask in (own3, edge3)]
@@ -370,7 +438,7 @@
     ghost_group = iota((8, 128), 1) >> 4
     ghost_own = ghost_group == jnp.where(ghost8[:, 0:1] < 4, ghost_block - 24, ghost_block)
     for a in range(3):
-        ghost = jnp.where(ghost_own, grads[384 + 8 * a : 392 + 8 * a], 0.0)
+        ghost = jnp.where(ghost_own, ghost_grads[8 * a : 8 * a + 8], 0.0)
         from_below = jnp.sum(jnp.where(ghost8 < 4, ghost, 0.0), axis=0, keepdims=True)
         from_above = jnp.sum(jnp.where(ghost8 >= 4, ghost, 0.0), axis=0, keepdims=True)
         block = packed[:, 128 * a : 128 * a + 128]
@@ -561,53 +629,59 @@
     near = lax.all_to_all(dense, ("x", "z"), 0, 0, tiled=True)
     (
         cols, places, by_source, base, by_lane, by_row, pack, index, peers, choose, up, down, wide,
-        offsets,
+        ghost, products, normals, rhs, held, offsets,
     ) = run_kernel(
         prepare_kernel, 3,
         [
-            (128, 128), half(128, 256), half(128, SRC_N), (CROSS, ROWS), half(384, 128),
-            half(384, 128), half(SKY_N, 512), (SKY_N, 128), half(128, 128), (8, 128), (40, 128),
-            (40, 128), (32, RUN), jax.ShapeDtypeStruct((3,), I32),
+            (128, 128), half(144, 256), half(128, SRC_N), (CROSS, ROWS), half(384, 128),
+            half(384, 128), half(SKY_N, 512), (SKY_N, 128), half(144, 128), (8, 128), (40, 128),
+            (40, 128), (32, RUN), (40, 128), (1920, 128), (640, 128), (128, 128),
+            (3, 4, 128), jax.ShapeDtypeStruct((3,), I32),
         ],
         live_count, core, band_offsets, observed, att_partials, src_partials, slot, kb, sources, bands, extra,
+        knots,
     )
     near, cols = lax.optimization_barrier((near, cols))
     far = lax.ppermute(near, "c", [(0, 1), (1, 0)])
-    resid, plain, up, down, sides = run_kernel(
-        first_kernel, 3,
-        [(CROSS, ROWS), (HEAD, 128), (HEAD + 48, 128), (HEAD + 48, 128), (8, 128)],
-        live_count, core, chip, near, far, att_partials, src_partials, cols, places, by_source,
-        base, by_lane, choose, up, down,
+    masked, rhs, plain, up, down, sides = run_kernel(
+        first_kernel, 2,
+        [(384, 128), (128, 128), (HEAD, 128), (HEAD + 48, 128), (HEAD + 48, 128), (8, 128)],
+        core, chip, near, far, cols, places, by_source, by_lane, up, down, ghost, products, rhs,
     )
     across = lax.ppermute(plain, "tm", shifts(2))
     up = lax.ppermute(up, "tm", shifts(1))
     down = lax.ppermute(down, "tm", shifts(-1))
-    back_shapes = [(SKY_N, 4, 128), (5, SRC_N)]
-    outgoing, sources, resid = run_kernel(
-        return_kernel, 2, [*back_shapes, (CROSS, ROWS)],
-        live_count, tm, across, plain, up, down, up, down, inverses, sources, resid,
-        att_partials, src_partials, cols, by_source, by_row, pack, index,
+    grads, resid = run_kernel(
+        beside_kernel, 1, [(384, 128), (CROSS, ROWS)],
+        live_count, masked, base, att_partials, by_lane, by_row,
+    )
+    outgoing, sources, resid, rhs = run_kernel(
+        return_kernel, 2, [(SKY_N, 4, 128), (5, SRC_N), (CROSS, ROWS), (128, 128)],
+        live_count, tm, across, plain, up, down, up, down, inverses, sources, grads, products,
+        cols, by_source, by_row, pack, index, resid, src_partials, normals, rhs,
         scratch=[(HEAD, 128)], second=False,
     )
     got = lax.all_to_all(outgoing, SKY, 0, 0, tiled=True)
     knots, served, pick, rims = run_kernel(
         smooth_kernel, 4, [(3, 4, 128), (SKY_N, 2, 128), half(128, 128), (32, 128)],
-        offsets, chip, core, tm, got, knots, wide, sides, up, down, choose, last=False,
+        offsets, chip, core, tm, got, held, wide, sides, up, down, choose, last=False,
     )
     arrived = lax.all_to_all(served, SKY, 0, 0, tiled=True)
-    resid, mine = run_kernel(
-        middle_kernel, 1, [(CROSS, ROWS), (HEAD + 8, 128)],
-        live_count, arrived, resid, att_partials, src_partials, cols, peers, by_source, by_lane,
-        choose,
+    masked, mine = run_kernel(
+        middle_kernel, 0, [(384, 128), (HEAD + 8, 128)],
+        arrived, resid, rhs, cols, peers, by_source, by_lane, choose, ghost, products,
     )
     across = lax.ppermute(mine, "tm", shifts(2))
     below = lax.ppermute(mine, "tm", shifts(1))
     above = lax.ppermute(mine, "tm", shifts(-1))
+    (grads,) = run_kernel(
+        beside_kernel, 1, [(384, 128)],
+        live_count, masked, resid, att_partials, by_lane, by_row,
+    )
     outgoing, step = run_kernel(
-        return_kernel, 2, back_shapes,
-        live_count, tm, across, mine, below, above, up, down, inverses, sources, resid,
-        att_partials, src_partials, cols, by_source, by_row, pack, index,
-        scratch=[(HEAD, 128)], second=True,
+        return_kernel, 2, [(SKY_N, 4, 128), (5, SRC_N)],
+        live_count, tm, across, mine, below, above, up, down, inverses, sources, grads, products,
+        cols, by_source, by_row, pack, scratch=[(HEAD, 128)], second=True,
     )
     got = lax.all_to_all(outgoing, SKY, 0, 0, tiled=True)
     knots, sources = run_kernel(

time: 95.8 us -> 95.1 us (level)
  waiting for transfers between devices: 13.1 us -> 11.5 us
    pallas_call x7 -> x9, Pallas kernels: 8.24 us -> 9.18 us  [run_kernel(): pl.pallas_call(kernel, out_shape=shapes, in_specs=specs, out_specs=[pl.Bl...]
  transfers between devices with their start and end apart: 8 -> 8, of which waited for: 5 -> 5; matrix products, arithmetic and copies ran while one was open for 0% -> 0% of each run, Pallas kernels for 2% -> 3%
where the time goes in v5:
time: 95.1 us; the launch traced here: 94.7 us
  blocking collectives  46.9 us (49%)
  starting transfers between devices  23.4 us (25%)
  waiting for transfers between devices  11.5 us (12%)
  Pallas kernels  10.7 us (11%)
  between operations  1.53 us (2%)
    all_to_all x2, blocking collectives, per_device(): got = lax.all_to_all(outgoing, SKY, 0, 0, tiled=True)  32.4 us
    all_to_all x1, blocking collectives, per_device(): arrived = lax.all_to_all(served, SKY, 0, 0, tiled=True)  14.5 us
    all_to_all x1, starting transfers between devices, per_device(): near = lax.all_to_all(dense, ('x', 'z'), 0, 0, tiled=True)  12 us
    pallas_call x9, Pallas kernels, run_kernel(): pl.pallas_call(kernel, out_shape=shapes, in_specs=specs, out_specs=[pl.Bl...  9.18 us
    all_to_all x1, waiting for transfers between devices, per_device(): near = lax.all_to_all(dense, ('x', 'z'), 0, 0, tiled=True)  6.08 us
    ppermute x1, starting transfers between devices, per_device(): far = lax.ppermute(near, 'c', [(0, 1), (1, 0)])  3.72 us
    ppermute x1, waiting for transfers between devices, per_device(): across = lax.ppermute(plain, 'tm', shifts(2))  2.11 us
  transfers between devices with their start and end apart: 8, of which 5 were waited for; matrix products, arithmetic and copies ran while one was open for 0% of the time, Pallas kernels for 3%

profile of v5, /device:TPU:1, one launch (start us, length us, event | category | flops | bytes accessed | tf_op | source)
XLA Modules:
  0.0 94.7 jit_solution(15135001258820152640)
XLA Ops:
  0.6 1.5 %shard_map.132 = f32[32,4,4,128]{3,2,1,0:T(4,128)} custom-call(f32[3,4,128]{2,1,0:T(4,128)} %bitcast.13, f32[3,3,4,128]{3,2,1,0:T(4,128)} %bitcast.9, f32[3,4,128]{2,1,0:T(4,128)} %bitcast.11), custom_call_target="tpu_custom_call" | custom-call | tf_op jit(solution)/shard_map/pallas_call | solution.py:616
  2.2 0.0 copy-start
  2.2 0.0 copy-start.2
  2.2 0.0 copy-start.3
  2.2 0.0 copy-start.4
  2.2 0.0 copy-start.5
  2.2 0.0 copy-start.10
  2.2 12.0 %all-to-all-start = ((f32[32,4,4,128]{3,2,1,0:T(4,128)}), f32[32,4,4,128]{3,2,1,0:T(4,128)S(1)}, u32[]{:S(2)}, u32[]{:S(2)}) async-start(f32[32,4,4,128]{3,2,1,0:T(4,128)} %shard_map.132), calls=%async_computation | async-start | bytes 524288 | tf_op jit(solution)/shard_map/all_to_all | solution.py:629
  14.3 0.0 copy-start.7
  14.3 0.0 copy-start.6
  15.0 0.0 copy-start.8
  15.0 0.0 copy-start.9
  15.0 0.0 copy-done
  15.0 0.0 copy-done.2
  15.0 0.0 copy-done.3
  15.0 0.0 copy-done.4
  15.0 0.0 copy-done.5
  15.0 0.0 copy-done.10
  15.0 0.0 copy-done.7
  15.1 0.6 copy-done.8
  15.6 0.0 copy-done.9
  15.6 2.2 %shard_map.131 = (f32[128,128]{1,0:T(8,128)S(1)}, bf16[144,256]{1,0:T(8,128)(2,1)S(1)}, bf16[128,1024]{1,0:T(8,128)(2,1)S(1)}, f32[128,128]{1,0:T(8,128)S(1)}, b...) custom-call(s32[1]{0:T(128)S(6)} %copy.16.refs_0_, ...), custom_call_target="tpu_custom_call" | custom-call | flops 10000000 | bytes 2000000 | tf_op jit(solution)/shard_map/pallas_call | solution.py:572
  17.9 6.1 %all-to-all-done.refs_2_ = f32[32,4,4,128]{3,2,1,0:T(4,128)S(1)} async-done(((f32[32,4,4,128]{3,2,1,0:T(4,128)}), f32[32,4,4,128]{3,2,1,0:T(4,128)S(1)}, u32[]{:S(2)}, u32[]{:S(2)}) %all-to-all-start) | async-done | bytes 262176 | tf_op jit(solution)/shard_map/all_to_all | solution.py:629
  24.0 3.7 %collective-permute-start = (f32[32,4,4,128]{3,2,1,0:T(4,128)S(1)}, f32[32,4,4,128]{3,2,1,0:T(4,128)S(1)}, u32[]{:S(2)}, u32[]{:S(2)}) collective-permute-start(f32[32,4,4,128]{3,2,1,0:T(4,128)S(1)} %all-to-all-done.refs_2_), channel_id=1, source_target_pairs={{0,4},{4,0},{1,5},{5,1},{2,6},{6,2},{3,7},{7,3},{8,12},{12,8},{9,1... | collective-permute-start | bytes 786440 | tf_op jit(solution)/shard_map/ppermute | solution.py:645
  27.7 1.2 %collective-permute-done.refs_3_ = f32[32,4,4,128]{3,2,1,0:T(4,128)S(1)} collective-permute-done((f32[32,4,4,128]{3,2,1,0:T(4,128)S(1)}, f32[32,4,4,128]{3,2,1,0:T(4,128)S(1)}, u32[]{:S(2)}, u32[]{:S(2)}) %collective-permute-start) | collective-permute-done | bytes 262176 | tf_op jit(solution)/shard_map/ppermute | solution.py:645
  28.8 0.8 shard_map.133
  29.6 1.4 %collective-permute-start.2 = (f32[88,128]{1,0:T(8,128)S(1)}, f32[88,128]{1,0:T(8,128)S(1)}, u32[]{:S(2)}, u32[]{:S(2)}) collective-permute-start(f32[88,128]{1,0:T(8,128)S(1)} %get-tuple-element.58), channel_id=1, source_target_pairs={{0,1},{1,2},{2,3},{3,0},{4,5},{5,6},{6,7},{7,4},{8,9},{9,10},{10,1... | collective-permute-start | bytes 135176 | tf_op jit(solution)/shard_map/ppermute | solution.py:652
  31.0 1.5 %collective-permute-start.3 = (f32[88,128]{1,0:T(8,128)S(1)}, f32[88,128]{1,0:T(8,128)S(1)}, u32[]{:S(2)}, u32[]{:S(2)}) collective-permute-start(f32[88,128]{1,0:T(8,128)S(1)} %get-tuple-element.59), channel_id=1, source_target_pairs={{0,3},{1,0},{2,1},{3,2},{4,7},{5,4},{6,5},{7,6},{8,11},{9,8},{10,9... | collective-permute-start | bytes 135176 | tf_op jit(solution)/shard_map/ppermute | solution.py:653
  32.5 1.6 %collective-permute-start.1 = (f32[40,128]{1,0:T(8,128)S(1)}, f32[40,128]{1,0:T(8,128)S(1)}, u32[]{:S(2)}, u32[]{:S(2)}) collective-permute-start(f32[40,128]{1,0:T(8,128)S(1)} %get-tuple-element.57.refs_3_), channel_id=1, source_target_pairs={{0,2},{1,3},{2,0},{3,1},{4,6},{5,7},{6,4},{7,5},{8,10},{9,11},{10,... | collective-permute-start | bytes 61448 | tf_op jit(solution)/shard_map/ppermute | solution.py:651
  34.1 0.5 shard_map.134
  34.5 2.1 %collective-permute-done.1.refs_2_ = f32[40,128]{1,0:T(8,128)S(1)} collective-permute-done((f32[40,128]{1,0:T(8,128)S(1)}, f32[40,128]{1,0:T(8,128)S(1)}, u32[]{:S(2)}, u32[]{:S(2)}) %collective-permute-start.1) | collective-permute-done | bytes 20512 | tf_op jit(solution)/shard_map/ppermute | solution.py:651
  36.7 0.0 collective-permute-done.2.refs_4_.refs_6_.refs_8_
  36.7 0.0 collective-permute-done.3.refs_5_.refs_7_.refs_9_
  36.7 0.8 shard_map.135
  37.5 16.7 %all_to_all.20.refs_4_ = f32[64,4,128]{2,1,0:T(4,128)S(1)} all-to-all(f32[64,4,128]{2,1,0:T(4,128)S(1)} %get-tuple-element.69), channel_id=1, replica_groups=mesh['x'=4,'z'=8,'c'=2,'tm'=4] {'x','z','c'}, dimensions={0} | all-to-all | bytes 262144 | tf_op jit(solution)/shard_map/all_to_all | solution.py:664
  54.1 1.5 %shard_map.136 = (f32[3,4,128]{2,1,0:T(4,128)S(1)}, f32[64,2,128]{2,1,0:T(2,128)S(1)}, bf16[128,128]{1,0:T(8,128)(2,1)S(1)}, f32[32,128]{1,0:T(8,128)S(1)}) custom-call(s32[3]{0:T(128)S(1)} %get-tuple-element.45.refs_0_, s32[1]{0:T(128)} %bitcast.6.refs_1_, s32[1]{0:T(128)} %bitcast.refs_1_.refs_0_.refs_2_, s32[1]{0:T(128)} %bitcast.7.refs_1_.refs_3_, ...), custom_call_target="tpu_custom_call" | custom-call | flops 10000000 | bytes 2000000 | tf_op jit(solution)/shard_map/pallas_call | solution.py:572
  55.6 14.5 %all_to_all.21.refs_0_ = f32[64,2,128]{2,1,0:T(2,128)S(1)} all-to-all(f32[64,2,128]{2,1,0:T(2,128)S(1)} %get-tuple-element.74), channel_id=1, replica_groups=mesh['x'=4,'z'=8,'c'=2,'tm'=4] {'x','z','c'}, dimensions={0} | all-to-all | bytes 131072 | tf_op jit(solution)/shard_map/all_to_all | solution.py:669
  70.1 0.6 shard_map.137
  70.6 1.6 %collective-permute-start.6 = (f32[48,128]{1,0:T(8,128)S(1)}, f32[48,128]{1,0:T(8,128)S(1)}, u32[]{:S(2)}, u32[]{:S(2)}) collective-permute-start(f32[48,128]{1,0:T(8,128)S(1)} %get-tuple-element.78.refs_3_), channel_id=1, source_target_pairs={{0,3},{1,0},{2,1},{3,2},{4,7},{5,4},{6,5},{7,6},{8,11},{9,8},{10,9... | collective-permute-start | bytes 73736 | tf_op jit(solution)/shard_map/ppermute | solution.py:676
  72.2 0.0 collective-permute-start.5
  72.2 1.6 %collective-permute-start.4 = (f32[48,128]{1,0:T(8,128)S(1)}, f32[48,128]{1,0:T(8,128)S(1)}, u32[]{:S(2)}, u32[]{:S(2)}) collective-permute-start(f32[48,128]{1,0:T(8,128)S(1)} %get-tuple-element.78.refs_3_), channel_id=1, source_target_pairs={{0,2},{1,3},{2,0},{3,1},{4,6},{5,7},{6,4},{7,5},{8,10},{9,11},{10,... | collective-permute-start | bytes 73736 | tf_op jit(solution)/shard_map/ppermute | solution.py:674
  73.9 0.5 shard_map.138.refs_10_
  74.4 0.0 collective-permute-done.6.refs_5_
  74.4 1.8 %collective-permute-done.5.refs_4_ = f32[48,128]{1,0:T(8,128)S(1)} collective-permute-done((f32[48,128]{1,0:T(8,128)S(1)}, f32[48,128]{1,0:T(8,128)S(1)}, u32[]{:S(2)}, u32[]{:S(2)}) %collective-permute-start.5) | collective-permute-done | bytes 24608 | tf_op jit(solution)/shard_map/ppermute | solution.py:675
  76.1 0.4 collective-permute-done.4.refs_2_
  76.5 0.8 shard_map.139
  77.3 15.8 %all_to_all.22.refs_4_ = f32[64,4,128]{2,1,0:T(4,128)S(1)} all-to-all(f32[64,4,128]{2,1,0:T(4,128)S(1)} %get-tuple-element.81), channel_id=1, replica_groups=mesh['x'=4,'z'=8,'c'=2,'tm'=4] {'x','z','c'}, dimensions={0} | all-to-all | bytes 262144 | tf_op jit(solution)/shard_map/all_to_all | solution.py:686
  93.1 1.7 %shard_map.140 = (f32[3,4,128]{2,1,0:T(4,128)}, f32[5,1024]{1,0:T(8,128)}) custom-call(s32[3]{0:T(128)S(1)} %get-tuple-element.45.refs_0_, s32[1]{0:T(128)} %bitcast.6.refs_1_, s32[1]{0:T(128)} %bitcast.refs_1_.refs_0_.refs_2_, s32[1]{0:T(128)} %bitcast.7.refs_1_.refs_3_, f32[64,4,128]{2,1,0:T(4,128)S(1)} %all_to_all.22.refs_4_, ...), custom_call_target="tpu_custom_call" | custom-call | flops 10000000 | bytes 2000000 | tf_op jit(solution)/shard_map/pallas_call | solution.py:572
  (3 shorter events, 0.0 us)
Async XLA Ops:
  2.2 12.8 %copy-start = (bf16[3,128,128]{2,1,0:T(8,128)(2,1)S(1)}, bf16[3,128,128]{2,1,0:T(8,128)(2,1)}, u32[]{:S(2)}) copy-start(bf16[3,128,128]{2,1,0:T(8,128)(2,1)} %refs_3_.5) | copy-start | bytes 294916
  2.2 12.8 %copy-start.2 = (bf16[5,128,128]{2,1,0:T(8,128)(2,1)S(1)}, bf16[5,128,128]{2,1,0:T(8,128)(2,1)}, u32[]{:S(2)}) copy-start(bf16[5,128,128]{2,1,0:T(8,128)(2,1)} %refs_18_.1) | copy-start | bytes 491524
  2.2 12.8 %copy-start.3 = (f32[5,1024]{1,0:T(8,128)S(1)}, f32[5,1024]{1,0:T(8,128)}, u32[]{:S(2)}) copy-start(f32[5,1024]{1,0:T(8,128)} %refs_9_.1) | copy-start | bytes 61444
  2.2 12.8 %copy-start.4 = (f32[3,3,1,512]{3,2,1,0:T(1,128)S(1)}, f32[3,3,1,512]{3,2,1,0:T(1,128)}, u32[]{:S(2)}) copy-start(f32[3,3,1,512]{3,2,1,0:T(1,128)} %param.21) | copy-start | bytes 55300
  2.2 12.8 %copy-start.5 = (f32[128,128]{1,0:T(8,128)S(1)}, f32[128,128]{1,0:T(8,128)}, u32[]{:S(2)}) copy-start(f32[128,128]{1,0:T(8,128)} %refs_3_.3) | copy-start | bytes 196612
  2.2 12.8 %copy-start.10 = (s32[128]{0:T(128)S(1)}, s32[128]{0:T(128)}, u32[]{:S(2)}) copy-start(s32[128]{0:T(128)} %param.16) | copy-start | bytes 1540
  2.2 21.7 %all-to-all-start = ((f32[32,4,4,128]{3,2,1,0:T(4,128)}), f32[32,4,4,128]{3,2,1,0:T(4,128)S(1)}, u32[]{:S(2)}, u32[]{:S(2)}) async-start(f32[32,4,4,128]{3,2,1,0:T(4,128)} %shard_map.132), calls=%async_computation | async-start | bytes 524288 | tf_op jit(solution)/shard_map/all_to_all | solution.py:629
  14.3 0.8 copy-start.7
  14.3 0.8 copy-start.6
  15.0 0.7 copy-start.8
  15.0 0.7 copy-start.9
  24.0 4.9 %collective-permute-start = (f32[32,4,4,128]{3,2,1,0:T(4,128)S(1)}, f32[32,4,4,128]{3,2,1,0:T(4,128)S(1)}, u32[]{:S(2)}, u32[]{:S(2)}) collective-permute-start(f32[32,4,4,128]{3,2,1,0:T(4,128)S(1)} %all-to-all-done.refs_2_), channel_id=1, source_target_pairs={{0,4},{4,0},{1,5},{5,1},{2,6},{6,2},{3,7},{7,3},{8,12},{12,8},{9,1... | collective-permute-start | bytes 786440 | tf_op jit(solution)/shard_map/ppermute | solution.py:645
  29.6 7.0 %collective-permute-start.2 = (f32[88,128]{1,0:T(8,128)S(1)}, f32[88,128]{1,0:T(8,128)S(1)}, u32[]{:S(2)}, u32[]{:S(2)}) collective-permute-start(f32[88,128]{1,0:T(8,128)S(1)} %get-tuple-element.58), channel_id=1, source_target_pairs={{0,1},{1,2},{2,3},{3,0},{4,5},{5,6},{6,7},{7,4},{8,9},{9,10},{10,1... | collective-permute-start | bytes 135176 | tf_op jit(solution)/shard_map/ppermute | solution.py:652
  31.0 5.7 %collective-permute-start.3 = (f32[88,128]{1,0:T(8,128)S(1)}, f32[88,128]{1,0:T(8,128)S(1)}, u32[]{:S(2)}, u32[]{:S(2)}) collective-permute-start(f32[88,128]{1,0:T(8,128)S(1)} %get-tuple-element.59), channel_id=1, source_target_pairs={{0,3},{1,0},{2,1},{3,2},{4,7},{5,4},{6,5},{7,6},{8,11},{9,8},{10,9... | collective-permute-start | bytes 135176 | tf_op jit(solution)/shard_map/ppermute | solution.py:653
  32.5 4.1 %collective-permute-start.1 = (f32[40,128]{1,0:T(8,128)S(1)}, f32[40,128]{1,0:T(8,128)S(1)}, u32[]{:S(2)}, u32[]{:S(2)}) collective-permute-start(f32[40,128]{1,0:T(8,128)S(1)} %get-tuple-element.57.refs_3_), channel_id=1, source_target_pairs={{0,2},{1,3},{2,0},{3,1},{4,6},{5,7},{6,4},{7,5},{8,10},{9,11},{10,... | collective-permute-start | bytes 61448 | tf_op jit(solution)/shard_map/ppermute | solution.py:651
  34.1 2.6 %copy-start.1 = (f32[5,5,1024]{2,1,0:T(8,128)S(1)}, f32[5,5,1024]{2,1,0:T(8,128)}, u32[]{:S(2)}) copy-start(f32[5,5,1024]{2,1,0:T(8,128)} %refs_8_.5) | copy-start | bytes 307204
  70.6 3.7 %collective-permute-start.6 = (f32[48,128]{1,0:T(8,128)S(1)}, f32[48,128]{1,0:T(8,128)S(1)}, u32[]{:S(2)}, u32[]{:S(2)}) collective-permute-start(f32[48,128]{1,0:T(8,128)S(1)} %get-tuple-element.78.refs_3_), channel_id=1, source_target_pairs={{0,3},{1,0},{2,1},{3,2},{4,7},{5,4},{6,5},{7,6},{8,11},{9,8},{10,9... | collective-permute-start | bytes 73736 | tf_op jit(solution)/shard_map/ppermute | solution.py:676
  72.2 3.9 %collective-permute-start.5 = (f32[48,128]{1,0:T(8,128)S(1)}, f32[48,128]{1,0:T(8,128)S(1)}, u32[]{:S(2)}, u32[]{:S(2)}) collective-permute-start(f32[48,128]{1,0:T(8,128)S(1)} %get-tuple-element.78.refs_3_), channel_id=1, source_target_pairs={{0,1},{1,2},{2,3},{3,0},{4,5},{5,6},{6,7},{7,4},{8,9},{9,10},{10,1... | collective-permute-start | bytes 73736 | tf_op jit(solution)/shard_map/ppermute | solution.py:675
  72.2 4.3 %collective-permute-start.4 = (f32[48,128]{1,0:T(8,128)S(1)}, f32[48,128]{1,0:T(8,128)S(1)}, u32[]{:S(2)}, u32[]{:S(2)}) collective-permute-start(f32[48,128]{1,0:T(8,128)S(1)} %get-tuple-element.78.refs_3_), channel_id=1, source_target_pairs={{0,2},{1,3},{2,0},{3,1},{4,6},{5,7},{6,4},{7,5},{8,10},{9,11},{10,... | collective-permute-start | bytes 73736 | tf_op jit(solution)/shard_map/ppermute | solution.py:674

commit v6 on v5

--- a/solution.py
+++ b/solution.py
@@ -444,8 +444,12 @@
         block = packed[:, 128 * a : 128 * a + 128]
         block = block + jnp.where(peer == 0, from_below, 0.0)
         block = block + jnp.where(peer == SKY_N - 1, from_above, 0.0)
-        out_ref[:, a, :] = block
-    out_ref[:, 3, :] = jnp.zeros((SKY_N, 128), F32) if second else index_ref[...]
+        if second:
+            out_ref[:, 0, 128 * a : 128 * a + 128] = block
+        else:
+            out_ref[:, a, :] = block
+    if not second:
+        out_ref[:, 3, :] = index_ref[...]
 
 
 def smooth_kernel(
@@ -479,7 +483,7 @@
             0,
         ).astype(BF16)
         outs[2][...] = pick
-    got = [got_ref[:, a, :] for a in range(3)]
+    got = [got_ref[:, 0, 128 * a : 128 * a + 128] if last else got_ref[:, a, :] for a in range(3)]
     summed = split_dot(pick, jnp.concatenate(got, 1))
     row128 = iota((128, 128), 0)
     group128 = iota((128, 128), 1) >> 4
@@ -679,7 +683,7 @@
         live_count, masked, resid, att_partials, by_lane, by_row,
     )
     outgoing, step = run_kernel(
-        return_kernel, 2, [(SKY_N, 4, 128), (5, SRC_N)],
+        return_kernel, 2, [(SKY_N, 1, 384), (5, SRC_N)],
         live_count, tm, across, mine, below, above, up, down, inverses, sources, grads, products,
         cols, by_source, by_row, pack, scratch=[(HEAD, 128)], second=True,
     )

time: 95.1 us -> 94.9 us (level)
  no operation moved by 1% of the time
where the time goes in v6:
time: 94.9 us; the launch traced here: 94.6 us
  blocking collectives  46.7 us (49%)
  starting transfers between devices  23.4 us (25%)
  waiting for transfers between devices  11.5 us (12%)
  Pallas kernels  10.7 us (11%)
  between operations  1.54 us (2%)
    all_to_all x2, blocking collectives, per_device(): got = lax.all_to_all(outgoing, SKY, 0, 0, tiled=True)  32.3 us
    all_to_all x1, blocking collectives, per_device(): arrived = lax.all_to_all(served, SKY, 0, 0, tiled=True)  14.5 us
    all_to_all x1, starting transfers between devices, per_device(): near = lax.all_to_all(dense, ('x', 'z'), 0, 0, tiled=True)  12 us
    pallas_call x9, Pallas kernels, run_kernel(): pl.pallas_call(kernel, out_shape=shapes, in_specs=specs, out_specs=[pl.Bl...  9.18 us
    all_to_all x1, waiting for transfers between devices, per_device(): near = lax.all_to_all(dense, ('x', 'z'), 0, 0, tiled=True)  6.08 us
    ppermute x1, starting transfers between devices, per_device(): far = lax.ppermute(near, 'c', [(0, 1), (1, 0)])  3.72 us
    ppermute x1, waiting for transfers between devices, per_device(): across = lax.ppermute(plain, 'tm', shifts(2))  2.11 us
  transfers between devices with their start and end apart: 8, of which 5 were waited for; matrix products, arithmetic and copies ran while one was open for 0% of the time, Pallas kernels for 3%

profile of v6, /device:TPU:1, one launch (start us, length us, event | category | flops | bytes accessed | tf_op | source)
XLA Modules:
  0.0 94.6 jit_solution(12752978594303944254)
XLA Ops:
  0.6 1.5 %shard_map.132 = f32[32,4,4,128]{3,2,1,0:T(4,128)} custom-call(f32[3,4,128]{2,1,0:T(4,128)} %bitcast.13, f32[3,3,4,128]{3,2,1,0:T(4,128)} %bitcast.9, f32[3,4,128]{2,1,0:T(4,128)} %bitcast.11), custom_call_target="tpu_custom_call" | custom-call | tf_op jit(solution)/shard_map/pallas_call | solution.py:620
  2.2 0.0 copy-start
  2.2 0.0 copy-start.2
  2.2 0.0 copy-start.3
  2.2 0.0 copy-start.4
  2.2 0.0 copy-start.5
  2.2 0.0 copy-start.10
  2.2 12.0 %all-to-all-start = ((f32[32,4,4,128]{3,2,1,0:T(4,128)}), f32[32,4,4,128]{3,2,1,0:T(4,128)S(1)}, u32[]{:S(2)}, u32[]{:S(2)}) async-start(f32[32,4,4,128]{3,2,1,0:T(4,128)} %shard_map.132), calls=%async_computation | async-start | bytes 524288 | tf_op jit(solution)/shard_map/all_to_all | solution.py:633
  14.3 0.0 copy-start.7
  14.3 0.0 copy-start.6
  15.0 0.0 copy-start.8
  15.0 0.0 copy-start.9
  15.0 0.0 copy-done
  15.0 0.0 copy-done.2
  15.0 0.0 copy-done.3
  15.0 0.0 copy-done.4
  15.0 0.0 copy-done.5
  15.0 0.0 copy-done.10
  15.0 0.0 copy-done.7
  15.1 0.6 copy-done.8
  15.6 0.0 copy-done.9
  15.6 2.2 %shard_map.131 = (f32[128,128]{1,0:T(8,128)S(1)}, bf16[144,256]{1,0:T(8,128)(2,1)S(1)}, bf16[128,1024]{1,0:T(8,128)(2,1)S(1)}, f32[128,128]{1,0:T(8,128)S(1)}, b...) custom-call(s32[1]{0:T(128)S(6)} %copy.16.refs_0_, ...), custom_call_target="tpu_custom_call" | custom-call | flops 10000000 | bytes 2000000 | tf_op jit(solution)/shard_map/pallas_call | solution.py:576
  17.9 6.1 %all-to-all-done.refs_2_ = f32[32,4,4,128]{3,2,1,0:T(4,128)S(1)} async-done(((f32[32,4,4,128]{3,2,1,0:T(4,128)}), f32[32,4,4,128]{3,2,1,0:T(4,128)S(1)}, u32[]{:S(2)}, u32[]{:S(2)}) %all-to-all-start) | async-done | bytes 262176 | tf_op jit(solution)/shard_map/all_to_all | solution.py:633
  24.0 3.7 %collective-permute-start = (f32[32,4,4,128]{3,2,1,0:T(4,128)S(1)}, f32[32,4,4,128]{3,2,1,0:T(4,128)S(1)}, u32[]{:S(2)}, u32[]{:S(2)}) collective-permute-start(f32[32,4,4,128]{3,2,1,0:T(4,128)S(1)} %all-to-all-done.refs_2_), channel_id=1, source_target_pairs={{0,4},{4,0},{1,5},{5,1},{2,6},{6,2},{3,7},{7,3},{8,12},{12,8},{9,1... | collective-permute-start | bytes 786440 | tf_op jit(solution)/shard_map/ppermute | solution.py:649
  27.7 1.2 %collective-permute-done.refs_3_ = f32[32,4,4,128]{3,2,1,0:T(4,128)S(1)} collective-permute-done((f32[32,4,4,128]{3,2,1,0:T(4,128)S(1)}, f32[32,4,4,128]{3,2,1,0:T(4,128)S(1)}, u32[]{:S(2)}, u32[]{:S(2)}) %collective-permute-start) | collective-permute-done | bytes 262176 | tf_op jit(solution)/shard_map/ppermute | solution.py:649
  28.8 0.8 shard_map.133
  29.6 1.4 %collective-permute-start.2 = (f32[88,128]{1,0:T(8,128)S(1)}, f32[88,128]{1,0:T(8,128)S(1)}, u32[]{:S(2)}, u32[]{:S(2)}) collective-permute-start(f32[88,128]{1,0:T(8,128)S(1)} %get-tuple-element.58), channel_id=1, source_target_pairs={{0,1},{1,2},{2,3},{3,0},{4,5},{5,6},{6,7},{7,4},{8,9},{9,10},{10,1... | collective-permute-start | bytes 135176 | tf_op jit(solution)/shard_map/ppermute | solution.py:656
  31.0 1.5 %collective-permute-start.3 = (f32[88,128]{1,0:T(8,128)S(1)}, f32[88,128]{1,0:T(8,128)S(1)}, u32[]{:S(2)}, u32[]{:S(2)}) collective-permute-start(f32[88,128]{1,0:T(8,128)S(1)} %get-tuple-element.59), channel_id=1, source_target_pairs={{0,3},{1,0},{2,1},{3,2},{4,7},{5,4},{6,5},{7,6},{8,11},{9,8},{10,9... | collective-permute-start | bytes 135176 | tf_op jit(solution)/shard_map/ppermute | solution.py:657
  32.5 1.6 %collective-permute-start.1 = (f32[40,128]{1,0:T(8,128)S(1)}, f32[40,128]{1,0:T(8,128)S(1)}, u32[]{:S(2)}, u32[]{:S(2)}) collective-permute-start(f32[40,128]{1,0:T(8,128)S(1)} %get-tuple-element.57.refs_3_), channel_id=1, source_target_pairs={{0,2},{1,3},{2,0},{3,1},{4,6},{5,7},{6,4},{7,5},{8,10},{9,11},{10,... | collective-permute-start | bytes 61448 | tf_op jit(solution)/shard_map/ppermute | solution.py:655
  34.1 0.5 shard_map.134
  34.5 2.1 %collective-permute-done.1.refs_2_ = f32[40,128]{1,0:T(8,128)S(1)} collective-permute-done((f32[40,128]{1,0:T(8,128)S(1)}, f32[40,128]{1,0:T(8,128)S(1)}, u32[]{:S(2)}, u32[]{:S(2)}) %collective-permute-start.1) | collective-permute-done | bytes 20512 | tf_op jit(solution)/shard_map/ppermute | solution.py:655
  36.7 0.0 collective-permute-done.2.refs_4_.refs_6_.refs_8_
  36.7 0.0 collective-permute-done.3.refs_5_.refs_7_.refs_9_
  36.7 0.8 shard_map.135
  37.5 16.7 %all_to_all.20.refs_4_ = f32[64,4,128]{2,1,0:T(4,128)S(1)} all-to-all(f32[64,4,128]{2,1,0:T(4,128)S(1)} %get-tuple-element.69), channel_id=1, replica_groups=mesh['x'=4,'z'=8,'c'=2,'tm'=4] {'x','z','c'}, dimensions={0} | all-to-all | bytes 262144 | tf_op jit(solution)/shard_map/all_to_all | solution.py:668
  54.1 1.5 %shard_map.136 = (f32[3,4,128]{2,1,0:T(4,128)S(1)}, f32[64,2,128]{2,1,0:T(2,128)S(1)}, bf16[128,128]{1,0:T(8,128)(2,1)S(1)}, f32[32,128]{1,0:T(8,128)S(1)}) custom-call(s32[3]{0:T(128)S(1)} %get-tuple-element.45.refs_0_, s32[1]{0:T(128)} %bitcast.6.refs_1_, s32[1]{0:T(128)} %bitcast.refs_1_.refs_0_.refs_2_, s32[1]{0:T(128)} %bitcast.7.refs_1_.refs_3_, ...), custom_call_target="tpu_custom_call" | custom-call | flops 10000000 | bytes 2000000 | tf_op jit(solution)/shard_map/pallas_call | solution.py:576
  55.6 14.5 %all_to_all.21.refs_0_ = f32[64,2,128]{2,1,0:T(2,128)S(1)} all-to-all(f32[64,2,128]{2,1,0:T(2,128)S(1)} %get-tuple-element.74), channel_id=1, replica_groups=mesh['x'=4,'z'=8,'c'=2,'tm'=4] {'x','z','c'}, dimensions={0} | all-to-all | bytes 131072 | tf_op jit(solution)/shard_map/all_to_all | solution.py:673
  70.1 0.6 shard_map.137
  70.6 1.6 %collective-permute-start.6 = (f32[48,128]{1,0:T(8,128)S(1)}, f32[48,128]{1,0:T(8,128)S(1)}, u32[]{:S(2)}, u32[]{:S(2)}) collective-permute-start(f32[48,128]{1,0:T(8,128)S(1)} %get-tuple-element.78.refs_3_), channel_id=1, source_target_pairs={{0,3},{1,0},{2,1},{3,2},{4,7},{5,4},{6,5},{7,6},{8,11},{9,8},{10,9... | collective-permute-start | bytes 73736 | tf_op jit(solution)/shard_map/ppermute | solution.py:680
  72.2 0.0 collective-permute-start.5
  72.2 1.6 %collective-permute-start.4 = (f32[48,128]{1,0:T(8,128)S(1)}, f32[48,128]{1,0:T(8,128)S(1)}, u32[]{:S(2)}, u32[]{:S(2)}) collective-permute-start(f32[48,128]{1,0:T(8,128)S(1)} %get-tuple-element.78.refs_3_), channel_id=1, source_target_pairs={{0,2},{1,3},{2,0},{3,1},{4,6},{5,7},{6,4},{7,5},{8,10},{9,11},{10,... | collective-permute-start | bytes 73736 | tf_op jit(solution)/shard_map/ppermute | solution.py:678
  73.9 0.5 shard_map.138.refs_10_
  74.4 0.0 collective-permute-done.6.refs_5_
  74.4 1.8 %collective-permute-done.5.refs_4_ = f32[48,128]{1,0:T(8,128)S(1)} collective-permute-done((f32[48,128]{1,0:T(8,128)S(1)}, f32[48,128]{1,0:T(8,128)S(1)}, u32[]{:S(2)}, u32[]{:S(2)}) %collective-permute-start.5) | collective-permute-done | bytes 24608 | tf_op jit(solution)/shard_map/ppermute | solution.py:679
  76.1 0.4 collective-permute-done.4.refs_2_
  76.5 0.8 shard_map.139
  77.3 15.6 %all_to_all.22.refs_4_ = f32[64,1,384]{2,1,0:T(1,128)S(1)} all-to-all(f32[64,1,384]{2,1,0:T(1,128)S(1)} %get-tuple-element.81), channel_id=1, replica_groups=mesh['x'=4,'z'=8,'c'=2,'tm'=4] {'x','z','c'}, dimensions={0} | all-to-all | bytes 196608 | tf_op jit(solution)/shard_map/all_to_all | solution.py:690
  92.9 1.7 %shard_map.140 = (f32[3,4,128]{2,1,0:T(4,128)}, f32[5,1024]{1,0:T(8,128)}) custom-call(s32[3]{0:T(128)S(1)} %get-tuple-element.45.refs_0_, s32[1]{0:T(128)} %bitcast.6.refs_1_, s32[1]{0:T(128)} %bitcast.refs_1_.refs_0_.refs_2_, s32[1]{0:T(128)} %bitcast.7.refs_1_.refs_3_, f32[64,1,384]{2,1,0:T(1,128)S(1)} %all_to_all.22.refs_4_, ...), custom_call_target="tpu_custom_call" | custom-call | flops 10000000 | bytes 2000000 | tf_op jit(solution)/shard_map/pallas_call | solution.py:576
  (3 shorter events, 0.0 us)
Async XLA Ops:
  2.2 12.8 %copy-start = (bf16[3,128,128]{2,1,0:T(8,128)(2,1)S(1)}, bf16[3,128,128]{2,1,0:T(8,128)(2,1)}, u32[]{:S(2)}) copy-start(bf16[3,128,128]{2,1,0:T(8,128)(2,1)} %refs_3_.5) | copy-start | bytes 294916
  2.2 12.8 %copy-start.2 = (bf16[5,128,128]{2,1,0:T(8,128)(2,1)S(1)}, bf16[5,128,128]{2,1,0:T(8,128)(2,1)}, u32[]{:S(2)}) copy-start(bf16[5,128,128]{2,1,0:T(8,128)(2,1)} %refs_18_.1) | copy-start | bytes 491524
  2.2 12.8 %copy-start.3 = (f32[5,1024]{1,0:T(8,128)S(1)}, f32[5,1024]{1,0:T(8,128)}, u32[]{:S(2)}) copy-start(f32[5,1024]{1,0:T(8,128)} %refs_9_.1) | copy-start | bytes 61444
  2.2 12.8 %copy-start.4 = (f32[3,3,1,512]{3,2,1,0:T(1,128)S(1)}, f32[3,3,1,512]{3,2,1,0:T(1,128)}, u32[]{:S(2)}) copy-start(f32[3,3,1,512]{3,2,1,0:T(1,128)} %param.21) | copy-start | bytes 55300
  2.2 12.8 %copy-start.5 = (f32[128,128]{1,0:T(8,128)S(1)}, f32[128,128]{1,0:T(8,128)}, u32[]{:S(2)}) copy-start(f32[128,128]{1,0:T(8,128)} %refs_3_.3) | copy-start | bytes 196612
  2.2 12.8 %copy-start.10 = (s32[128]{0:T(128)S(1)}, s32[128]{0:T(128)}, u32[]{:S(2)}) copy-start(s32[128]{0:T(128)} %param.16) | copy-start | bytes 1540
  2.2 21.7 %all-to-all-start = ((f32[32,4,4,128]{3,2,1,0:T(4,128)}), f32[32,4,4,128]{3,2,1,0:T(4,128)S(1)}, u32[]{:S(2)}, u32[]{:S(2)}) async-start(f32[32,4,4,128]{3,2,1,0:T(4,128)} %shard_map.132), calls=%async_computation | async-start | bytes 524288 | tf_op jit(solution)/shard_map/all_to_all | solution.py:633
  14.3 0.8 copy-start.7
  14.3 0.8 copy-start.6
  15.0 0.7 copy-start.8
  15.0 0.7 copy-start.9
  24.0 4.9 %collective-permute-start = (f32[32,4,4,128]{3,2,1,0:T(4,128)S(1)}, f32[32,4,4,128]{3,2,1,0:T(4,128)S(1)}, u32[]{:S(2)}, u32[]{:S(2)}) collective-permute-start(f32[32,4,4,128]{3,2,1,0:T(4,128)S(1)} %all-to-all-done.refs_2_), channel_id=1, source_target_pairs={{0,4},{4,0},{1,5},{5,1},{2,6},{6,2},{3,7},{7,3},{8,12},{12,8},{9,1... | collective-permute-start | bytes 786440 | tf_op jit(solution)/shard_map/ppermute | solution.py:649
  29.6 7.0 %collective-permute-start.2 = (f32[88,128]{1,0:T(8,128)S(1)}, f32[88,128]{1,0:T(8,128)S(1)}, u32[]{:S(2)}, u32[]{:S(2)}) collective-permute-start(f32[88,128]{1,0:T(8,128)S(1)} %get-tuple-element.58), channel_id=1, source_target_pairs={{0,1},{1,2},{2,3},{3,0},{4,5},{5,6},{6,7},{7,4},{8,9},{9,10},{10,1... | collective-permute-start | bytes 135176 | tf_op jit(solution)/shard_map/ppermute | solution.py:656
  31.0 5.7 %collective-permute-start.3 = (f32[88,128]{1,0:T(8,128)S(1)}, f32[88,128]{1,0:T(8,128)S(1)}, u32[]{:S(2)}, u32[]{:S(2)}) collective-permute-start(f32[88,128]{1,0:T(8,128)S(1)} %get-tuple-element.59), channel_id=1, source_target_pairs={{0,3},{1,0},{2,1},{3,2},{4,7},{5,4},{6,5},{7,6},{8,11},{9,8},{10,9... | collective-permute-start | bytes 135176 | tf_op jit(solution)/shard_map/ppermute | solution.py:657
  32.5 4.1 %collective-permute-start.1 = (f32[40,128]{1,0:T(8,128)S(1)}, f32[40,128]{1,0:T(8,128)S(1)}, u32[]{:S(2)}, u32[]{:S(2)}) collective-permute-start(f32[40,128]{1,0:T(8,128)S(1)} %get-tuple-element.57.refs_3_), channel_id=1, source_target_pairs={{0,2},{1,3},{2,0},{3,1},{4,6},{5,7},{6,4},{7,5},{8,10},{9,11},{10,... | collective-permute-start | bytes 61448 | tf_op jit(solution)/shard_map/ppermute | solution.py:655
  34.1 2.6 %copy-start.1 = (f32[5,5,1024]{2,1,0:T(8,128)S(1)}, f32[5,5,1024]{2,1,0:T(8,128)}, u32[]{:S(2)}) copy-start(f32[5,5,1024]{2,1,0:T(8,128)} %refs_8_.5) | copy-start | bytes 307204
  70.6 3.7 %collective-permute-start.6 = (f32[48,128]{1,0:T(8,128)S(1)}, f32[48,128]{1,0:T(8,128)S(1)}, u32[]{:S(2)}, u32[]{:S(2)}) collective-permute-start(f32[48,128]{1,0:T(8,128)S(1)} %get-tuple-element.78.refs_3_), channel_id=1, source_target_pairs={{0,3},{1,0},{2,1},{3,2},{4,7},{5,4},{6,5},{7,6},{8,11},{9,8},{10,9... | collective-permute-start | bytes 73736 | tf_op jit(solution)/shard_map/ppermute | solution.py:680
  72.2 3.9 %collective-permute-start.5 = (f32[48,128]{1,0:T(8,128)S(1)}, f32[48,128]{1,0:T(8,128)S(1)}, u32[]{:S(2)}, u32[]{:S(2)}) collective-permute-start(f32[48,128]{1,0:T(8,128)S(1)} %get-tuple-element.78.refs_3_), channel_id=1, source_target_pairs={{0,1},{1,2},{2,3},{3,0},{4,5},{5,6},{6,7},{7,4},{8,9},{9,10},{10,1... | collective-permute-start | bytes 73736 | tf_op jit(solution)/shard_map/ppermute | solution.py:679
  72.2 4.3 %collective-permute-start.4 = (f32[48,128]{1,0:T(8,128)S(1)}, f32[48,128]{1,0:T(8,128)S(1)}, u32[]{:S(2)}, u32[]{:S(2)}) collective-permute-start(f32[48,128]{1,0:T(8,128)S(1)} %get-tuple-element.78.refs_3_), channel_id=1, source_target_pairs={{0,2},{1,3},{2,0},{3,1},{4,6},{5,7},{6,4},{7,5},{8,10},{9,11},{10,... | collective-permute-start | bytes 73736 | tf_op jit(solution)/shard_map/ppermute | solution.py:678

commit v7 on v6

--- a/solution.py
+++ b/solution.py
@@ -292,7 +292,7 @@
 
 def first_kernel(
     core_ref, chip_ref, near_ref, far_ref, cols_ref, places_ref, by_source_ref, by_lane_ref,
-    up_in_ref, down_in_ref, ghost_ref, products_ref, rhs_in_ref,
+    ghost_ref, products_ref, rhs_in_ref,
     masked_ref, rhs_ref, plain_ref, up_ref, down_ref, sides_ref,
 ):
     tables = []
@@ -314,10 +314,8 @@
     send_normal(rhs, by_source_ref[...], (plain_ref, up_ref, down_ref))
     ghost_att = [ghost_ref[8 * a : 8 * a + 8, :] for a in range(3)]
     ghosts = ghost_ref[24:32, :] - attitude_term(ghost_att, ghost_masked, by_lane_ref)
-    up_ref[HEAD : HEAD + 40, :] = up_in_ref[...]
-    down_ref[HEAD : HEAD + 40, :] = down_in_ref[...]
-    up_ref[HEAD + 32 : HEAD + 36, :] = ghosts[0:4]
-    down_ref[HEAD + 32 : HEAD + 36, :] = ghosts[4:8]
+    up_ref[HEAD : HEAD + 8, :] = ghosts
+    down_ref[HEAD : HEAD + 8, :] = ghosts
     core, chip = core_ref[0], chip_ref[0]
     before = jnp.where(core == 0, jnp.maximum(chip - 1, 0), chip)
     after = jnp.where(core == 0, chip, jnp.minimum(chip + 1, CHIPS - 1))
@@ -326,8 +324,8 @@
     empty = jnp.zeros((4, 128), F32)
     final = jnp.where(core == 1, near_ref[CHIPS - 1, 3], far_ref[CHIPS - 1, 3])
     initial = jnp.where(core == 0, near_ref[0, 3], far_ref[0, 3])
-    up_ref[HEAD + 40 : HEAD + 48, :] = jnp.concatenate([final, empty], 0)
-    down_ref[HEAD + 40 : HEAD + 48, :] = jnp.concatenate([initial, empty], 0)
+    up_ref[HEAD + 8 : HEAD + 16, :] = jnp.concatenate([final, empty], 0)
+    down_ref[HEAD + 8 : HEAD + 16, :] = jnp.concatenate([initial, empty], 0)
 
 
 def beside_kernel(
@@ -389,7 +387,7 @@
     there = jnp.where(ghost8 < 4, jnp.where(tm > 0, 1.0, 0.0), jnp.where(tm < TM_N - 1, 1.0, 0.0))
 
     def item(i):
-        row = HEAD + 4 * i
+        row = 4 * i
         return jnp.concatenate([up_ref[row : row + 4, :], down_ref[row : row + 4, :]], 0)
 
     facts = item(9)
@@ -401,12 +399,10 @@
     ghost_change = jnp.zeros((8, ROWS), F32)
     for p in range(5):
         ghost_change = ghost_change + item(3 + p) * ghost_values[p]
-    if second:
-        ghost_resid = jnp.concatenate(
-            [below_ref[HEAD : HEAD + 4, :], above_ref[HEAD + 4 : HEAD + 8, :]], 0
-        )
-    else:
-        ghost_resid = item(8)
+    ghost_resid = jnp.concatenate(
+        [below_ref[HEAD : HEAD + 4, :], above_ref[HEAD + 4 : HEAD + 8, :]], 0
+    )
+    if not second:
         used = jnp.where(iota((CROSS, 1), 0) < live_ref[0], 1.0, 0.0)
         change = jnp.zeros((CROSS, ROWS), F32)
         rhs = rhs_in_ref[...]
@@ -465,8 +461,8 @@
     else:
         sides_ref, up_ref, down_ref = one_ref, two_ref, three_ref
         place, tm = chip_ref[0] * 2 + core_ref[0], tm_ref[0]
-        below = jnp.where(tm > 0, up_ref[HEAD + 40 : HEAD + 44, :], 0.0)
-        above = jnp.where(tm < TM_N - 1, down_ref[HEAD + 40 : HEAD + 44, :], 0.0)
+        below = jnp.where(tm > 0, up_ref[HEAD + 8 : HEAD + 12, :], 0.0)
+        above = jnp.where(tm < TM_N - 1, down_ref[HEAD + 8 : HEAD + 12, :], 0.0)
         before = jnp.where(place == 0, below, sides_ref[0:4, :])
         after = jnp.where(place == SKY_N - 1, above, sides_ref[4:8, :])
         rims = rim_tiles(before, after)
@@ -645,12 +641,16 @@
         live_count, core, band_offsets, observed, att_partials, src_partials, slot, kb, sources, bands, extra,
         knots,
     )
-    near, cols = lax.optimization_barrier((near, cols))
+    ghosts_below = lax.ppermute(up, "tm", shifts(1))
+    ghosts_above = lax.ppermute(down, "tm", shifts(-1))
+    near, cols, ghosts_below, ghosts_above = lax.optimization_barrier(
+        (near, cols, ghosts_below, ghosts_above)
+    )
     far = lax.ppermute(near, "c", [(0, 1), (1, 0)])
     masked, rhs, plain, up, down, sides = run_kernel(
         first_kernel, 2,
-        [(384, 128), (128, 128), (HEAD, 128), (HEAD + 48, 128), (HEAD + 48, 128), (8, 128)],
-        core, chip, near, far, cols, places, by_source, by_lane, up, down, ghost, products, rhs,
+        [(384, 128), (128, 128), (HEAD, 128), (HEAD + 16, 128), (HEAD + 16, 128), (8, 128)],
+        core, chip, near, far, cols, places, by_source, by_lane, ghost, products, rhs,
     )
     across = lax.ppermute(plain, "tm", shifts(2))
     up = lax.ppermute(up, "tm", shifts(1))
@@ -661,7 +661,7 @@
     )
     outgoing, sources, resid, rhs = run_kernel(
         return_kernel, 2, [(SKY_N, 4, 128), (5, SRC_N), (CROSS, ROWS), (128, 128)],
-        live_count, tm, across, plain, up, down, up, down, inverses, sources, grads, products,
+        live_count, tm, across, plain, up, down, ghosts_below, ghosts_above, inverses, sources, grads, products,
         cols, by_source, by_row, pack, index, resid, src_partials, normals, rhs,
         scratch=[(HEAD, 128)], second=False,
     )
@@ -684,7 +684,7 @@
     )
     outgoing, step = run_kernel(
         return_kernel, 2, [(SKY_N, 1, 384), (5, SRC_N)],
-        live_count, tm, across, mine, below, above, up, down, inverses, sources, grads, products,
+        live_count, tm, across, mine, below, above, ghosts_below, ghosts_above, inverses, sources, grads, products,
         cols, by_source, by_row, pack, scratch=[(HEAD, 128)], second=True,
     )
     got = lax.all_to_all(outgoing, SKY, 0, 0, tiled=True)

time: 94.9 us -> 97 us (1.022)
  waiting for transfers between devices: 11.5 us -> 8.71 us
  starting transfers between devices: 23.4 us -> 26 us
  blocking collectives: 46.7 us -> 48.9 us
    all_to_all x1, waiting for transfers between devices: 6.08 us -> 1.75 us  [per_device(): near = lax.all_to_all(dense, ('x', 'z'), 0, 0, tiled=True)]
    ppermute x0 -> x2, starting transfers between devices: none -> 2.9 us  [the longest x1 1.53 us: per_device(): ghosts_above = lax.ppermute(down, 'tm', shifts(-1))]
    all_to_all x2, blocking collectives: 32.3 us -> 34.4 us  [per_device(): got = lax.all_to_all(outgoing, SKY, 0, 0, tiled=True)]
    ppermute x0 -> x2, waiting for transfers between devices: none -> 1.4 us  [the longest x1 1.38 us: per_device(): ghosts_below = lax.ppermute(up, 'tm', shifts(1))]
  transfers between devices with their start and end apart: 8 -> 10, of which waited for: 5 -> 6; matrix products, arithmetic and copies ran while one was open for 0% -> 0% of each run, Pallas kernels for 3% -> 3%
where the time goes in v7:
time: 97 us; the launch traced here: 96.6 us
  blocking collectives  48.9 us (50%)
  starting transfers between devices  26 us (27%)
  Pallas kernels  10.8 us (11%)
  waiting for transfers between devices  8.71 us (9%)
  between operations  1.54 us (2%)
    all_to_all x2, blocking collectives, per_device(): got = lax.all_to_all(outgoing, SKY, 0, 0, tiled=True)  34.4 us
    all_to_all x1, blocking collectives, per_device(): arrived = lax.all_to_all(served, SKY, 0, 0, tiled=True)  14.5 us
    all_to_all x1, starting transfers between devices, per_device(): near = lax.all_to_all(dense, ('x', 'z'), 0, 0, tiled=True)  12 us
    pallas_call x9, Pallas kernels, run_kernel(): pl.pallas_call(kernel, out_shape=shapes, in_specs=specs, out_specs=[pl.Bl...  9.25 us
    ppermute x1, starting transfers between devices, per_device(): far = lax.ppermute(near, 'c', [(0, 1), (1, 0)])  3.72 us
    ppermute x1, waiting for transfers between devices, per_device(): across = lax.ppermute(plain, 'tm', shifts(2))  2.11 us
  transfers between devices with their start and end apart: 10, of which 6 were waited for; matrix products, arithmetic and copies ran while one was open for 0% of the time, Pallas kernels for 3%

profile of v7, /device:TPU:1, one launch (start us, length us, event | category | flops | bytes accessed | tf_op | source)
XLA Modules:
  0.0 96.6 jit_solution(5660189467445370451)
XLA Ops:
  0.6 1.5 %shard_map.132 = f32[32,4,4,128]{3,2,1,0:T(4,128)} custom-call(f32[3,4,128]{2,1,0:T(4,128)} %bitcast.13, f32[3,3,4,128]{3,2,1,0:T(4,128)} %bitcast.9, f32[3,4,128]{2,1,0:T(4,128)} %bitcast.11), custom_call_target="tpu_custom_call" | custom-call | tf_op jit(solution)/shard_map/pallas_call | solution.py:616
  2.2 0.0 copy-start
  2.2 0.0 copy-start.2
  2.2 0.0 copy-start.3
  2.2 0.0 copy-start.4
  2.2 0.0 copy-start.5
  2.2 0.0 copy-start.10
  2.3 12.0 %all-to-all-start = ((f32[32,4,4,128]{3,2,1,0:T(4,128)}), f32[32,4,4,128]{3,2,1,0:T(4,128)S(1)}, u32[]{:S(2)}, u32[]{:S(2)}) async-start(f32[32,4,4,128]{3,2,1,0:T(4,128)} %shard_map.132), calls=%async_computation | async-start | bytes 524288 | tf_op jit(solution)/shard_map/all_to_all | solution.py:629
  14.3 0.0 copy-start.7
  14.3 0.0 copy-start.6
  15.0 0.0 copy-start.8
  15.0 0.0 copy-start.9
  15.0 0.0 copy-done
  15.0 0.0 copy-done.2
  15.0 0.0 copy-done.3
  15.1 0.6 copy-done.8
  15.6 0.0 copy-done.9
  15.6 2.3 %shard_map.131 = (f32[128,128]{1,0:T(8,128)S(1)}, bf16[144,256]{1,0:T(8,128)(2,1)S(1)}, bf16[128,1024]{1,0:T(8,128)(2,1)S(1)}, f32[128,128]{1,0:T(8,128)S(1)}, b...) custom-call(s32[1]{0:T(128)S(6)} %copy.16.refs_0_, ...), custom_call_target="tpu_custom_call" | custom-call | flops 10000000 | bytes 2000000 | tf_op jit(solution)/shard_map/pallas_call | solution.py:572
  17.9 1.4 %collective-permute-start = (f32[40,128]{1,0:T(8,128)S(1)}, f32[40,128]{1,0:T(8,128)S(1)}, u32[]{:S(2)}, u32[]{:S(2)}) collective-permute-start(f32[40,128]{1,0:T(8,128)S(1)} %get-tuple-element.49), channel_id=1, source_target_pairs={{0,1},{1,2},{2,3},{3,0},{4,5},{5,6},{6,7},{7,4},{8,9},{9,10},{10,1... | collective-permute-start | bytes 61448 | tf_op jit(solution)/shard_map/ppermute | solution.py:644
  19.3 1.5 %collective-permute-start.1 = (f32[40,128]{1,0:T(8,128)S(1)}, f32[40,128]{1,0:T(8,128)S(1)}, u32[]{:S(2)}, u32[]{:S(2)}) collective-permute-start(f32[40,128]{1,0:T(8,128)S(1)} %get-tuple-element.50), channel_id=1, source_target_pairs={{0,3},{1,0},{2,1},{3,2},{4,7},{5,4},{6,5},{7,6},{8,11},{9,8},{10,9... | collective-permute-start | bytes 61448 | tf_op jit(solution)/shard_map/ppermute | solution.py:645
  20.8 1.4 %collective-permute-done.refs_6_ = f32[40,128]{1,0:T(8,128)S(1)} collective-permute-done((f32[40,128]{1,0:T(8,128)S(1)}, f32[40,128]{1,0:T(8,128)S(1)}, u32[]{:S(2)}, u32[]{:S(2)}) %collective-permute-start) | collective-permute-done | bytes 20512 | tf_op jit(solution)/shard_map/ppermute | solution.py:644
  22.2 0.0 collective-permute-done.1.refs_7_
  22.2 1.8 %all-to-all-done.refs_2_ = f32[32,4,4,128]{3,2,1,0:T(4,128)S(1)} async-done(((f32[32,4,4,128]{3,2,1,0:T(4,128)}), f32[32,4,4,128]{3,2,1,0:T(4,128)S(1)}, u32[]{:S(2)}, u32[]{:S(2)}) %all-to-all-start) | async-done | bytes 262176 | tf_op jit(solution)/shard_map/all_to_all | solution.py:629
  24.0 3.7 %collective-permute-start.2 = (f32[32,4,4,128]{3,2,1,0:T(4,128)S(1)}, f32[32,4,4,128]{3,2,1,0:T(4,128)S(1)}, u32[]{:S(2)}, u32[]{:S(2)}) collective-permute-start(f32[32,4,4,128]{3,2,1,0:T(4,128)S(1)} %all-to-all-done.refs_2_), channel_id=1, source_target_pairs={{0,4},{4,0},{1,5},{5,1},{2,6},{6,2},{3,7},{7,3},{8,12},{12,8},{9,1... | collective-permute-start | bytes 786440 | tf_op jit(solution)/shard_map/ppermute | solution.py:649
  27.7 1.2 %collective-permute-done.2.refs_3_ = f32[32,4,4,128]{3,2,1,0:T(4,128)S(1)} collective-permute-done((f32[32,4,4,128]{3,2,1,0:T(4,128)S(1)}, f32[32,4,4,128]{3,2,1,0:T(4,128)S(1)}, u32[]{:S(2)}, u32[]{:S(2)}) %collective-permute-start.2) | collective-permute-done | bytes 262176 | tf_op jit(solution)/shard_map/ppermute | solution.py:649
  28.8 0.8 shard_map.133
  29.6 1.4 %collective-permute-start.4 = (f32[56,128]{1,0:T(8,128)S(1)}, f32[56,128]{1,0:T(8,128)S(1)}, u32[]{:S(2)}, u32[]{:S(2)}) collective-permute-start(f32[56,128]{1,0:T(8,128)S(1)} %get-tuple-element.60), channel_id=1, source_target_pairs={{0,1},{1,2},{2,3},{3,0},{4,5},{5,6},{6,7},{7,4},{8,9},{9,10},{10,1... | collective-permute-start | bytes 86024 | tf_op jit(solution)/shard_map/ppermute | solution.py:656
  31.0 1.5 %collective-permute-start.5 = (f32[56,128]{1,0:T(8,128)S(1)}, f32[56,128]{1,0:T(8,128)S(1)}, u32[]{:S(2)}, u32[]{:S(2)}) collective-permute-start(f32[56,128]{1,0:T(8,128)S(1)} %get-tuple-element.61), channel_id=1, source_target_pairs={{0,3},{1,0},{2,1},{3,2},{4,7},{5,4},{6,5},{7,6},{8,11},{9,8},{10,9... | collective-permute-start | bytes 86024 | tf_op jit(solution)/shard_map/ppermute | solution.py:657
  32.5 1.6 %collective-permute-start.3 = (f32[40,128]{1,0:T(8,128)S(1)}, f32[40,128]{1,0:T(8,128)S(1)}, u32[]{:S(2)}, u32[]{:S(2)}) collective-permute-start(f32[40,128]{1,0:T(8,128)S(1)} %get-tuple-element.59.refs_3_), channel_id=1, source_target_pairs={{0,2},{1,3},{2,0},{3,1},{4,6},{5,7},{6,4},{7,5},{8,10},{9,11},{10,... | collective-permute-start | bytes 61448 | tf_op jit(solution)/shard_map/ppermute | solution.py:655
  34.1 0.5 shard_map.134
  34.6 2.1 %collective-permute-done.3.refs_2_ = f32[40,128]{1,0:T(8,128)S(1)} collective-permute-done((f32[40,128]{1,0:T(8,128)S(1)}, f32[40,128]{1,0:T(8,128)S(1)}, u32[]{:S(2)}, u32[]{:S(2)}) %collective-permute-start.3) | collective-permute-done | bytes 20512 | tf_op jit(solution)/shard_map/ppermute | solution.py:655
  36.7 0.0 collective-permute-done.4.refs_4_.refs_8_
  36.7 0.0 collective-permute-done.5.refs_5_.refs_9_
  36.7 0.8 shard_map.135
  37.5 18.7 %all_to_all.20.refs_4_ = f32[64,4,128]{2,1,0:T(4,128)S(1)} all-to-all(f32[64,4,128]{2,1,0:T(4,128)S(1)} %get-tuple-element.73), channel_id=1, replica_groups=mesh['x'=4,'z'=8,'c'=2,'tm'=4] {'x','z','c'}, dimensions={0} | all-to-all | bytes 262144 | tf_op jit(solution)/shard_map/all_to_all | solution.py:668
  56.2 1.5 %shard_map.136 = (f32[3,4,128]{2,1,0:T(4,128)S(1)}, f32[64,2,128]{2,1,0:T(2,128)S(1)}, bf16[128,128]{1,0:T(8,128)(2,1)S(1)}, f32[32,128]{1,0:T(8,128)S(1)}) custom-call(s32[3]{0:T(128)S(1)} %get-tuple-element.47.refs_0_, s32[1]{0:T(128)} %bitcast.6.refs_1_, s32[1]{0:T(128)} %bitcast.refs_1_.refs_0_.refs_2_, s32[1]{0:T(128)} %bitcast.7.refs_1_.refs_3_, ...), custom_call_target="tpu_custom_call" | custom-call | flops 10000000 | bytes 2000000 | tf_op jit(solution)/shard_map/pallas_call | solution.py:572
  57.6 14.5 %all_to_all.21.refs_0_ = f32[64,2,128]{2,1,0:T(2,128)S(1)} all-to-all(f32[64,2,128]{2,1,0:T(2,128)S(1)} %get-tuple-element.78), channel_id=1, replica_groups=mesh['x'=4,'z'=8,'c'=2,'tm'=4] {'x','z','c'}, dimensions={0} | all-to-all | bytes 131072 | tf_op jit(solution)/shard_map/all_to_all | solution.py:673
  72.1 0.6 shard_map.137
  72.7 1.5 %collective-permute-start.8 = (f32[48,128]{1,0:T(8,128)S(1)}, f32[48,128]{1,0:T(8,128)S(1)}, u32[]{:S(2)}, u32[]{:S(2)}) collective-permute-start(f32[48,128]{1,0:T(8,128)S(1)} %get-tuple-element.82.refs_3_), channel_id=1, source_target_pairs={{0,3},{1,0},{2,1},{3,2},{4,7},{5,4},{6,5},{7,6},{8,11},{9,8},{10,9... | collective-permute-start | bytes 73736 | tf_op jit(solution)/shard_map/ppermute | solution.py:680
  74.1 0.1 collective-permute-start.7
  74.2 1.4 %collective-permute-start.6 = (f32[48,128]{1,0:T(8,128)S(1)}, f32[48,128]{1,0:T(8,128)S(1)}, u32[]{:S(2)}, u32[]{:S(2)}) collective-permute-start(f32[48,128]{1,0:T(8,128)S(1)} %get-tuple-element.82.refs_3_), channel_id=1, source_target_pairs={{0,2},{1,3},{2,0},{3,1},{4,6},{5,7},{6,4},{7,5},{8,10},{9,11},{10,... | collective-permute-start | bytes 73736 | tf_op jit(solution)/shard_map/ppermute | solution.py:678
  75.6 0.5 shard_map.138.refs_10_
  76.1 0.0 collective-permute-done.8.refs_5_
  76.1 1.9 %collective-permute-done.7.refs_4_ = f32[48,128]{1,0:T(8,128)S(1)} collective-permute-done((f32[48,128]{1,0:T(8,128)S(1)}, f32[48,128]{1,0:T(8,128)S(1)}, u32[]{:S(2)}, u32[]{:S(2)}) %collective-permute-start.7) | collective-permute-done | bytes 24608 | tf_op jit(solution)/shard_map/ppermute | solution.py:679
  78.0 0.4 collective-permute-done.6.refs_2_
  78.4 0.8 shard_map.139
  79.2 15.7 %all_to_all.22.refs_4_ = f32[64,1,384]{2,1,0:T(1,128)S(1)} all-to-all(f32[64,1,384]{2,1,0:T(1,128)S(1)} %get-tuple-element.85), channel_id=1, replica_groups=mesh['x'=4,'z'=8,'c'=2,'tm'=4] {'x','z','c'}, dimensions={0} | all-to-all | bytes 196608 | tf_op jit(solution)/shard_map/all_to_all | solution.py:690
  94.9 1.7 %shard_map.140 = (f32[3,4,128]{2,1,0:T(4,128)}, f32[5,1024]{1,0:T(8,128)}) custom-call(s32[3]{0:T(128)S(1)} %get-tuple-element.47.refs_0_, s32[1]{0:T(128)} %bitcast.6.refs_1_, s32[1]{0:T(128)} %bitcast.refs_1_.refs_0_.refs_2_, s32[1]{0:T(128)} %bitcast.7.refs_1_.refs_3_, f32[64,1,384]{2,1,0:T(1,128)S(1)} %all_to_all.22.refs_4_, ...), custom_call_target="tpu_custom_call" | custom-call | flops 10000000 | bytes 2000000 | tf_op jit(solution)/shard_map/pallas_call | solution.py:572
  (7 shorter events, 0.0 us)
Async XLA Ops:
  2.2 12.8 %copy-start = (bf16[3,128,128]{2,1,0:T(8,128)(2,1)S(1)}, bf16[3,128,128]{2,1,0:T(8,128)(2,1)}, u32[]{:S(2)}) copy-start(bf16[3,128,128]{2,1,0:T(8,128)(2,1)} %refs_3_.5) | copy-start | bytes 294916
  2.2 12.8 %copy-start.2 = (bf16[5,128,128]{2,1,0:T(8,128)(2,1)S(1)}, bf16[5,128,128]{2,1,0:T(8,128)(2,1)}, u32[]{:S(2)}) copy-start(bf16[5,128,128]{2,1,0:T(8,128)(2,1)} %refs_18_.1) | copy-start | bytes 491524
  2.2 12.8 %copy-start.3 = (f32[5,1024]{1,0:T(8,128)S(1)}, f32[5,1024]{1,0:T(8,128)}, u32[]{:S(2)}) copy-start(f32[5,1024]{1,0:T(8,128)} %refs_9_.1) | copy-start | bytes 61444
  2.2 12.8 %copy-start.4 = (f32[3,3,1,512]{3,2,1,0:T(1,128)S(1)}, f32[3,3,1,512]{3,2,1,0:T(1,128)}, u32[]{:S(2)}) copy-start(f32[3,3,1,512]{3,2,1,0:T(1,128)} %param.21) | copy-start | bytes 55300
  2.2 12.8 %copy-start.5 = (f32[128,128]{1,0:T(8,128)S(1)}, f32[128,128]{1,0:T(8,128)}, u32[]{:S(2)}) copy-start(f32[128,128]{1,0:T(8,128)} %refs_3_.3) | copy-start | bytes 196612
  2.2 12.8 %copy-start.10 = (s32[128]{0:T(128)S(1)}, s32[128]{0:T(128)}, u32[]{:S(2)}) copy-start(s32[128]{0:T(128)} %param.16) | copy-start | bytes 1540
  2.3 21.7 %all-to-all-start = ((f32[32,4,4,128]{3,2,1,0:T(4,128)}), f32[32,4,4,128]{3,2,1,0:T(4,128)S(1)}, u32[]{:S(2)}, u32[]{:S(2)}) async-start(f32[32,4,4,128]{3,2,1,0:T(4,128)} %shard_map.132), calls=%async_computation | async-start | bytes 524288 | tf_op jit(solution)/shard_map/all_to_all | solution.py:629
  14.3 0.8 copy-start.7
  14.3 0.8 copy-start.6
  15.0 0.7 copy-start.8
  15.0 0.7 copy-start.9
  17.9 4.3 %collective-permute-start = (f32[40,128]{1,0:T(8,128)S(1)}, f32[40,128]{1,0:T(8,128)S(1)}, u32[]{:S(2)}, u32[]{:S(2)}) collective-permute-start(f32[40,128]{1,0:T(8,128)S(1)} %get-tuple-element.49), channel_id=1, source_target_pairs={{0,1},{1,2},{2,3},{3,0},{4,5},{5,6},{6,7},{7,4},{8,9},{9,10},{10,1... | collective-permute-start | bytes 61448 | tf_op jit(solution)/shard_map/ppermute | solution.py:644
  19.3 2.9 %collective-permute-start.1 = (f32[40,128]{1,0:T(8,128)S(1)}, f32[40,128]{1,0:T(8,128)S(1)}, u32[]{:S(2)}, u32[]{:S(2)}) collective-permute-start(f32[40,128]{1,0:T(8,128)S(1)} %get-tuple-element.50), channel_id=1, source_target_pairs={{0,3},{1,0},{2,1},{3,2},{4,7},{5,4},{6,5},{7,6},{8,11},{9,8},{10,9... | collective-permute-start | bytes 61448 | tf_op jit(solution)/shard_map/ppermute | solution.py:645
  24.0 4.9 %collective-permute-start.2 = (f32[32,4,4,128]{3,2,1,0:T(4,128)S(1)}, f32[32,4,4,128]{3,2,1,0:T(4,128)S(1)}, u32[]{:S(2)}, u32[]{:S(2)}) collective-permute-start(f32[32,4,4,128]{3,2,1,0:T(4,128)S(1)} %all-to-all-done.refs_2_), channel_id=1, source_target_pairs={{0,4},{4,0},{1,5},{5,1},{2,6},{6,2},{3,7},{7,3},{8,12},{12,8},{9,1... | collective-permute-start | bytes 786440 | tf_op jit(solution)/shard_map/ppermute | solution.py:649
  29.6 7.0 %collective-permute-start.4 = (f32[56,128]{1,0:T(8,128)S(1)}, f32[56,128]{1,0:T(8,128)S(1)}, u32[]{:S(2)}, u32[]{:S(2)}) collective-permute-start(f32[56,128]{1,0:T(8,128)S(1)} %get-tuple-element.60), channel_id=1, source_target_pairs={{0,1},{1,2},{2,3},{3,0},{4,5},{5,6},{6,7},{7,4},{8,9},{9,10},{10,1... | collective-permute-start | bytes 86024 | tf_op jit(solution)/shard_map/ppermute | solution.py:656
  31.0 5.7 %collective-permute-start.5 = (f32[56,128]{1,0:T(8,128)S(1)}, f32[56,128]{1,0:T(8,128)S(1)}, u32[]{:S(2)}, u32[]{:S(2)}) collective-permute-start(f32[56,128]{1,0:T(8,128)S(1)} %get-tuple-element.61), channel_id=1, source_target_pairs={{0,3},{1,0},{2,1},{3,2},{4,7},{5,4},{6,5},{7,6},{8,11},{9,8},{10,9... | collective-permute-start | bytes 86024 | tf_op jit(solution)/shard_map/ppermute | solution.py:657
  32.5 4.1 %collective-permute-start.3 = (f32[40,128]{1,0:T(8,128)S(1)}, f32[40,128]{1,0:T(8,128)S(1)}, u32[]{:S(2)}, u32[]{:S(2)}) collective-permute-start(f32[40,128]{1,0:T(8,128)S(1)} %get-tuple-element.59.refs_3_), channel_id=1, source_target_pairs={{0,2},{1,3},{2,0},{3,1},{4,6},{5,7},{6,4},{7,5},{8,10},{9,11},{10,... | collective-permute-start | bytes 61448 | tf_op jit(solution)/shard_map/ppermute | solution.py:655
  34.1 2.6 %copy-start.1 = (f32[5,5,1024]{2,1,0:T(8,128)S(1)}, f32[5,5,1024]{2,1,0:T(8,128)}, u32[]{:S(2)}) copy-start(f32[5,5,1024]{2,1,0:T(8,128)} %refs_8_.5) | copy-start | bytes 307204
  72.7 3.4 %collective-permute-start.8 = (f32[48,128]{1,0:T(8,128)S(1)}, f32[48,128]{1,0:T(8,128)S(1)}, u32[]{:S(2)}, u32[]{:S(2)}) collective-permute-start(f32[48,128]{1,0:T(8,128)S(1)} %get-tuple-element.82.refs_3_), channel_id=1, source_target_pairs={{0,3},{1,0},{2,1},{3,2},{4,7},{5,4},{6,5},{7,6},{8,11},{9,8},{10,9... | collective-permute-start | bytes 73736 | tf_op jit(solution)/shard_map/ppermute | solution.py:680
  74.1 3.9 %collective-permute-start.7 = (f32[48,128]{1,0:T(8,128)S(1)}, f32[48,128]{1,0:T(8,128)S(1)}, u32[]{:S(2)}, u32[]{:S(2)}) collective-permute-start(f32[48,128]{1,0:T(8,128)S(1)} %get-tuple-element.82.refs_3_), channel_id=1, source_target_pairs={{0,1},{1,2},{2,3},{3,0},{4,5},{5,6},{6,7},{7,4},{8,9},{9,10},{10,1... | collective-permute-start | bytes 73736 | tf_op jit(solution)/shard_map/ppermute | solution.py:679
  74.2 4.2 %collective-permute-start.6 = (f32[48,128]{1,0:T(8,128)S(1)}, f32[48,128]{1,0:T(8,128)S(1)}, u32[]{:S(2)}, u32[]{:S(2)}) collective-permute-start(f32[48,128]{1,0:T(8,128)S(1)} %get-tuple-element.82.refs_3_), channel_id=1, source_target_pairs={{0,2},{1,3},{2,0},{3,1},{4,6},{5,7},{6,4},{7,5},{8,10},{9,11},{10,... | collective-permute-start | bytes 73736 | tf_op jit(solution)/shard_map/ppermute | solution.py:678

commit v8 on v6

--- a/solution.py
+++ b/solution.py
@@ -238,12 +238,15 @@
     copies = [
         pltpu.make_async_copy(source, target, sems.at[i])
         for i, (source, target) in enumerate(
-            ((bands_hbm, bands_ref), (extra_hbm, extra_ref), (knots_hbm, knots_ref))
+            ((knots_hbm, knots_ref), (bands_hbm, bands_ref), (extra_hbm, extra_ref))
         )
     ]
     for copy in copies:
         copy.start()
-    for copy in copies:
+    copies[0].wait()
+    for chip in range(CHIPS):
+        out_ref[chip, 0:3] = knots_ref[...]
+    for copy in copies[1:]:
         copy.wait()
     lane = iota((1, 128), 1)
 
@@ -264,7 +267,6 @@
     for i, row in enumerate(rows):
         edge = jnp.where(sub == i, row, edge)
     for chip in range(CHIPS):
-        out_ref[chip, 0:3] = knots_ref[...]
         out_ref[chip, 3] = edge
 
 
@@ -502,9 +504,11 @@
         for r in range(5):
             if r < 4:
                 piece = jnp.where(in_row, spread[32 * a + 8 * r : 32 * a + 8 * r + 8], 0.0)
+                here = sub8 == a
             else:
-                piece = jnp.where((lane < 32) | (lane >= 96), got[a], 0.0)
-            grad[r] = jnp.where(sub8 == a, jnp.sum(piece, axis=0, keepdims=True), grad[r])
+                piece = got[a]
+                here = (sub8 == a) & ((lane8 < 32) | (lane8 >= 96))
+            grad[r] = jnp.where(here, jnp.sum(piece, axis=0, keepdims=True), grad[r])
     bands, scale = [], None
     for i in range(4):
         tiles = [wide_ref[8 * i : 8 * i + 8, 128 * r : 128 * r + 128] for r in range(4)]

time: 94.9 us -> 94.9 us (level)
  no operation moved by 1% of the time
where the time goes in v8:
time: 94.9 us; the launch traced here: 94.6 us
  blocking collectives  46.7 us (49%)
  starting transfers between devices  23.4 us (25%)
  waiting for transfers between devices  11.5 us (12%)
  Pallas kernels  10.7 us (11%)
  between operations  1.54 us (2%)
    all_to_all x2, blocking collectives, per_device(): got = lax.all_to_all(outgoing, SKY, 0, 0, tiled=True)  32.3 us
    all_to_all x1, blocking collectives, per_device(): arrived = lax.all_to_all(served, SKY, 0, 0, tiled=True)  14.5 us
    all_to_all x1, starting transfers between devices, per_device(): near = lax.all_to_all(dense, ('x', 'z'), 0, 0, tiled=True)  12 us
    pallas_call x9, Pallas kernels, run_kernel(): pl.pallas_call(kernel, out_shape=shapes, in_specs=specs, out_specs=[pl.Bl...  9.17 us
    all_to_all x1, waiting for transfers between devices, per_device(): near = lax.all_to_all(dense, ('x', 'z'), 0, 0, tiled=True)  6.08 us
    ppermute x1, starting transfers between devices, per_device(): far = lax.ppermute(near, 'c', [(0, 1), (1, 0)])  3.72 us
    ppermute x1, waiting for transfers between devices, per_device(): across = lax.ppermute(plain, 'tm', shifts(2))  2.11 us
  transfers between devices with their start and end apart: 8, of which 5 were waited for; matrix products, arithmetic and copies ran while one was open for 0% of the time, Pallas kernels for 3%

profile of v8, /device:TPU:1, one launch (start us, length us, event | category | flops | bytes accessed | tf_op | source)
XLA Modules:
  0.0 94.6 jit_solution(14998575063676514509)
XLA Ops:
  0.6 1.6 %shard_map.132 = f32[32,4,4,128]{3,2,1,0:T(4,128)} custom-call(f32[3,4,128]{2,1,0:T(4,128)} %bitcast.13, f32[3,3,4,128]{3,2,1,0:T(4,128)} %bitcast.9, f32[3,4,128]{2,1,0:T(4,128)} %bitcast.11), custom_call_target="tpu_custom_call" | custom-call | tf_op jit(solution)/shard_map/pallas_call | solution.py:624
  2.2 0.0 copy-start
  2.2 0.0 copy-start.2
  2.2 0.0 copy-start.3
  2.2 0.0 copy-start.4
  2.2 0.0 copy-start.5
  2.2 0.0 copy-start.10
  2.3 12.0 %all-to-all-start = ((f32[32,4,4,128]{3,2,1,0:T(4,128)}), f32[32,4,4,128]{3,2,1,0:T(4,128)S(1)}, u32[]{:S(2)}, u32[]{:S(2)}) async-start(f32[32,4,4,128]{3,2,1,0:T(4,128)} %shard_map.132), calls=%async_computation | async-start | bytes 524288 | tf_op jit(solution)/shard_map/all_to_all | solution.py:637
  14.3 0.0 copy-start.7
  14.3 0.0 copy-start.6
  15.0 0.0 copy-start.8
  15.0 0.0 copy-start.9
  15.0 0.0 copy-done
  15.0 0.0 copy-done.2
  15.0 0.0 copy-done.3
  15.0 0.0 copy-done.4
  15.0 0.0 copy-done.5
  15.0 0.0 copy-done.10
  15.1 0.0 copy-done.7
  15.1 0.6 copy-done.8
  15.6 0.0 copy-done.9
  15.6 2.2 %shard_map.131 = (f32[128,128]{1,0:T(8,128)S(1)}, bf16[144,256]{1,0:T(8,128)(2,1)S(1)}, bf16[128,1024]{1,0:T(8,128)(2,1)S(1)}, f32[128,128]{1,0:T(8,128)S(1)}, b...) custom-call(s32[1]{0:T(128)S(6)} %copy.16.refs_0_, ...), custom_call_target="tpu_custom_call" | custom-call | flops 10000000 | bytes 2000000 | tf_op jit(solution)/shard_map/pallas_call | solution.py:580
  17.9 6.1 %all-to-all-done.refs_2_ = f32[32,4,4,128]{3,2,1,0:T(4,128)S(1)} async-done(((f32[32,4,4,128]{3,2,1,0:T(4,128)}), f32[32,4,4,128]{3,2,1,0:T(4,128)S(1)}, u32[]{:S(2)}, u32[]{:S(2)}) %all-to-all-start) | async-done | bytes 262176 | tf_op jit(solution)/shard_map/all_to_all | solution.py:637
  24.0 3.7 %collective-permute-start = (f32[32,4,4,128]{3,2,1,0:T(4,128)S(1)}, f32[32,4,4,128]{3,2,1,0:T(4,128)S(1)}, u32[]{:S(2)}, u32[]{:S(2)}) collective-permute-start(f32[32,4,4,128]{3,2,1,0:T(4,128)S(1)} %all-to-all-done.refs_2_), channel_id=1, source_target_pairs={{0,4},{4,0},{1,5},{5,1},{2,6},{6,2},{3,7},{7,3},{8,12},{12,8},{9,1... | collective-permute-start | bytes 786440 | tf_op jit(solution)/shard_map/ppermute | solution.py:653
  27.7 1.2 %collective-permute-done.refs_3_ = f32[32,4,4,128]{3,2,1,0:T(4,128)S(1)} collective-permute-done((f32[32,4,4,128]{3,2,1,0:T(4,128)S(1)}, f32[32,4,4,128]{3,2,1,0:T(4,128)S(1)}, u32[]{:S(2)}, u32[]{:S(2)}) %collective-permute-start) | collective-permute-done | bytes 262176 | tf_op jit(solution)/shard_map/ppermute | solution.py:653
  28.9 0.8 shard_map.133
  29.6 1.4 %collective-permute-start.2 = (f32[88,128]{1,0:T(8,128)S(1)}, f32[88,128]{1,0:T(8,128)S(1)}, u32[]{:S(2)}, u32[]{:S(2)}) collective-permute-start(f32[88,128]{1,0:T(8,128)S(1)} %get-tuple-element.58), channel_id=1, source_target_pairs={{0,1},{1,2},{2,3},{3,0},{4,5},{5,6},{6,7},{7,4},{8,9},{9,10},{10,1... | collective-permute-start | bytes 135176 | tf_op jit(solution)/shard_map/ppermute | solution.py:660
  31.0 1.5 %collective-permute-start.3 = (f32[88,128]{1,0:T(8,128)S(1)}, f32[88,128]{1,0:T(8,128)S(1)}, u32[]{:S(2)}, u32[]{:S(2)}) collective-permute-start(f32[88,128]{1,0:T(8,128)S(1)} %get-tuple-element.59), channel_id=1, source_target_pairs={{0,3},{1,0},{2,1},{3,2},{4,7},{5,4},{6,5},{7,6},{8,11},{9,8},{10,9... | collective-permute-start | bytes 135176 | tf_op jit(solution)/shard_map/ppermute | solution.py:661
  32.5 1.6 %collective-permute-start.1 = (f32[40,128]{1,0:T(8,128)S(1)}, f32[40,128]{1,0:T(8,128)S(1)}, u32[]{:S(2)}, u32[]{:S(2)}) collective-permute-start(f32[40,128]{1,0:T(8,128)S(1)} %get-tuple-element.57.refs_3_), channel_id=1, source_target_pairs={{0,2},{1,3},{2,0},{3,1},{4,6},{5,7},{6,4},{7,5},{8,10},{9,11},{10,... | collective-permute-start | bytes 61448 | tf_op jit(solution)/shard_map/ppermute | solution.py:659
  34.1 0.5 shard_map.134
  34.6 2.1 %collective-permute-done.1.refs_2_ = f32[40,128]{1,0:T(8,128)S(1)} collective-permute-done((f32[40,128]{1,0:T(8,128)S(1)}, f32[40,128]{1,0:T(8,128)S(1)}, u32[]{:S(2)}, u32[]{:S(2)}) %collective-permute-start.1) | collective-permute-done | bytes 20512 | tf_op jit(solution)/shard_map/ppermute | solution.py:659
  36.7 0.0 collective-permute-done.2.refs_4_.refs_6_.refs_8_
  36.7 0.0 collective-permute-done.3.refs_5_.refs_7_.refs_9_
  36.7 0.8 shard_map.135
  37.5 16.7 %all_to_all.20.refs_4_ = f32[64,4,128]{2,1,0:T(4,128)S(1)} all-to-all(f32[64,4,128]{2,1,0:T(4,128)S(1)} %get-tuple-element.69), channel_id=1, replica_groups=mesh['x'=4,'z'=8,'c'=2,'tm'=4] {'x','z','c'}, dimensions={0} | all-to-all | bytes 262144 | tf_op jit(solution)/shard_map/all_to_all | solution.py:672
  54.1 1.5 %shard_map.136 = (f32[3,4,128]{2,1,0:T(4,128)S(1)}, f32[64,2,128]{2,1,0:T(2,128)S(1)}, bf16[128,128]{1,0:T(8,128)(2,1)S(1)}, f32[32,128]{1,0:T(8,128)S(1)}) custom-call(s32[3]{0:T(128)S(1)} %get-tuple-element.45.refs_0_, s32[1]{0:T(128)} %bitcast.6.refs_1_, s32[1]{0:T(128)} %bitcast.refs_1_.refs_0_.refs_2_, s32[1]{0:T(128)} %bitcast.7.refs_1_.refs_3_, ...), custom_call_target="tpu_custom_call" | custom-call | flops 10000000 | bytes 2000000 | tf_op jit(solution)/shard_map/pallas_call | solution.py:580
  55.6 14.5 %all_to_all.21.refs_0_ = f32[64,2,128]{2,1,0:T(2,128)S(1)} all-to-all(f32[64,2,128]{2,1,0:T(2,128)S(1)} %get-tuple-element.74), channel_id=1, replica_groups=mesh['x'=4,'z'=8,'c'=2,'tm'=4] {'x','z','c'}, dimensions={0} | all-to-all | bytes 131072 | tf_op jit(solution)/shard_map/all_to_all | solution.py:677
  70.1 0.6 shard_map.137
  70.6 1.6 %collective-permute-start.6 = (f32[48,128]{1,0:T(8,128)S(1)}, f32[48,128]{1,0:T(8,128)S(1)}, u32[]{:S(2)}, u32[]{:S(2)}) collective-permute-start(f32[48,128]{1,0:T(8,128)S(1)} %get-tuple-element.78.refs_3_), channel_id=1, source_target_pairs={{0,3},{1,0},{2,1},{3,2},{4,7},{5,4},{6,5},{7,6},{8,11},{9,8},{10,9... | collective-permute-start | bytes 73736 | tf_op jit(solution)/shard_map/ppermute | solution.py:684
  72.2 0.0 collective-permute-start.5
  72.2 1.6 %collective-permute-start.4 = (f32[48,128]{1,0:T(8,128)S(1)}, f32[48,128]{1,0:T(8,128)S(1)}, u32[]{:S(2)}, u32[]{:S(2)}) collective-permute-start(f32[48,128]{1,0:T(8,128)S(1)} %get-tuple-element.78.refs_3_), channel_id=1, source_target_pairs={{0,2},{1,3},{2,0},{3,1},{4,6},{5,7},{6,4},{7,5},{8,10},{9,11},{10,... | collective-permute-start | bytes 73736 | tf_op jit(solution)/shard_map/ppermute | solution.py:682
  73.9 0.5 shard_map.138.refs_10_
  74.4 0.0 collective-permute-done.6.refs_5_
  74.4 1.8 %collective-permute-done.5.refs_4_ = f32[48,128]{1,0:T(8,128)S(1)} collective-permute-done((f32[48,128]{1,0:T(8,128)S(1)}, f32[48,128]{1,0:T(8,128)S(1)}, u32[]{:S(2)}, u32[]{:S(2)}) %collective-permute-start.5) | collective-permute-done | bytes 24608 | tf_op jit(solution)/shard_map/ppermute | solution.py:683
  76.1 0.4 collective-permute-done.4.refs_2_
  76.5 0.8 shard_map.139
  77.3 15.6 %all_to_all.22.refs_4_ = f32[64,1,384]{2,1,0:T(1,128)S(1)} all-to-all(f32[64,1,384]{2,1,0:T(1,128)S(1)} %get-tuple-element.81), channel_id=1, replica_groups=mesh['x'=4,'z'=8,'c'=2,'tm'=4] {'x','z','c'}, dimensions={0} | all-to-all | bytes 196608 | tf_op jit(solution)/shard_map/all_to_all | solution.py:694
  92.9 1.7 %shard_map.140 = (f32[3,4,128]{2,1,0:T(4,128)}, f32[5,1024]{1,0:T(8,128)}) custom-call(s32[3]{0:T(128)S(1)} %get-tuple-element.45.refs_0_, s32[1]{0:T(128)} %bitcast.6.refs_1_, s32[1]{0:T(128)} %bitcast.refs_1_.refs_0_.refs_2_, s32[1]{0:T(128)} %bitcast.7.refs_1_.refs_3_, f32[64,1,384]{2,1,0:T(1,128)S(1)} %all_to_all.22.refs_4_, ...), custom_call_target="tpu_custom_call" | custom-call | flops 10000000 | bytes 2000000 | tf_op jit(solution)/shard_map/pallas_call | solution.py:580
  (3 shorter events, 0.0 us)
Async XLA Ops:
  2.2 12.8 %copy-start = (bf16[3,128,128]{2,1,0:T(8,128)(2,1)S(1)}, bf16[3,128,128]{2,1,0:T(8,128)(2,1)}, u32[]{:S(2)}) copy-start(bf16[3,128,128]{2,1,0:T(8,128)(2,1)} %refs_3_.5) | copy-start | bytes 294916
  2.2 12.8 %copy-start.2 = (bf16[5,128,128]{2,1,0:T(8,128)(2,1)S(1)}, bf16[5,128,128]{2,1,0:T(8,128)(2,1)}, u32[]{:S(2)}) copy-start(bf16[5,128,128]{2,1,0:T(8,128)(2,1)} %refs_18_.1) | copy-start | bytes 491524
  2.2 12.8 %copy-start.3 = (f32[5,1024]{1,0:T(8,128)S(1)}, f32[5,1024]{1,0:T(8,128)}, u32[]{:S(2)}) copy-start(f32[5,1024]{1,0:T(8,128)} %refs_9_.1) | copy-start | bytes 61444
  2.2 12.8 %copy-start.4 = (f32[3,3,1,512]{3,2,1,0:T(1,128)S(1)}, f32[3,3,1,512]{3,2,1,0:T(1,128)}, u32[]{:S(2)}) copy-start(f32[3,3,1,512]{3,2,1,0:T(1,128)} %param.21) | copy-start | bytes 55300
  2.2 12.8 %copy-start.5 = (f32[128,128]{1,0:T(8,128)S(1)}, f32[128,128]{1,0:T(8,128)}, u32[]{:S(2)}) copy-start(f32[128,128]{1,0:T(8,128)} %refs_3_.3) | copy-start | bytes 196612
  2.2 12.8 %copy-start.10 = (s32[128]{0:T(128)S(1)}, s32[128]{0:T(128)}, u32[]{:S(2)}) copy-start(s32[128]{0:T(128)} %param.16) | copy-start | bytes 1540
  2.3 21.7 %all-to-all-start = ((f32[32,4,4,128]{3,2,1,0:T(4,128)}), f32[32,4,4,128]{3,2,1,0:T(4,128)S(1)}, u32[]{:S(2)}, u32[]{:S(2)}) async-start(f32[32,4,4,128]{3,2,1,0:T(4,128)} %shard_map.132), calls=%async_computation | async-start | bytes 524288 | tf_op jit(solution)/shard_map/all_to_all | solution.py:637
  14.3 0.8 copy-start.7
  14.3 0.8 copy-start.6
  15.0 0.7 copy-start.8
  15.0 0.7 copy-start.9
  24.0 4.9 %collective-permute-start = (f32[32,4,4,128]{3,2,1,0:T(4,128)S(1)}, f32[32,4,4,128]{3,2,1,0:T(4,128)S(1)}, u32[]{:S(2)}, u32[]{:S(2)}) collective-permute-start(f32[32,4,4,128]{3,2,1,0:T(4,128)S(1)} %all-to-all-done.refs_2_), channel_id=1, source_target_pairs={{0,4},{4,0},{1,5},{5,1},{2,6},{6,2},{3,7},{7,3},{8,12},{12,8},{9,1... | collective-permute-start | bytes 786440 | tf_op jit(solution)/shard_map/ppermute | solution.py:653
  29.6 7.0 %collective-permute-start.2 = (f32[88,128]{1,0:T(8,128)S(1)}, f32[88,128]{1,0:T(8,128)S(1)}, u32[]{:S(2)}, u32[]{:S(2)}) collective-permute-start(f32[88,128]{1,0:T(8,128)S(1)} %get-tuple-element.58), channel_id=1, source_target_pairs={{0,1},{1,2},{2,3},{3,0},{4,5},{5,6},{6,7},{7,4},{8,9},{9,10},{10,1... | collective-permute-start | bytes 135176 | tf_op jit(solution)/shard_map/ppermute | solution.py:660
  31.0 5.7 %collective-permute-start.3 = (f32[88,128]{1,0:T(8,128)S(1)}, f32[88,128]{1,0:T(8,128)S(1)}, u32[]{:S(2)}, u32[]{:S(2)}) collective-permute-start(f32[88,128]{1,0:T(8,128)S(1)} %get-tuple-element.59), channel_id=1, source_target_pairs={{0,3},{1,0},{2,1},{3,2},{4,7},{5,4},{6,5},{7,6},{8,11},{9,8},{10,9... | collective-permute-start | bytes 135176 | tf_op jit(solution)/shard_map/ppermute | solution.py:661
  32.5 4.1 %collective-permute-start.1 = (f32[40,128]{1,0:T(8,128)S(1)}, f32[40,128]{1,0:T(8,128)S(1)}, u32[]{:S(2)}, u32[]{:S(2)}) collective-permute-start(f32[40,128]{1,0:T(8,128)S(1)} %get-tuple-element.57.refs_3_), channel_id=1, source_target_pairs={{0,2},{1,3},{2,0},{3,1},{4,6},{5,7},{6,4},{7,5},{8,10},{9,11},{10,... | collective-permute-start | bytes 61448 | tf_op jit(solution)/shard_map/ppermute | solution.py:659
  34.1 2.6 %copy-start.1 = (f32[5,5,1024]{2,1,0:T(8,128)S(1)}, f32[5,5,1024]{2,1,0:T(8,128)}, u32[]{:S(2)}) copy-start(f32[5,5,1024]{2,1,0:T(8,128)} %refs_8_.5) | copy-start | bytes 307204
  70.6 3.7 %collective-permute-start.6 = (f32[48,128]{1,0:T(8,128)S(1)}, f32[48,128]{1,0:T(8,128)S(1)}, u32[]{:S(2)}, u32[]{:S(2)}) collective-permute-start(f32[48,128]{1,0:T(8,128)S(1)} %get-tuple-element.78.refs_3_), channel_id=1, source_target_pairs={{0,3},{1,0},{2,1},{3,2},{4,7},{5,4},{6,5},{7,6},{8,11},{9,8},{10,9... | collective-permute-start | bytes 73736 | tf_op jit(solution)/shard_map/ppermute | solution.py:684
  72.2 3.9 %collective-permute-start.5 = (f32[48,128]{1,0:T(8,128)S(1)}, f32[48,128]{1,0:T(8,128)S(1)}, u32[]{:S(2)}, u32[]{:S(2)}) collective-permute-start(f32[48,128]{1,0:T(8,128)S(1)} %get-tuple-element.78.refs_3_), channel_id=1, source_target_pairs={{0,1},{1,2},{2,3},{3,0},{4,5},{5,6},{6,7},{7,4},{8,9},{9,10},{10,1... | collective-permute-start | bytes 73736 | tf_op jit(solution)/shard_map/ppermute | solution.py:683
  72.2 4.3 %collective-permute-start.4 = (f32[48,128]{1,0:T(8,128)S(1)}, f32[48,128]{1,0:T(8,128)S(1)}, u32[]{:S(2)}, u32[]{:S(2)}) collective-permute-start(f32[48,128]{1,0:T(8,128)S(1)} %get-tuple-element.78.refs_3_), channel_id=1, source_target_pairs={{0,2},{1,3},{2,0},{3,1},{4,6},{5,7},{6,4},{7,5},{8,10},{9,11},{10,... | collective-permute-start | bytes 73736 | tf_op jit(solution)/shard_map/ppermute | solution.py:682
